TPU v7x, 256 devices: a whole 4x4x8 slice. The times are simulated.
256 devices in a mesh: role: 2 (over x_hi), dp: 4 (over y), tensor: 32 (over x_lo, z, core).
Axes of the slice: x: 4 (x_hi: 2, x_lo: 2; x = x_hi * 2 + x_lo), y: 4, z: 8, core: 2. Of those that a mesh axis runs over, the one named last changes fastest.
Arguments:
- grad_parts: bfloat16 [2, 4, 512, 2, 18432], P('role', 'dp', 'tensor'), may hold values from -18 to 18
- master: float32 [2, 512, 2, 18432], P('role', 'tensor', None, 'dp'), may hold values from -2 to 2
- moment1: float32 [2, 512, 2, 18432], P('role', 'tensor', None, 'dp'), may hold values from -6 to 6
- moment2: float32 [2, 512, 2, 18432], P('role', 'tensor', None, 'dp'), may hold values from 0.05 to 0.5
- kv_cache: bfloat16 [2, 64, 32, 256, 384], P('role', 'dp', 'tensor'), may hold values from -200 to 200
- hidden_in: bfloat16 [64, 4, 18432], P('dp', None, 'tensor'), may hold values from -60 to 60
- attn_gain: float32 [18432], replicated, may hold values from 0.1 to 1.9
- ffn_gain: float32 [18432], replicated, may hold values from 0.1 to 1.9
- lengths: int32 [64], P('dp'), may hold values from 2 to 256, as said below
Outputs:
- weights_after: float32 [2, 512, 2, 18432], P('role', 'tensor', None, 'dp')
- decoded: bfloat16 [64, 4, 18432], P('dp', None, 'tensor')
Inputs may be any that keep to these rules, and one draw needn't show every extreme that they name: `lengths`: some row holds all 256 positions.
All inputs are finite; a program needn't handle non-finite values.
Results may differ from a plain program's by a relative error of at most 0.015.
Values may be sent and summed in bfloat16 or wider, within the bound.
No kernel may reach another device: no remote copies, remote signals or barrier semaphores. Data moves between devices by JAX's collectives and lax.ppermute only.
A program may use at most 128 MiB of HBM per device.

v0:
```python
import math

import jax
import jax.numpy as jnp
from jax import lax
from jax.sharding import PartitionSpec as P

D = 18432
HEAD = 192
STEPS = 4


beta_one = 0.9
beta_two = 0.95
rate_factor = 0.5
decay_rate = 0.1
adam_eps = 1e-08
norm_eps = 1e-05
step_count = 10


def passed_along(shard, axis, by):
    devices = lax.axis_size(axis)
    pairs = [(i, i + by) for i in range(devices) if 0 <= i + by < devices]
    return lax.ppermute(shard, axis, pairs)


def adam_update(grad_sum, weights, first, second):
    learn_rate = rate_factor / math.sqrt(D)
    first_new = beta_one * first + (1.0 - beta_one) * grad_sum
    second_new = beta_two * second + (1.0 - beta_two) * grad_sum * grad_sum
    corr_one = 1.0 - beta_one**step_count
    corr_two = 1.0 - beta_two**step_count
    ratio = first_new / corr_one / (jnp.sqrt(second_new / corr_two) + adam_eps)
    return weights - learn_rate * (ratio + decay_rate * weights)


def attend(query, keys, values, lengths, new_keys, new_values):
    scale = 1.0 / math.sqrt(HEAD)
    cache_scores = (
        jnp.einsum("rgqe,rgce->rgqc", query, keys, preferred_element_type=jnp.float32) * scale
    )
    positions = jnp.arange(keys.shape[2], dtype=jnp.int32)
    valid = positions[None, None, None, :] < lengths[:, None, None, None]
    cache_scores = jnp.where(valid, cache_scores, -jnp.inf)
    fresh_scores = (
        jnp.einsum("rgqe,rgse->rgqs", query, new_keys, preferred_element_type=jnp.float32) * scale
    )
    top = jnp.maximum(jnp.max(cache_scores, axis=3), jnp.max(fresh_scores, axis=3))[..., None]
    cache_exp = jnp.exp(cache_scores - top)
    fresh_exp = jnp.exp(fresh_scores - top)
    total = jnp.sum(cache_exp, axis=3, keepdims=True) + jnp.sum(fresh_exp, axis=3, keepdims=True)
    cache_prob = (cache_exp / total).astype(jnp.bfloat16)
    fresh_prob = (fresh_exp / total).astype(jnp.bfloat16)
    first_part = jnp.einsum(
        "rgqc,rgce->rgqe", cache_prob, values, preferred_element_type=jnp.float32
    )
    second_part = jnp.einsum(
        "rgqs,rgse->rgqe", fresh_prob, new_values, preferred_element_type=jnp.float32
    )
    return first_part + second_part


def body(grad_parts, master, moment1, moment2, kv_cache, hidden_in, attn_gain, ffn_gain, lengths):
    role_index = lax.axis_index("role")
    grad_local = grad_parts[0, 0].astype(jnp.float32)
    grad_sum = lax.psum_scatter(
        grad_local.astype(jnp.bfloat16), "dp", scatter_dimension=2, tiled=True
    ).astype(jnp.float32)
    new_master = adam_update(grad_sum, master[0], moment1[0], moment2[0])
    sending = new_master.astype(jnp.bfloat16)
    full_rows = lax.all_gather(sending, "dp", axis=2, tiled=True)
    received = passed_along(full_rows, "role", 1)
    quarter = sending.shape[2]
    own_columns = lax.dynamic_slice_in_dim(
        received, lax.axis_index("dp") * quarter, quarter, 2
    ).astype(jnp.float32)
    weights_after = jnp.where(role_index == 0, new_master, own_columns)[None]
    up_rows = received[:, 0, :]
    down_rows = received[:, 1, :]
    cache = kv_cache[0]
    keys = cache[..., :HEAD]
    values = cache[..., HEAD:]
    local_width = hidden_in.shape[2]
    per_group = local_width // HEAD
    row_count = hidden_in.shape[0]
    feature_start = lax.axis_index("tensor") * local_width
    gain_attn = lax.dynamic_slice_in_dim(attn_gain, feature_start, local_width)
    gain_ffn = lax.dynamic_slice_in_dim(ffn_gain, feature_start, local_width)
    fresh_keys = []
    fresh_values = []
    outputs = []
    for step in range(STEPS):
        hidden = hidden_in[:, step, :].astype(jnp.float32)
        squares = lax.psum(jnp.sum(hidden * hidden, axis=1), "tensor")
        normed = (hidden * lax.rsqrt(squares / D + norm_eps)[:, None] * gain_attn).astype(
            jnp.bfloat16
        )
        query = normed.reshape(row_count, 1, per_group, HEAD)
        fresh_keys.append(jnp.flip(query[:, :, 0, :], axis=-1))
        fresh_values.append(query[:, :, 1, :])
        attended = attend(
            query,
            keys,
            values,
            lengths,
            jnp.stack(fresh_keys, axis=2),
            jnp.stack(fresh_values, axis=2),
        )
        middle = hidden + attended.reshape(row_count, local_width)
        mid_squares = lax.psum(jnp.sum(middle * middle, axis=1), "tensor")
        ffn_in = (middle * lax.rsqrt(mid_squares / D + norm_eps)[:, None] * gain_ffn).astype(
            jnp.bfloat16
        )
        upper = lax.dot_general(
            lax.all_gather(ffn_in, "tensor", axis=1, tiled=True),
            up_rows,
            (((1,), (1,)), ((), ())),
            preferred_element_type=jnp.float32,
        )
        active = jnp.square(jnp.maximum(upper, 0.0)).astype(jnp.bfloat16)
        partial_out = jnp.dot(active, down_rows, preferred_element_type=jnp.float32)
        ffn_out = lax.psum_scatter(
            partial_out.astype(jnp.bfloat16), "tensor", scatter_dimension=1, tiled=True
        ).astype(jnp.float32)
        outputs.append((middle + ffn_out).astype(jnp.bfloat16))
    decoded_local = jnp.stack(outputs, axis=1)
    returned = passed_along(decoded_local, "role", -1)
    decoded = jnp.where(role_index == 0, returned, decoded_local)
    return (weights_after, decoded)


def solution(mesh):
    in_specs = (
        P("role", "dp", "tensor", None, None),
        P("role", "tensor", None, "dp"),
        P("role", "tensor", None, "dp"),
        P("role", "tensor", None, "dp"),
        P("role", "dp", "tensor", None, None),
        P("dp", None, "tensor"),
        P(),
        P(),
        P("dp"),
    )
    out_specs = (P("role", "tensor", None, "dp"), P("dp", None, "tensor"))
    return jax.shard_map(body, mesh=mesh, in_specs=in_specs, out_specs=out_specs, check_vma=False)
```

profile of v0, /device:TPU:38, one launch (start us, length us, event | category | flops | bytes accessed | tf_op | source)
XLA Modules:
  0.0 704.7 jit_solution(1777162413560525329)
XLA Ops:
  7.2 2.6 copy.198
  10.5 0.7 reshape.554
  11.2 0.7 reshape.552
  11.9 0.7 reshape.551
  12.6 54.8 %all-reduce.1 = (f32[16]{0:T(128)S(1)}, f32[16]{0:T(128)}, f32[16]{0:T(128)S(1)}, f32[16]{0:T(128)}) all-reduce(f32[16]{0:T(128)S(1)} %get-tuple-element.67, f32[16]{0:T(128)S(1)} %get-tuple-element.68, f32[16]{0:T(128)S(1)} %get-tuple-element.69, f32[16]{0:T(128)S(1)} %get-tuple-element.70), channel_id=1, replica_groups=mesh['role'=2,'dp'=4,'tensor'=32] {'tensor'}, use_global_device_ids=true, to_apply=%region_27.28 | all-reduce | flops 64 | bytes 512 | tf_op jit(solution)/shard_map/psum | solution.py:95
  67.4 0.8 dynamic_slice.10
  68.9 0.7 add_rsqrt_fusion.3
  69.6 0.7 reshape.558
  70.3 1.6 multiply_convert_fusion.6
  72.8 0.7 slice_bitcast_fusion.28
  73.5 2.9 copy.112
  76.4 0.7 iota_compare_fusion
  80.2 2.0 fusion.108
  82.3 1.9 fusion.110
  84.7 0.8 fusion.27
  86.1 0.8 fusion.26
  87.6 0.7 copy.200
  88.3 0.8 reverse
  89.1 0.7 add.180
  89.8 0.7 add.173
  90.6 0.8 multiply_convert_fusion.7
  91.3 0.8 fusion.79
  92.2 1.1 fusion.112
  94.1 1.4 multiply_reduce_fusion.2
  95.5 1.2 fusion.13
  96.7 1.7 multiply_reduce_fusion.3
  98.3 3.0 fusion.100
  101.6 0.8 dynamic_slice.11
  103.0 0.9 reshape.536
  104.0 0.9 reshape.539
  104.9 2.3 multiply_reduce_fusion.1
  107.2 0.9 reshape.542
  108.2 1.1 fusion.107
  109.2 1.1 fusion.106
  111.8 53.0 %all-reduce = (f32[16]{0:T(128)S(1)}, f32[16]{0:T(128)S(1)}, f32[16]{0:T(128)S(1)}, f32[16]{0:T(128)S(1)}) all-reduce(f32[16]{0:T(128)S(1)} %get-tuple-element.49, f32[16]{0:T(128)} %get-tuple-element.55, f32[16]{0:T(128)S(1)} %copy-done.37, f32[16]{0:T(128)} %get-tuple-element.65), channel_id=1, replica_groups=mesh['role'=2,'dp'=4,'tensor'=32] {'tensor'}, use_global_device_ids=true, to_apply=%region_33.34 | all-reduce | flops 64 | bytes 512 | tf_op jit(solution)/shard_map/psum | solution.py:111
  164.9 1.3 collective-permute-start
  166.3 36.5 %all-gather.3 = bf16[32,576,16]{1,2,0:T(8,128)(2,1)S(1)} all-gather(bf16[1,576,16]{1,2,0:T(8,128)(2,1)S(1)} %get-tuple-element.40), channel_id=1, replica_groups=mesh['role'=2,'dp'=4,'tensor'=32] {'tensor'}, dimensions={0}, use_global_device_ids=true | all-gather | bytes 608256 | tf_op jit(solution)/shard_map/all_gather | solution.py:116
  203.0 0.8 reshape.566
  203.8 1.0 convolution_convert_fusion
  204.7 3.2 copy.141
  208.1 32.3 %all-gather.2 = bf16[32,576,16]{1,2,0:T(8,128)(2,1)S(1)} all-gather(bf16[1,576,16]{1,2,0:T(8,128)(2,1)S(1)} %get-tuple-element.39), channel_id=1, replica_groups=mesh['role'=2,'dp'=4,'tensor'=32] {'tensor'}, dimensions={0}, use_global_device_ids=true | all-gather | bytes 608256 | tf_op jit(solution)/shard_map/all_gather | solution.py:116
  240.5 0.8 reshape.564
  241.3 1.0 convolution_convert_fusion.1
  242.3 3.4 copy.139
  245.7 35.0 %all-gather.1 = bf16[32,576,16]{1,2,0:T(8,128)(2,1)S(1)} all-gather(bf16[1,576,16]{1,2,0:T(8,128)(2,1)S(1)} %get-tuple-element.38), channel_id=1, replica_groups=mesh['role'=2,'dp'=4,'tensor'=32] {'tensor'}, dimensions={0}, use_global_device_ids=true | all-gather | bytes 608256 | tf_op jit(solution)/shard_map/all_gather | solution.py:116
  280.8 0.8 reshape.562
  281.6 1.0 convolution_convert_fusion.2
  282.6 3.3 copy.137
  286.0 32.4 %all-gather = bf16[32,576,16]{1,2,0:T(8,128)(2,1)S(1)} all-gather(bf16[1,576,16]{1,2,0:T(8,128)(2,1)S(1)} %get-tuple-element.37), channel_id=1, replica_groups=mesh['role'=2,'dp'=4,'tensor'=32] {'tensor'}, dimensions={0}, use_global_device_ids=true | all-gather | bytes 608256 | tf_op jit(solution)/shard_map/all_gather | solution.py:116
  318.5 0.8 reshape.560
  319.3 1.0 convolution_convert_fusion.3
  320.3 3.3 copy.135
  323.6 3.6 reduce-scatter.22.cloned.1.call-done
  327.2 1.0 copy.142
  328.2 120.0 %reduce-scatter.20.cloned.1.call-done = bf16[576,16]{1,0:T(8,128)(2,1)} async-done(((bf16[18432,16]{1,0:T(8,128)(2,1)}), bf16[576,16]{1,0:T(8,128)(2,1)}) %reduce-scatter.20.cloned.1.call-update) | async-done | bytes 18448
  448.2 1.0 copy.140
  449.2 120.2 %reduce-scatter.18.cloned.1.call-done = bf16[576,16]{1,0:T(8,128)(2,1)} async-done(((bf16[18432,16]{1,0:T(8,128)(2,1)}), bf16[576,16]{1,0:T(8,128)(2,1)}) %reduce-scatter.18.cloned.1.call-update) | async-done | bytes 18448
  569.4 1.0 copy.138
  570.5 120.3 %reduce-scatter.16.cloned.1.call-done = bf16[576,16]{1,0:T(8,128)(2,1)} async-done(((bf16[18432,16]{1,0:T(8,128)(2,1)}), bf16[576,16]{1,0:T(8,128)(2,1)}) %reduce-scatter.16.cloned.1.call-update) | async-done | bytes 18448
  690.8 1.0 copy.136
  691.9 3.3 collective-permute-start.1
  695.2 1.3 copy.130
  696.5 0.7 collective-permute-done.1
  697.2 0.7 copy.131
  (156 shorter events, 11.2 us)
Async XLA Ops:
  7.2 2.8 copy-start.3
  7.2 91.2 %reduce-scatter.14.cloned.1.call-start = ((), (), s32[]{:S(2)}) async-start(), calls=%async_computation.5 | async-start | bytes 1474560 | tf_op jit(solution)/shard_map/reduce_scatter | solution.py:67
  9.9 63.7 %copy-start = (bf16[1,16,1,256,384]{4,3,2,1,0:T(8,128)(2,1)S(1)}, bf16[1,16,1,256,384]{4,3,2,1,0:T(8,128)(2,1)}, u32[]{:S(2)}) copy-start(bf16[1,16,1,256,384]{4,3,2,1,0:T(8,128)(2,1)} %param.13) | copy-start | bytes 9437188
  9.9 155.0 %all-gather.6.cloned.1.call-start = ((), (), s32[]{:S(2)}) async-start(), calls=%async_computation.6 | async-start | bytes 1474560 | tf_op jit(solution)/shard_map/all_gather | solution.py:72
  67.4 5.5 copy-start.31
  68.2 4.6 copy-start.13
  68.9 3.9 copy-start.30
  68.9 3.0 copy-start.34
  69.6 3.2 copy-start.32
  73.5 2.9 copy-start.36
  73.5 3.6 copy-start.6
  73.5 4.2 copy-start.5
  73.5 5.7 copy-start.4
  78.4 3.9 copy-start.29
  80.0 2.2 copy-start.11
  80.1 4.3 copy-start.20
  80.2 4.2 copy-start.21
  80.2 4.0 copy-start.14
  80.2 4.0 copy-start.35
  80.2 4.2 copy-start.9
  80.2 4.2 copy-start.19
  80.2 4.2 copy-start.33
  80.2 11.9 %copy-start.1 = (bf16[1,16,1,256,384]{3,4,1,2,0:T(8,128)(2,1)S(1)}, bf16[1,16,1,256,384]{3,4,1,2,0:T(8,128)(2,1)}, u32[]{:S(2)}) copy-start(bf16[1,16,1,256,384]{3,4,1,2,0:T(8,128)(2,1)} %copy.112) | copy-start | bytes 9437188
  84.2 2.7 copy-start.7
  84.5 2.4 copy-start.22
  84.7 2.2 copy-start.16
  89.1 4.5 copy-start.8
  89.8 5.6 copy-start.28
  92.2 1.9 copy-start.12
  92.2 1.9 copy-start.18
  92.2 1.9 copy-start.23
  92.2 1.9 copy-start.26
  98.3 3.1 copy-start.17
  98.3 6.6 copy-start.10
  98.3 9.8 %copy-start.15 = (f32[3,192]{1,0:T(4,128)S(1)}, f32[3,192]{1,0:T(4,128)}, u32[]{:S(2)}) copy-start(f32[3,192]{1,0:T(4,128)} %copy-done.13) | copy-start | bytes 6916
  101.4 225.8 %reduce-scatter.22.cloned.1.call-start = ((), (), s32[]{:S(2)}) async-start(), calls=%async_computation.10 | async-start | bytes 4866048
  110.4 0.9 copy-start.24
  110.4 0.9 copy-start.25
  110.4 1.0 copy-start.27
  110.4 1.4 copy-start.37
  164.9 38.9 %collective-permute-start = (bf16[16,2,18432]{2,0,1:T(8,128)(2,1)}, bf16[16,2,18432]{2,0,1:T(8,128)(2,1)S(1)}, u32[]{:S(2)}, u32[]{:S(2)}) collective-permute-start(bf16[16,2,18432]{2,0,1:T(8,128)(2,1)} %all-gather.6.cloned.1.call-done), channel_id=1, source_target_pairs={{0,128},{1,129},{2,130},{3,131},{4,132},{5,133},{6,134},{7,135},{8... | collective-permute-start | bytes 3538952 | tf_op jit(solution)/shard_map/ppermute | solution.py:25
  208.0 240.2 %reduce-scatter.20.cloned.1.call-start = ((), (), s32[]{:S(2)}) async-start(), calls=%async_computation.9 | async-start | bytes 4866048
  245.7 323.8 %reduce-scatter.18.cloned.1.call-start = ((), (), s32[]{:S(2)}) async-start(), calls=%async_computation.8 | async-start | bytes 4866048
  285.9 404.9 %reduce-scatter.16.cloned.1.call-start = ((), (), s32[]{:S(2)}) async-start(), calls=%async_computation.7 | async-start | bytes 4866048
  323.6 371.5 %copy-start.2 = (f32[16,2,4608]{2,0,1:T(8,128)S(1)}, f32[16,2,4608]{2,0,1:T(8,128)}, u32[]{:S(2)}) copy-start(f32[16,2,4608]{2,0,1:T(8,128)} %get-tuple-element.21) | copy-start | bytes 1769476
  691.9 5.3 collective-permute-start.1
Sparse Core Ops, SparseCore 0:
  10.6 29.1 reduce-scatter.13
  101.5 27.5 all-gather.5
  208.1 119.0 reduce-scatter.21
  329.6 118.5 reduce-scatter.19
  450.6 118.7 reduce-scatter.17
  571.8 118.9 reduce-scatter.15
where the time goes:
time: 714 us; the launch traced here: 705 us
  waiting for transfers between devices  365 us (51%)
  blocking collectives  244 us (34%)
  local copies, waits for them, and re-layouts  42.5 us (6%)
  matrix products  20.4 us (3%)
  between operations  14.8 us (2%)
  other arithmetic  13.4 us (2%)
    unnamed x10, waiting for transfers between devices  364 us
    all_gather x4, blocking collectives, body(): lax.all_gather(ffn_in, 'tensor', axis=1, tiled=True)  136 us
    psum x1, blocking collectives, body(): squares = lax.psum(jnp.sum(hidden * hidden, axis=1), 'tensor')  54.8 us
    psum x1, blocking collectives, body(): mid_squares = lax.psum(jnp.sum(middle * middle, axis=1), 'tensor')  53 us
    unnamed x101, local copies, waits for them, and re-layouts  30.1 us
  transfers between devices with their start and end apart: 8, of which 5 were waited for; matrix products, arithmetic and copies ran while one was open for 9% of the time, Pallas kernels for 0%

commit v1 on v0

v1 whole, which is shorter than its diff:
```python
import functools
import math

import jax
import jax.numpy as jnp
from jax import lax
from jax.experimental import pallas as pl
from jax.experimental.pallas import tpu as pltpu
from jax.sharding import PartitionSpec as P

D = 18432
HEAD = 192
STEPS = 4
BAND = 8


beta_one = 0.9
beta_two = 0.95
rate_factor = 0.5
decay_rate = 0.1
adam_eps = 1e-08
norm_eps = 1e-05
step_count = 10


def adam_update(grad_sum, weights, first, second):
    learn_rate = rate_factor / math.sqrt(D)
    first_new = beta_one * first + (1.0 - beta_one) * grad_sum
    second_new = beta_two * second + (1.0 - beta_two) * grad_sum * grad_sum
    corr_one = 1.0 - beta_one**step_count
    corr_two = 1.0 - beta_two**step_count
    ratio = first_new / corr_one / (jnp.sqrt(second_new / corr_two) + adam_eps)
    return weights - learn_rate * (ratio + decay_rate * weights)


def to_lanes(column, lanes):
    rows = column.shape[0]
    here = lax.broadcasted_iota(jnp.int32, (rows, lanes), 0)
    lane = lax.broadcasted_iota(jnp.int32, (rows, lanes), 1)
    return jnp.sum(jnp.where(here == lane, column, 0.0), axis=0, keepdims=True)


def to_rows(line, rows):
    lanes = line.shape[1]
    here = lax.broadcasted_iota(jnp.int32, (rows, lanes), 0)
    lane = lax.broadcasted_iota(jnp.int32, (rows, lanes), 1)
    return jnp.sum(jnp.where(here == lane, line, 0.0), axis=1, keepdims=True)


def squares_kernel(hidden_ref, out_ref):
    hidden = hidden_ref[...]
    line = to_lanes(jnp.sum(hidden * hidden, axis=1, keepdims=True), 128)
    out_ref[...] = jnp.broadcast_to(line[None], out_ref.shape)


def attend_kernel(
    pairs,
    role_ref,
    len_ref,
    hidden_ref,
    squares_ref,
    gain_ref,
    flip_gain_ref,
    flip_ref,
    out_gain_ref,
    kv_ref,
    middle_ref,
    sent_ref,
    normed_ref,
    hidden_parts_ref,
    flip_normed_ref,
):
    step = pl.program_id(0)
    groups = normed_ref.shape[0]
    rows = hidden_ref.shape[0]
    scale = 1.0 / math.sqrt(HEAD)

    @pl.when(role_ref[0] == 1)
    def _():
        @pl.when(step == 0)
        def _():
            total = jnp.sum(squares_ref[...], axis=0)[0:1]
            factor = lax.rsqrt(to_rows(total, rows) / D + norm_eps)
            hidden = hidden_ref[...]
            normed = hidden * factor * gain_ref[...]
            for q in range(groups):
                part = slice(q * HEAD, (q + 1) * HEAD)
                normed_ref[q] = normed[:, part]
                hidden_parts_ref[q] = hidden[:, part]
            flip_normed_ref[...] = flip_ref[...] * factor * flip_gain_ref[...]

        high = lax.broadcasted_iota(jnp.int32, (groups * 8, 1), 0) % 8 >= 4
        row_id = lax.broadcasted_iota(jnp.int32, (groups * 8, 8), 0) % 8
        col_id = lax.broadcasted_iota(jnp.int32, (groups * 8, 8), 1)
        fresh_ok = (row_id // 4 == col_id // 4) & (col_id % 4 <= row_id % 4)
        context = kv_ref.shape[1]
        position = lax.broadcasted_iota(jnp.int32, (groups * 8, context), 1)
        for p in range(pairs):
            pair = step * pairs + p
            first = pl.multiple_of(pair * 8, 8)
            query = jnp.concatenate(
                [normed_ref[q, pl.ds(first, 8), :] for q in range(groups)], axis=0
            ).astype(jnp.bfloat16)
            new_keys = flip_normed_ref[pl.ds(first, 8), :].astype(jnp.bfloat16)
            new_values = normed_ref[1, pl.ds(first, 8), :].astype(jnp.bfloat16)
            contract = (((1,), (1,)), ((), ()))
            scores = []
            for half in range(2):
                keys = kv_ref[2 * p + half, :, :HEAD]
                scores.append(
                    lax.dot_general(query, keys, contract, preferred_element_type=jnp.float32)
                )
            cache = jnp.where(high, scores[1], scores[0]) * scale
            length = jnp.where(high, len_ref[2 * pair + 1], len_ref[2 * pair])
            cache = jnp.where(position < length, cache, -jnp.inf)
            fresh = (
                lax.dot_general(query, new_keys, contract, preferred_element_type=jnp.float32)
                * scale
            )
            fresh = jnp.where(fresh_ok, fresh, -jnp.inf)
            top = jnp.maximum(
                jnp.max(cache, axis=1, keepdims=True), jnp.max(fresh, axis=1, keepdims=True)
            )
            cache = jnp.exp(cache - top)
            fresh = jnp.exp(fresh - top)
            total = jnp.sum(cache, axis=1, keepdims=True) + jnp.sum(fresh, axis=1, keepdims=True)
            cache = (cache / total).astype(jnp.bfloat16)
            fresh = (fresh / total).astype(jnp.bfloat16)
            weighed = []
            for half in range(2):
                values = kv_ref[2 * p + half, :, HEAD:]
                weighed.append(jnp.dot(cache, values, preferred_element_type=jnp.float32))
            attended = jnp.where(high, weighed[1], weighed[0]) + jnp.dot(
                fresh, new_values, preferred_element_type=jnp.float32
            )
            for q in range(groups):
                middle_ref[pl.ds(first, 8), q * HEAD : (q + 1) * HEAD] = (
                    hidden_parts_ref[q, pl.ds(first, 8), :] + attended[q * 8 : (q + 1) * 8]
                )

        @pl.when(step == pl.num_programs(0) - 1)
        def _():
            middle = middle_ref[...]
            width = middle.shape[1]
            squares = jnp.sum(middle * middle, axis=1, keepdims=True)
            high_part = squares.astype(jnp.bfloat16).astype(jnp.float32)
            mid_part = (squares - high_part).astype(jnp.bfloat16).astype(jnp.float32)
            low_part = squares - high_part - mid_part
            lane = lax.broadcasted_iota(jnp.int32, (rows, sent_ref.shape[1] - width), 1)
            tail = jnp.where(
                lane == 0,
                high_part,
                jnp.where(lane == 1, mid_part, jnp.where(lane == 2, low_part, 0.0)),
            )
            sent_ref[:, :width] = (middle * out_gain_ref[...]).astype(jnp.bfloat16)
            sent_ref[:, width:] = tail.astype(jnp.bfloat16)


def up_kernel(place_ref, x_ref, w0_ref, w1_ref, w2_ref, w3_ref, out_ref):
    copies, height, units = out_ref.shape
    bands, rows, wide = x_ref.shape
    width = w0_ref.shape[3]
    total = jnp.zeros((rows, units), jnp.float32)
    for k, w_ref in enumerate((w0_ref, w1_ref, w2_ref, w3_ref)):
        features = x_ref[lax.rem(place_ref[0] + bands - k, bands)][:, :width]
        weights = w_ref[:, 0].reshape(units, width)
        total += lax.dot_general(
            features, weights, (((1,), (1,)), ((), ())), preferred_element_type=jnp.float32
        )
    squares = jnp.zeros((rows, 1), jnp.float32)
    for band in range(bands):
        squares += jnp.sum(x_ref[band][:, width:].astype(jnp.float32), axis=1, keepdims=True)
    line = jnp.broadcast_to(to_lanes(squares, units), (height - rows, units))
    for copy in range(copies):
        out_ref[copy, :rows] = total
        out_ref[copy, rows:] = line


def down_kernel(place_ref, sums_ref, w0_ref, w1_ref, w2_ref, w3_ref, out_ref):
    bands, rows, width = out_ref.shape
    total = jnp.sum(sums_ref[...], axis=0)
    factor = lax.rsqrt(to_rows(total[rows : rows + 1], rows) / D + norm_eps)
    upper = jnp.maximum(total[:rows] * factor, 0.0)
    active = (upper * upper).astype(jnp.bfloat16)
    for k, w_ref in enumerate((w0_ref, w1_ref, w2_ref, w3_ref)):
        weights = w_ref[:, 1].reshape(active.shape[1], width)
        out_ref[lax.rem(place_ref[0] + bands - k, bands)] = jnp.dot(
            active, weights, preferred_element_type=jnp.float32
        ).astype(jnp.bfloat16)


VMEM = pl.BlockSpec(memory_space=pltpu.VMEM)
SMEM = pl.BlockSpec(memory_space=pltpu.SMEM)


def whole(shape):
    return pl.BlockSpec(shape, lambda i: (0,) * len(shape))


def attend(role, lengths, hidden, squares, gain, flip_gain, flip, out_gain, kv):
    rows, width = hidden.shape
    count = kv.shape[0]
    groups = width // HEAD
    pairs = 2
    block = (2 * pairs,) + kv.shape[1:]
    return pl.pallas_call(
        functools.partial(attend_kernel, pairs),
        grid=(count // (2 * pairs),),
        out_shape=(
            jax.ShapeDtypeStruct((rows, width), jnp.float32),
            jax.ShapeDtypeStruct((rows, 640), jnp.bfloat16),
        ),
        in_specs=[
            SMEM,
            SMEM,
            whole(hidden.shape),
            whole(squares.shape),
            whole(gain.shape),
            whole(flip_gain.shape),
            whole(flip.shape),
            whole(out_gain.shape),
            pl.BlockSpec(block, lambda i: (i, 0, 0)),
        ],
        out_specs=(whole((rows, width)), whole((rows, 640))),
        scratch_shapes=[
            pltpu.VMEM((groups, rows, HEAD), jnp.float32),
            pltpu.VMEM((groups, rows, HEAD), jnp.float32),
            pltpu.VMEM((rows, HEAD), jnp.float32),
        ],
        compiler_params=pltpu.CompilerParams(vmem_limit_bytes=24 * 1024 * 1024),
    )(role, lengths, hidden, squares, gain, flip_gain, flip, out_gain, kv)


def body(grad_parts, master, moment1, moment2, kv_cache, hidden_in, attn_gain, ffn_gain, lengths):
    role_index = lax.axis_index("role")
    place = lax.axis_index("dp")
    shards = lax.axis_size("dp")
    tensor = lax.axis_size("tensor")
    bands = tensor // BAND
    bf16 = jnp.bfloat16
    band_groups = [[b * BAND + m for m in range(BAND)] for b in range(bands)]
    member_groups = [[b * BAND + m for b in range(bands)] for m in range(BAND)]
    quarter = master.shape[3]

    def learner_pairs(by):
        return [(i, (i + by) % shards) for i in range(shards)]

    grads = grad_parts[0, 0]

    def grad_quarter(owner):
        return lax.dynamic_slice_in_dim(grads, owner * quarter, quarter, 2)

    arriving = [
        lax.ppermute(grad_quarter((place + k) % shards), ("role", "dp"), learner_pairs(k))
        for k in range(1, shards)
    ]

    row_count, steps, width = hidden_in.shape
    rows = row_count * steps
    hidden = hidden_in.astype(jnp.float32).reshape(rows, width)
    squares = pl.pallas_call(
        squares_kernel,
        out_shape=jax.ShapeDtypeStruct((tensor, 8, 128), jnp.float32),
        in_specs=[VMEM],
        out_specs=VMEM,
    )(hidden)
    squares = lax.all_to_all(squares, "tensor", 0, 0, tiled=True)

    feature_start = lax.axis_index("tensor") * width
    gain_attn = lax.dynamic_slice_in_dim(attn_gain, feature_start, width)[None]
    gain_ffn = lax.dynamic_slice_in_dim(ffn_gain, feature_start, width)[None]
    middle, outgoing = attend(
        role_index.astype(jnp.int32)[None],
        lengths,
        hidden,
        squares,
        gain_attn,
        jnp.flip(gain_attn[:, :HEAD], axis=1),
        jnp.flip(hidden[:, :HEAD], axis=1),
        gain_ffn,
        kv_cache[0, :, 0],
    )
    features = lax.ppermute(outgoing, "role", [(1, 0)])
    middle_home = lax.ppermute(middle, "role", [(1, 0)])

    grad_sum = grad_quarter(place).astype(jnp.float32)
    for part in arriving:
        grad_sum = grad_sum + part.astype(jnp.float32)
    new_master = adam_update(grad_sum, master[0], moment1[0], moment2[0])
    synced = new_master.astype(bf16)
    copied = lax.ppermute(synced, "role", [(0, 1)])
    weights_after = jnp.where(role_index == 0, new_master, copied.astype(jnp.float32))[None]

    units = synced.shape[0]
    blocks = synced.reshape(units, 2, BAND, width).transpose(2, 1, 0, 3)
    own = lax.all_to_all(blocks, "tensor", 0, 0, tiled=True, axis_index_groups=band_groups)
    slabs = [own] + [
        lax.ppermute(own, ("role", "dp"), learner_pairs(k)) for k in range(1, shards)
    ]
    gathered = lax.all_to_all(
        jnp.broadcast_to(features[None], (bands,) + features.shape),
        "tensor",
        0,
        0,
        tiled=True,
        axis_index_groups=member_groups,
    )
    place_operand = place.astype(jnp.int32)[None]
    sums = pl.pallas_call(
        up_kernel,
        out_shape=jax.ShapeDtypeStruct((BAND, rows + 8, BAND * units), jnp.float32),
        in_specs=[SMEM] + [VMEM] * 5,
        out_specs=VMEM,
    )(place_operand, gathered, *slabs)
    sums = lax.all_to_all(sums, "tensor", 0, 0, tiled=True, axis_index_groups=band_groups)
    parts = pl.pallas_call(
        down_kernel,
        out_shape=jax.ShapeDtypeStruct((bands, rows, width), bf16),
        in_specs=[SMEM] + [VMEM] * 5,
        out_specs=VMEM,
    )(place_operand, sums, *slabs)
    parts = lax.all_to_all(parts, "tensor", 0, 0, tiled=True, axis_index_groups=member_groups)
    decoded = (middle_home + jnp.sum(parts.astype(jnp.float32), axis=0)).astype(bf16)
    decoded = decoded.reshape(row_count, steps, width)
    returned = lax.ppermute(decoded, "role", [(0, 1)])
    decoded = jnp.where(role_index == 0, decoded, returned)
    return (weights_after, decoded)


def solution(mesh):
    in_specs = (
        P("role", "dp", "tensor", None, None),
        P("role", "tensor", None, "dp"),
        P("role", "tensor", None, "dp"),
        P("role", "tensor", None, "dp"),
        P("role", "dp", "tensor", None, None),
        P("dp", None, "tensor"),
        P(),
        P(),
        P("dp"),
    )
    out_specs = (P("role", "tensor", None, "dp"), P("dp", None, "tensor"))
    return jax.shard_map(body, mesh=mesh, in_specs=in_specs, out_specs=out_specs, check_vma=False)
```

time: 714 us -> 132 us (0.18); the launches traced: 705 us -> 130 us
  waiting for transfers between devices: 365 us -> 22.3 us
  blocking collectives: 244 us -> 13.8 us
  starting transfers between devices: 4.8 us -> 60.9 us
  local copies, waits for them, and re-layouts: 42.5 us -> 13.7 us
  matrix products: 20.4 us -> 0 us
  between operations: 14.8 us -> 0.91 us
  Pallas kernels: 0 us -> 11.6 us
    unnamed x10 -> x0, waiting for transfers between devices: 364 us -> none
    all_gather x4 -> x0, blocking collectives: 136 us -> none  [body(): lax.all_gather(ffn_in, 'tensor', axis=1, tiled=True)]
    psum x2 -> x0, blocking collectives: 108 us -> none  [the longest x1 54.8 us: body(): squares = lax.psum(jnp.sum(hidden * hidden, axis=1), 'tensor')]
    ppermute x2 -> x10, starting transfers between devices: 4.55 us -> 34.2 us  [the longest x1 19.7 us: body(): middle_home = lax.ppermute(middle, 'role', [(1, 0)])]
    all_to_all x0 -> x4, starting transfers between devices: none -> 26.7 us  [the longest x1 9.63 us: body(): squares = lax.all_to_all(squares, 'tensor', 0, 0, tiled=True)]
    unnamed x101 -> x32, local copies, waits for them, and re-layouts: 30.1 us -> 5.14 us
    dot_general x19 -> x0, matrix products: 20.4 us -> none  [the longest x4 6.13 us: attend(): jnp.einsum('rgqe,rgce->rgqc', query, keys, preferred_element_type=jnp.flo...]
    all_to_all x0 -> x1, blocking collectives: none -> 13.8 us  [body(): lax.all_to_all(sums, 'tensor', 0, 0, tiled=True, axis_index_groups=band_g...]
  transfers between devices with their start and end apart: 8 -> 14, of which waited for: 5 -> 5; matrix products, arithmetic and copies ran while one was open for 9% -> 11% of each run, Pallas kernels for 0% -> 5%
where the time goes in v1:
time: 132 us; the launch traced here: 130 us
  starting transfers between devices  60.9 us (46%)
  waiting for transfers between devices  22.3 us (17%)
  blocking collectives  13.8 us (10%)
  local copies, waits for them, and re-layouts  13.7 us (10%)
  Pallas kernels  11.6 us (9%)
  other arithmetic  7.04 us (5%)
    ppermute x1, starting transfers between devices, body(): middle_home = lax.ppermute(middle, 'role', [(1, 0)])  19.7 us
    all_to_all x1, blocking collectives, body(): lax.all_to_all(sums, 'tensor', 0, 0, tiled=True, axis_index_groups=band_g...  13.8 us
    all_to_all x1, starting transfers between devices, body(): squares = lax.all_to_all(squares, 'tensor', 0, 0, tiled=True)  9.63 us
    all_to_all x1, waiting for transfers between devices, body(): lax.all_to_all(jnp.broadcast_to(features[None], (bands,) + features.shape...  9.57 us
    ppermute x1, waiting for transfers between devices, body(): copied = lax.ppermute(synced, 'role', [(0, 1)])  7.98 us
    all_to_all x1, starting transfers between devices, body(): lax.all_to_all(jnp.broadcast_to(features[None], (bands,) + features.shape...  7.54 us
    ppermute x1, starting transfers between devices, body(): features = lax.ppermute(outgoing, 'role', [(1, 0)])  7.21 us
    convert_element_type x1, other arithmetic, body(): synced = new_master.astype(bf16)  5.2 us
  transfers between devices with their start and end apart: 14, of which 5 were waited for; matrix products, arithmetic and copies ran while one was open for 11% of the time, Pallas kernels for 5%

profile of v1, /device:TPU:38, one launch (start us, length us, event | category | flops | bytes accessed | tf_op | source)
XLA Modules:
  0.0 130.3 jit_solution(7759077133217364114)
XLA Ops:
  0.6 0.0 copy-start.13
  0.7 1.8 %dynamic-slice_bitcast_fusion.2 = (bf16[16,2,4608]{2,1,0:T(2,128)(2,1)S(1)}, bf16[16,2,4608]{2,1,0:T(2,128)(2,1)S(1)}, bf16[16,2,4608]{2,1,0:T(2,128)(2,1)S(1)}) fusion(bf16[1,1,16,2,18432]{4,3,2,1,0:T(2,128)(2,1)} %param.9, s32[]{:T(128)S(6)} %select_n.50, s32[]{:T(128)S(6)} %select_n.54, s32[]{:T(128)S(6)} %select_n.52), kind=kLoop, calls=%fused_computation.19 | loop fusion | bytes 1769484 | tf_op jit(solution)/shard_map/dynamic_slice | solution.py:251
  2.4 0.7 collective-permute-start
  3.1 0.7 collective-permute-start.2
  3.8 1.4 %collective-permute-start.1 = (bf16[16,2,4608]{2,1,0:T(2,128)(2,1)S(1)}, bf16[16,2,4608]{2,1,0:T(2,128)(2,1)}, u32[]{:S(2)}, u32[]{:S(2)}) collective-permute-start(bf16[16,2,4608]{2,1,0:T(2,128)(2,1)S(1)} %get-tuple-element.10), channel_id=1, source_target_pairs={{0,64},{32,96},{64,0},{96,32},{1,65},{33,97},{65,1},{97,33},{2,66}... | collective-permute-start | bytes 884744 | tf_op jit(solution)/shard_map/ppermute | solution.py:254
  5.2 0.0 copy-done.13
  5.2 0.7 reshape.32.hidden_ref
  5.9 1.7 %shard_map.104 = f32[32,8,128]{2,1,0:T(8,128)} custom-call(f32[64,576]{1,0:T(8,128)} %reshape.32.hidden_ref), custom_call_target="tpu_custom_call" | custom-call | tf_op jit(solution)/shard_map/pallas_call | solution.py:261
  7.6 9.6 %all-to-all-start = ((f32[32,8,128]{2,1,0:T(8,128)}), f32[32,8,128]{2,1,0:T(8,128)S(1)}, u32[]{:S(2)}, u32[]{:S(2)}) async-start(f32[32,8,128]{2,1,0:T(8,128)} %shard_map.104), calls=%async_computation | async-start | bytes 262144 | tf_op jit(solution)/shard_map/all_to_all | solution.py:267
  17.2 0.0 collective-permute-done
  17.2 0.0 copy-start.11
  17.2 0.0 collective-permute-done.2
  17.2 0.7 copy-done.11
  18.0 0.7 copy-done.12
  18.7 0.0 collective-permute-done.1
  18.7 5.2 %fusion.9 = (bf16[16,2,4608]{2,1,0:T(2,128)(2,1)}, f32[16,2,4608]{2,1,0:T(2,128)}) fusion(f32[1,16,2,4608]{3,2,1,0:T(2,128)} %param.12, bf16[16,2,4608]{2,1,0:T(2,128)(2,1)} %copy-done.12, bf16[16,2,4608]{2,1,0:T(2,128)(2,1)} %collective-permute-done.1, bf16[16,2,4608]{2,1,0:T(2,128)(2,1)} %copy-done.11, bf16[1,1,16,2,18432]{4,3,2,1,0:T(2,128)(2,1)} %param.9, ...), kind=kLoop, calls=%fused_computation.22 | loop fusion | flops 3391488 | bytes 3833860 | tf_op jit(solution)/shard_map/convert_element_type | solution.py:290
  23.9 2.1 %reshape.33 = bf16[16,2,8,576]{3,2,1,0:T(8,128)(2,1)} reshape(bf16[16,2,4608]{2,1,0:T(2,128)(2,1)} %get-tuple-element.6) | data formatting | bytes 589824 | tf_op jit(solution)/shard_map/reshape | solution.py:295
  25.9 1.7 %copy.16 = bf16[16,2,8,576]{3,0,1,2:T(8,128)(2,1)} copy(bf16[16,2,8,576]{3,2,1,0:T(8,128)(2,1)} %reshape.33) | data formatting | bytes 589824 | tf_op jit(solution)/shard_map/reshape | solution.py:295
  27.7 0.0 all-to-all-done.squares_ref
  27.7 5.1 %all-to-all-start.2 = ((bf16[8,2,16,576]{3,2,1,0:T(8,128)(2,1)}), bf16[8,2,16,576]{3,2,1,0:T(8,128)(2,1)}, u32[]{:S(2)}, u32[]{:S(2)}) async-start(bf16[8,2,16,576]{3,2,1,0:T(8,128)(2,1)} %bitcast.51), calls=%async_computation.2 | async-start | bytes 655360 | tf_op jit(solution)/shard_map/all_to_all | solution.py:296
  32.8 0.8 dynamic_slice.31
  33.6 0.2 reverse
  33.8 0.1 slice.10.flip_gain_ref
  33.8 0.8 dynamic_slice.32
  34.6 0.0 slice-done
  34.6 0.8 reverse.1
  35.4 0.9 slice.11.flip_ref
  36.3 0.0 copy-done
  36.3 0.0 copy-done.1
  36.3 0.0 copy-done.2
  36.4 5.0 %shard_map.105 = (f32[64,576]{1,0:T(8,128)S(1)}, bf16[64,640]{1,0:T(8,128)(2,1)S(1)}) custom-call(s32[1]{0:T(128)} %bitcast.8.role_ref, s32[16]{0:T(128)S(1)} %copy-done.2, f32[64,576]{1,0:T(8,128)S(1)} %copy-done.1, f32[32,8,128]{2,1,0:T(8,128)S(1)} %all-to-all-done.squares_ref, f32[1,576]{1,0:T(1,128)S(1)} %broadcast_in_dim.23.gain_ref, ...), custom_call_target="tpu_custom_call" | custom-call | tf_op jit(solution)/shard_map/pallas_call | solution.py:206
  41.4 0.7 copy-done.3
  42.0 7.2 %collective-permute-start.5 = (bf16[64,640]{1,0:T(8,128)(2,1)S(1)}, bf16[64,640]{1,0:T(8,128)(2,1)S(1)}, u32[]{:S(2)}, u32[]{:S(2)}) collective-permute-start(bf16[64,640]{1,0:T(8,128)(2,1)S(1)} %get-tuple-element.5), channel_id=1, source_target_pairs={{128,0},{129,1},{130,2},{131,3},{132,4},{133,5},{134,6},{135,7},{1... | collective-permute-start | bytes 245768 | tf_op jit(solution)/shard_map/ppermute | solution.py:283
  49.3 2.0 %collective-permute-done.5 = bf16[64,640]{1,0:T(8,128)(2,1)S(1)} collective-permute-done((bf16[64,640]{1,0:T(8,128)(2,1)S(1)}, bf16[64,640]{1,0:T(8,128)(2,1)S(1)}, u32[]{:S(2)}, u32[]{:S(2)}) %collective-permute-start.5) | collective-permute-done | bytes 81952 | tf_op jit(solution)/shard_map/ppermute | solution.py:283
  51.3 0.0 all-to-all-done.2.w0_ref
  51.3 0.7 broadcast_in_dim.26
  52.0 7.5 %all-to-all-start.1 = ((bf16[4,64,640]{2,1,0:T(8,128)(2,1)}), bf16[4,64,640]{2,1,0:T(8,128)(2,1)S(1)}, u32[]{:S(2)}, u32[]{:S(2)}) async-start(bf16[4,64,640]{2,1,0:T(8,128)(2,1)} %broadcast_in_dim.26), calls=%async_computation.1 | async-start | bytes 655360 | tf_op jit(solution)/shard_map/all_to_all | solution.py:300
  59.6 0.7 collective-permute-start.8
  60.3 0.7 collective-permute-start.7
  60.9 0.7 collective-permute-start.6
  61.6 9.6 %all-to-all-done.1.x_ref = bf16[4,64,640]{2,1,0:T(8,128)(2,1)S(1)} async-done(((bf16[4,64,640]{2,1,0:T(8,128)(2,1)}), bf16[4,64,640]{2,1,0:T(8,128)(2,1)S(1)}, u32[]{:S(2)}, u32[]{:S(2)}) %all-to-all-start.1) | async-done | bytes 327712 | tf_op jit(solution)/shard_map/all_to_all | solution.py:300
  71.2 0.0 collective-permute-done.8.w3_ref
  71.2 0.0 collective-permute-done.7.w2_ref
  71.2 0.0 copy-start.8
  71.2 0.0 collective-permute-done.6.w1_ref
  71.2 0.0 copy-start.9
  71.2 0.7 copy-done.6
  71.9 0.1 copy-done.7
  72.1 0.1 copy-done.8
  72.2 0.1 copy-done.9
  72.3 2.5 %shard_map.106 = f32[8,72,128]{2,1,0:T(8,128)} custom-call(s32[1]{0:T(128)} %bitcast.10.place_ref, bf16[4,64,640]{2,1,0:T(8,128)(2,1)} %copy-done.6, bf16[8,2,16,576]{3,2,1,0:T(8,128)(2,1)} %all-to-all-done.2.w0_ref, bf16[8,2,16,576]{3,2,1,0:T(8,128)(2,1)} %copy-done.9, bf16[8,2,16,576]{3,2,1,0:T(8,128)(2,1)} %copy-done.8, bf16[8,2,16,576]{3,2,1,0:T(8,128)(2,1)} %copy-done.7), custom_call_target="tpu_custom_call" | custom-call | tf_op jit(solution)/shard_map/pallas_call | solution.py:309
  74.8 13.8 %all_to_all.25.sums_ref = f32[8,72,128]{2,1,0:T(8,128)} all-to-all(f32[8,72,128]{2,1,0:T(8,128)} %shard_map.106), channel_id=1, replica_groups={{0,1,2,3,4,5,6,7},{8,9,10,11,12,13,14,15},{16,17,18,19,20,21,22,23},{24..., dimensions={0} | all-to-all | bytes 589824 | tf_op jit(solution)/shard_map/all_to_all | solution.py:315
  88.5 2.5 %shard_map.107 = bf16[4,64,576]{2,1,0:T(8,128)(2,1)} custom-call(s32[1]{0:T(128)} %bitcast.10.place_ref, f32[8,72,128]{2,1,0:T(8,128)} %all_to_all.25.sums_ref, bf16[8,2,16,576]{3,2,1,0:T(8,128)(2,1)} %all-to-all-done.2.w0_ref, bf16[8,2,16,576]{3,2,1,0:T(8,128)(2,1)} %copy-done.9, bf16[8,2,16,576]{3,2,1,0:T(8,128)(2,1)} %copy-done.8, ...), custom_call_target="tpu_custom_call" | custom-call | tf_op jit(solution)/shard_map/pallas_call | solution.py:316
  91.0 4.4 %all-to-all-start.4 = ((bf16[4,64,576]{2,1,0:T(8,128)(2,1)}), bf16[4,64,576]{2,1,0:T(8,128)(2,1)S(1)}, u32[]{:S(2)}, u32[]{:S(2)}) async-start(bf16[4,64,576]{2,1,0:T(8,128)(2,1)} %shard_map.107), calls=%async_computation.4 | async-start | bytes 655360 | tf_op jit(solution)/shard_map/all_to_all | solution.py:322
  95.4 0.0 copy-done.4
  95.4 19.7 %collective-permute-start.4 = (f32[64,576]{1,0:T(8,128)S(1)}, f32[64,576]{1,0:T(8,128)S(1)}, u32[]{:S(2)}, u32[]{:S(2)}) collective-permute-start(f32[64,576]{1,0:T(8,128)S(1)} %copy-done.4), channel_id=1, source_target_pairs={{128,0},{129,1},{130,2},{131,3},{132,4},{133,5},{134,6},{135,7},{1... | collective-permute-start | bytes 442376 | tf_op jit(solution)/shard_map/ppermute | solution.py:284
  115.1 1.3 collective-permute-start.3
  116.4 0.0 all-to-all-done.4
  116.5 1.4 %collective-permute-done.4 = f32[64,576]{1,0:T(8,128)S(1)} collective-permute-done((f32[64,576]{1,0:T(8,128)S(1)}, f32[64,576]{1,0:T(8,128)S(1)}, u32[]{:S(2)}, u32[]{:S(2)}) %collective-permute-start.4) | collective-permute-done | bytes 147488 | tf_op jit(solution)/shard_map/ppermute | solution.py:284
  118.0 1.3 collective-permute-start.9
  119.3 8.0 %collective-permute-done.3 = bf16[16,2,4608]{2,1,0:T(2,128)(2,1)S(1)} collective-permute-done((bf16[16,2,4608]{2,1,0:T(2,128)(2,1)S(1)}, bf16[16,2,4608]{2,1,0:T(2,128)(2,1)S(1)}, u32[]{:S(2)}, u32[]{:S(2)}) %collective-permute-start.3) | collective-permute-done | bytes 294944 | tf_op jit(solution)/shard_map/ppermute | solution.py:291
  127.2 1.1 select_bitcast_fusion
  128.4 1.3 collective-permute-done.9
  129.7 0.6 broadcast_select_fusion
  (19 shorter events, 0.1 us)
Async XLA Ops:
  0.6 4.6 %copy-start.13 = (bf16[16,4,576]{2,1,0:T(4,128)(2,1)S(1)}, bf16[16,4,576]{2,1,0:T(4,128)(2,1)}, u32[]{:S(2)}) copy-start(bf16[16,4,576]{2,1,0:T(4,128)(2,1)} %param.14) | copy-start | bytes 221188
  2.4 14.8 %collective-permute-start = (bf16[16,2,4608]{2,1,0:T(2,128)(2,1)S(1)}, bf16[16,2,4608]{2,1,0:T(2,128)(2,1)S(1)}, u32[]{:S(2)}, u32[]{:S(2)}) collective-permute-start(bf16[16,2,4608]{2,1,0:T(2,128)(2,1)S(1)} %get-tuple-element.8), channel_id=1, source_target_pairs={{0,32},{32,64},{64,96},{96,0},{1,33},{33,65},{65,97},{97,1},{2,34}... | collective-permute-start | bytes 884744 | tf_op jit(solution)/shard_map/ppermute | solution.py:254
  3.1 14.1 %collective-permute-start.2 = (bf16[16,2,4608]{2,1,0:T(2,128)(2,1)S(1)}, bf16[16,2,4608]{2,1,0:T(2,128)(2,1)S(1)}, u32[]{:S(2)}, u32[]{:S(2)}) collective-permute-start(bf16[16,2,4608]{2,1,0:T(2,128)(2,1)S(1)} %get-tuple-element.9), channel_id=1, source_target_pairs={{0,96},{32,0},{64,32},{96,64},{1,97},{33,1},{65,33},{97,65},{2,98}... | collective-permute-start | bytes 884744 | tf_op jit(solution)/shard_map/ppermute | solution.py:254
  3.8 14.8 %collective-permute-start.1 = (bf16[16,2,4608]{2,1,0:T(2,128)(2,1)S(1)}, bf16[16,2,4608]{2,1,0:T(2,128)(2,1)}, u32[]{:S(2)}, u32[]{:S(2)}) collective-permute-start(bf16[16,2,4608]{2,1,0:T(2,128)(2,1)S(1)} %get-tuple-element.10), channel_id=1, source_target_pairs={{0,64},{32,96},{64,0},{96,32},{1,65},{33,97},{65,1},{97,33},{2,66}... | collective-permute-start | bytes 884744 | tf_op jit(solution)/shard_map/ppermute | solution.py:254
  7.6 20.1 %all-to-all-start = ((f32[32,8,128]{2,1,0:T(8,128)}), f32[32,8,128]{2,1,0:T(8,128)S(1)}, u32[]{:S(2)}, u32[]{:S(2)}) async-start(f32[32,8,128]{2,1,0:T(8,128)} %shard_map.104), calls=%async_computation | async-start | bytes 262144 | tf_op jit(solution)/shard_map/all_to_all | solution.py:267
  17.2 0.7 copy-start.11
  18.0 0.7 copy-start.12
  18.7 17.7 %copy-start = (bf16[1,16,1,256,384]{4,3,2,1,0:T(8,128)(2,1)S(1)}, bf16[1,16,1,256,384]{4,3,2,1,0:T(8,128)(2,1)}, u32[]{:S(2)}) copy-start(bf16[1,16,1,256,384]{4,3,2,1,0:T(8,128)(2,1)} %param.13) | copy-start | bytes 9437188
  23.9 10.8 %slice-start = ((f32[64,576]{1,0:T(8,128)}), f32[64,192]{1,0:T(8,128)S(1)}, s32[]{:S(2)}) async-start(f32[64,576]{1,0:T(8,128)} %reshape.32.hidden_ref), calls=%async_computation.5 | async-start | bytes 131072 | tf_op jit(solution)/shard_map/slice | solution.py:279
  23.9 12.5 %copy-start.1 = (f32[64,576]{1,0:T(8,128)S(1)}, f32[64,576]{1,0:T(8,128)}, u32[]{:S(2)}) copy-start(f32[64,576]{1,0:T(8,128)} %reshape.32.hidden_ref) | copy-start | bytes 442372
  23.9 12.5 %copy-start.2 = (s32[16]{0:T(128)S(1)}, s32[16]{0:T(128)}, u32[]{:S(2)}) copy-start(s32[16]{0:T(128)} %len_ref.1) | copy-start | bytes 196
  27.7 23.6 %all-to-all-start.2 = ((bf16[8,2,16,576]{3,2,1,0:T(8,128)(2,1)}), bf16[8,2,16,576]{3,2,1,0:T(8,128)(2,1)}, u32[]{:S(2)}, u32[]{:S(2)}) async-start(bf16[8,2,16,576]{3,2,1,0:T(8,128)(2,1)} %bitcast.51), calls=%async_computation.2 | async-start | bytes 655360 | tf_op jit(solution)/shard_map/all_to_all | solution.py:296
  41.4 0.7 copy-start.3
  42.0 9.3 %collective-permute-start.5 = (bf16[64,640]{1,0:T(8,128)(2,1)S(1)}, bf16[64,640]{1,0:T(8,128)(2,1)S(1)}, u32[]{:S(2)}, u32[]{:S(2)}) collective-permute-start(bf16[64,640]{1,0:T(8,128)(2,1)S(1)} %get-tuple-element.5), channel_id=1, source_target_pairs={{128,0},{129,1},{130,2},{131,3},{132,4},{133,5},{134,6},{135,7},{1... | collective-permute-start | bytes 245768 | tf_op jit(solution)/shard_map/ppermute | solution.py:283
  52.0 19.2 %all-to-all-start.1 = ((bf16[4,64,640]{2,1,0:T(8,128)(2,1)}), bf16[4,64,640]{2,1,0:T(8,128)(2,1)S(1)}, u32[]{:S(2)}, u32[]{:S(2)}) async-start(bf16[4,64,640]{2,1,0:T(8,128)(2,1)} %broadcast_in_dim.26), calls=%async_computation.1 | async-start | bytes 655360 | tf_op jit(solution)/shard_map/all_to_all | solution.py:300
  59.6 11.6 %collective-permute-start.8 = (bf16[8,2,16,576]{3,2,1,0:T(8,128)(2,1)}, bf16[8,2,16,576]{3,2,1,0:T(8,128)(2,1)S(1)}, u32[]{:S(2)}, u32[]{:S(2)}) collective-permute-start(bf16[8,2,16,576]{3,2,1,0:T(8,128)(2,1)} %all-to-all-done.2.w0_ref), channel_id=1, source_target_pairs={{0,96},{32,0},{64,32},{96,64},{1,97},{33,1},{65,33},{97,65},{2,98}... | collective-permute-start | bytes 884744 | tf_op jit(solution)/shard_map/ppermute | solution.py:298
  60.3 11.0 %collective-permute-start.7 = (bf16[8,2,16,576]{3,2,1,0:T(8,128)(2,1)}, bf16[8,2,16,576]{3,2,1,0:T(8,128)(2,1)S(1)}, u32[]{:S(2)}, u32[]{:S(2)}) collective-permute-start(bf16[8,2,16,576]{3,2,1,0:T(8,128)(2,1)} %all-to-all-done.2.w0_ref), channel_id=1, source_target_pairs={{0,64},{32,96},{64,0},{96,32},{1,65},{33,97},{65,1},{97,33},{2,66}... | collective-permute-start | bytes 884744 | tf_op jit(solution)/shard_map/ppermute | solution.py:298
  60.9 10.3 %collective-permute-start.6 = (bf16[8,2,16,576]{3,2,1,0:T(8,128)(2,1)}, bf16[8,2,16,576]{3,2,1,0:T(8,128)(2,1)S(1)}, u32[]{:S(2)}, u32[]{:S(2)}) collective-permute-start(bf16[8,2,16,576]{3,2,1,0:T(8,128)(2,1)} %all-to-all-done.2.w0_ref), channel_id=1, source_target_pairs={{0,32},{32,64},{64,96},{96,0},{1,33},{33,65},{65,97},{97,1},{2,34}... | collective-permute-start | bytes 884744 | tf_op jit(solution)/shard_map/ppermute | solution.py:298
  71.2 0.7 copy-start.6
  71.2 0.8 copy-start.7
  71.2 1.0 copy-start.8
  71.2 1.1 copy-start.9
  88.5 6.9 %copy-start.4 = (f32[64,576]{1,0:T(8,128)S(1)}, f32[64,576]{1,0:T(8,128)}, u32[]{:S(2)}) copy-start(f32[64,576]{1,0:T(8,128)} %copy-done.3) | copy-start | bytes 442372
  88.5 26.6 %copy-start.10 = (bf16[16,2,4608]{2,1,0:T(2,128)(2,1)S(1)}, bf16[16,2,4608]{2,1,0:T(2,128)(2,1)}, u32[]{:S(2)}) copy-start(bf16[16,2,4608]{2,1,0:T(2,128)(2,1)} %get-tuple-element.6) | copy-start | bytes 884740
  91.0 36.2 %copy-start.5 = (f32[16,2,4608]{2,1,0:T(2,128)S(1)}, f32[16,2,4608]{2,1,0:T(2,128)}, u32[]{:S(2)}) copy-start(f32[16,2,4608]{2,1,0:T(2,128)} %get-tuple-element.7) | copy-start | bytes 1769476
  91.0 25.4 %all-to-all-start.4 = ((bf16[4,64,576]{2,1,0:T(8,128)(2,1)}), bf16[4,64,576]{2,1,0:T(8,128)(2,1)S(1)}, u32[]{:S(2)}, u32[]{:S(2)}) async-start(bf16[4,64,576]{2,1,0:T(8,128)(2,1)} %shard_map.107), calls=%async_computation.4 | async-start | bytes 655360 | tf_op jit(solution)/shard_map/all_to_all | solution.py:322
  95.4 22.5 %collective-permute-start.4 = (f32[64,576]{1,0:T(8,128)S(1)}, f32[64,576]{1,0:T(8,128)S(1)}, u32[]{:S(2)}, u32[]{:S(2)}) collective-permute-start(f32[64,576]{1,0:T(8,128)S(1)} %copy-done.4), channel_id=1, source_target_pairs={{128,0},{129,1},{130,2},{131,3},{132,4},{133,5},{134,6},{135,7},{1... | collective-permute-start | bytes 442376 | tf_op jit(solution)/shard_map/ppermute | solution.py:284
  115.1 12.1 %collective-permute-start.3 = (bf16[16,2,4608]{2,1,0:T(2,128)(2,1)S(1)}, bf16[16,2,4608]{2,1,0:T(2,128)(2,1)S(1)}, u32[]{:S(2)}, u32[]{:S(2)}) collective-permute-start(bf16[16,2,4608]{2,1,0:T(2,128)(2,1)S(1)} %copy-done.10), channel_id=1, source_target_pairs={{0,128},{1,129},{2,130},{3,131},{4,132},{5,133},{6,134},{7,135},{8... | collective-permute-start | bytes 884744 | tf_op jit(solution)/shard_map/ppermute | solution.py:291
  118.0 11.7 %collective-permute-start.9 = (bf16[16,4,576]{2,1,0:T(4,128)(2,1)S(1)}, bf16[16,4,576]{2,1,0:T(4,128)(2,1)S(1)}, u32[]{:S(2)}, u32[]{:S(2)}) collective-permute-start(bf16[16,4,576]{2,1,0:T(4,128)(2,1)S(1)} %reshape.29), channel_id=1, source_target_pairs={{0,128},{1,129},{2,130},{3,131},{4,132},{5,133},{6,134},{7,135},{8... | collective-permute-start | bytes 221192 | tf_op jit(solution)/shard_map/ppermute | solution.py:325

commit v2 on v1

--- a/solution.py
+++ b/solution.py
@@ -47,6 +47,12 @@
     return jnp.sum(jnp.where(here == lane, line, 0.0), axis=1, keepdims=True)
 
 
+def three_terms(values):
+    high = values.astype(jnp.bfloat16).astype(jnp.float32)
+    middle = (values - high).astype(jnp.bfloat16).astype(jnp.float32)
+    return high, middle, values - high - middle
+
+
 def squares_kernel(hidden_ref, out_ref):
     hidden = hidden_ref[...]
     line = to_lanes(jnp.sum(hidden * hidden, axis=1, keepdims=True), 128)
@@ -60,8 +66,6 @@
     hidden_ref,
     squares_ref,
     gain_ref,
-    flip_gain_ref,
-    flip_ref,
     out_gain_ref,
     kv_ref,
     middle_ref,
@@ -87,7 +91,12 @@
                 part = slice(q * HEAD, (q + 1) * HEAD)
                 normed_ref[q] = normed[:, part]
                 hidden_parts_ref[q] = hidden[:, part]
-            flip_normed_ref[...] = flip_ref[...] * factor * flip_gain_ref[...]
+            across = lax.broadcasted_iota(jnp.int32, (HEAD, HEAD), 0)
+            down = lax.broadcasted_iota(jnp.int32, (HEAD, HEAD), 1)
+            reverse = jnp.where(across + down == HEAD - 1, 1.0, 0.0).astype(jnp.bfloat16)
+            flip_normed_ref[...] = jnp.dot(
+                normed_ref[0].astype(jnp.bfloat16), reverse, preferred_element_type=jnp.float32
+            )
 
         high = lax.broadcasted_iota(jnp.int32, (groups * 8, 1), 0) % 8 >= 4
         row_id = lax.broadcasted_iota(jnp.int32, (groups * 8, 8), 0) % 8
@@ -143,50 +152,79 @@
             middle = middle_ref[...]
             width = middle.shape[1]
             squares = jnp.sum(middle * middle, axis=1, keepdims=True)
-            high_part = squares.astype(jnp.bfloat16).astype(jnp.float32)
-            mid_part = (squares - high_part).astype(jnp.bfloat16).astype(jnp.float32)
-            low_part = squares - high_part - mid_part
             lane = lax.broadcasted_iota(jnp.int32, (rows, sent_ref.shape[1] - width), 1)
-            tail = jnp.where(
-                lane == 0,
-                high_part,
-                jnp.where(lane == 1, mid_part, jnp.where(lane == 2, low_part, 0.0)),
-            )
+            tail = jnp.zeros(lane.shape, jnp.float32)
+            for i, term in enumerate(three_terms(squares)):
+                tail = jnp.where(lane == i, term, tail)
             sent_ref[:, :width] = (middle * out_gain_ref[...]).astype(jnp.bfloat16)
             sent_ref[:, width:] = tail.astype(jnp.bfloat16)
 
 
-def up_kernel(place_ref, x_ref, w0_ref, w1_ref, w2_ref, w3_ref, out_ref):
+def adam_kernel(place_ref, grad_ref, g1_ref, g2_ref, g3_ref, w_ref, m1_ref, m2_ref, new_ref, blocks_ref):
+    members, halves, units, width = blocks_ref.shape
+    step = 2 * width
+    for half in range(halves):
+        for i in range(members // 2):
+            cut = slice(i * step, (i + 1) * step)
+            grad_sum = grad_ref[:, half, cut].astype(jnp.float32)
+            for ref in (g1_ref, g2_ref, g3_ref):
+                grad_sum = grad_sum + ref[:, half, cut].astype(jnp.float32)
+            new = adam_update(
+                grad_sum, w_ref[:, half, cut], m1_ref[:, half, cut], m2_ref[:, half, cut]
+            )
+            new_ref[:, half, cut] = new
+            blocks_ref[2 * i, half] = new[:, :width].astype(jnp.bfloat16)
+            blocks_ref[2 * i + 1, half] = new[:, width:].astype(jnp.bfloat16)
+
+
+def up_kernel(place_ref, x0_ref, x1_ref, x2_ref, x3_ref, w0_ref, w1_ref, w2_ref, w3_ref, out_ref):
     copies, height, units = out_ref.shape
-    bands, rows, wide = x_ref.shape
+    bands = 4
+    rows = x0_ref.shape[0]
     width = w0_ref.shape[3]
-    total = jnp.zeros((rows, units), jnp.float32)
-    for k, w_ref in enumerate((w0_ref, w1_ref, w2_ref, w3_ref)):
-        features = x_ref[lax.rem(place_ref[0] + bands - k, bands)][:, :width]
-        weights = w_ref[:, 0].reshape(units, width)
-        total += lax.dot_general(
-            features, weights, (((1,), (1,)), ((), ())), preferred_element_type=jnp.float32
-        )
-    squares = jnp.zeros((rows, 1), jnp.float32)
-    for band in range(bands):
-        squares += jnp.sum(x_ref[band][:, width:].astype(jnp.float32), axis=1, keepdims=True)
-    line = jnp.broadcast_to(to_lanes(squares, units), (height - rows, units))
-    for copy in range(copies):
-        out_ref[copy, :rows] = total
-        out_ref[copy, rows:] = line
+    x_refs = (x0_ref, x1_ref, x2_ref, x3_ref)
+    w_refs = (w0_ref, w1_ref, w2_ref, w3_ref)
+    shift = lax.rem(place_ref[1] - place_ref[0] + bands, bands)
+    for value in range(bands):
+
+        @pl.when(shift == value)
+        def _(value=value):
+            total = jnp.zeros((rows, units), jnp.float32)
+            squares = jnp.zeros((rows, 1), jnp.float32)
+            for k in range(bands):
+                x_ref = x_refs[(k + value) % bands]
+                total += lax.dot_general(
+                    x_ref[:, :width],
+                    w_refs[k][:, 0].reshape(units, width),
+                    (((1,), (1,)), ((), ())),
+                    preferred_element_type=jnp.float32,
+                )
+                squares += jnp.sum(x_ref[:, width:].astype(jnp.float32), axis=1, keepdims=True)
+            line = to_lanes(squares, units)
+            row = lax.broadcasted_iota(jnp.int32, (height - rows, units), 0)
+            tail = jnp.zeros((height - rows, units), jnp.float32)
+            for i, term in enumerate(three_terms(line)):
+                tail = jnp.where(row == i, term, tail)
+            total = total.astype(out_ref.dtype)
+            tail = tail.astype(out_ref.dtype)
+            for copy in range(copies):
+                out_ref[copy, :rows] = total
+                out_ref[copy, rows:] = tail
 
 
 def down_kernel(place_ref, sums_ref, w0_ref, w1_ref, w2_ref, w3_ref, out_ref):
-    bands, rows, width = out_ref.shape
-    total = jnp.sum(sums_ref[...], axis=0)
-    factor = lax.rsqrt(to_rows(total[rows : rows + 1], rows) / D + norm_eps)
+    roles, bands, rows, width = out_ref.shape
+    total = jnp.sum(sums_ref[...].astype(jnp.float32), axis=0)
+    squares = jnp.sum(total[rows : rows + 8], axis=0, keepdims=True)
+    factor = lax.rsqrt(to_rows(squares, rows) / D + norm_eps)
     upper = jnp.maximum(total[:rows] * factor, 0.0)
     active = (upper * upper).astype(jnp.bfloat16)
     for k, w_ref in enumerate((w0_ref, w1_ref, w2_ref, w3_ref)):
         weights = w_ref[:, 1].reshape(active.shape[1], width)
-        out_ref[lax.rem(place_ref[0] + bands - k, bands)] = jnp.dot(
-            active, weights, preferred_element_type=jnp.float32
-        ).astype(jnp.bfloat16)
+        band = lax.rem(place_ref[0] + bands - k, bands)
+        part = jnp.dot(active, weights, preferred_element_type=jnp.float32).astype(jnp.bfloat16)
+        for role in range(roles):
+            out_ref[role, band] = part
 
 
 VMEM = pl.BlockSpec(memory_space=pltpu.VMEM)
@@ -197,7 +235,7 @@
     return pl.BlockSpec(shape, lambda i: (0,) * len(shape))
 
 
-def attend(role, lengths, hidden, squares, gain, flip_gain, flip, out_gain, kv):
+def attend(role, lengths, hidden, squares, gain, out_gain, kv):
     rows, width = hidden.shape
     count = kv.shape[0]
     groups = width // HEAD
@@ -216,8 +254,6 @@
             whole(hidden.shape),
             whole(squares.shape),
             whole(gain.shape),
-            whole(flip_gain.shape),
-            whole(flip.shape),
             whole(out_gain.shape),
             pl.BlockSpec(block, lambda i: (i, 0, 0)),
         ],
@@ -228,7 +264,7 @@
             pltpu.VMEM((rows, HEAD), jnp.float32),
         ],
         compiler_params=pltpu.CompilerParams(vmem_limit_bytes=24 * 1024 * 1024),
-    )(role, lengths, hidden, squares, gain, flip_gain, flip, out_gain, kv)
+    )(role, lengths, hidden, squares, gain, out_gain, kv)
 
 
 def body(grad_parts, master, moment1, moment2, kv_cache, hidden_in, attn_gain, ffn_gain, lengths):
@@ -275,56 +311,76 @@
         hidden,
         squares,
         gain_attn,
-        jnp.flip(gain_attn[:, :HEAD], axis=1),
-        jnp.flip(hidden[:, :HEAD], axis=1),
         gain_ffn,
         kv_cache[0, :, 0],
     )
-    features = lax.ppermute(outgoing, "role", [(1, 0)])
+
+    def to_holders(by):
+        pairs = []
+        for d in range(shards):
+            for b in range(bands):
+                for m in range(BAND):
+                    source = (shards + d) * tensor + b * BAND + m
+                    pairs.append((source, d * tensor + (b + by) % bands * BAND + m))
+        return pairs
+
+    features = [
+        lax.ppermute(outgoing, ("role", "dp", "tensor"), to_holders(k)) for k in range(bands)
+    ]
     middle_home = lax.ppermute(middle, "role", [(1, 0)])
-
-    grad_sum = grad_quarter(place).astype(jnp.float32)
-    for part in arriving:
-        grad_sum = grad_sum + part.astype(jnp.float32)
-    new_master = adam_update(grad_sum, master[0], moment1[0], moment2[0])
-    synced = new_master.astype(bf16)
-    copied = lax.ppermute(synced, "role", [(0, 1)])
-    weights_after = jnp.where(role_index == 0, new_master, copied.astype(jnp.float32))[None]
-
-    units = synced.shape[0]
-    blocks = synced.reshape(units, 2, BAND, width).transpose(2, 1, 0, 3)
+    middle = jnp.where(role_index == 0, middle_home, middle)
+
+    place_operand = jnp.stack([place, lax.axis_index("tensor") // BAND]).astype(jnp.int32)
+    units = master.shape[1]
+    arriving, outgoing = lax.optimization_barrier((arriving, outgoing))
+    flat = pl.BlockSpec((units, 2, quarter), lambda i, place_ref: (0, 0, 0))
+    new_master, blocks = pl.pallas_call(
+        adam_kernel,
+        out_shape=(
+            jax.ShapeDtypeStruct((units, 2, quarter), jnp.float32),
+            jax.ShapeDtypeStruct((BAND, 2, units, width), bf16),
+        ),
+        grid_spec=pltpu.PrefetchScalarGridSpec(
+            num_scalar_prefetch=1,
+            grid=(1,),
+            in_specs=[pl.BlockSpec((units, 2, quarter), lambda i, place_ref: (0, 0, place_ref[0]))]
+            + [flat] * 6,
+            out_specs=(
+                flat,
+                pl.BlockSpec((BAND, 2, units, width), lambda i, place_ref: (0, 0, 0, 0)),
+            ),
+        ),
+        compiler_params=pltpu.CompilerParams(vmem_limit_bytes=24 * 1024 * 1024),
+    )(place_operand, grads, *arriving, master[0], moment1[0], moment2[0])
+    copied = lax.ppermute(new_master, "role", [(0, 1)]).astype(bf16).astype(jnp.float32)
+    weights_after = jnp.where(role_index == 0, new_master, copied)[None]
+
     own = lax.all_to_all(blocks, "tensor", 0, 0, tiled=True, axis_index_groups=band_groups)
     slabs = [own] + [
         lax.ppermute(own, ("role", "dp"), learner_pairs(k)) for k in range(1, shards)
     ]
-    gathered = lax.all_to_all(
-        jnp.broadcast_to(features[None], (bands,) + features.shape),
-        "tensor",
-        0,
-        0,
-        tiled=True,
-        axis_index_groups=member_groups,
-    )
-    place_operand = place.astype(jnp.int32)[None]
     sums = pl.pallas_call(
         up_kernel,
-        out_shape=jax.ShapeDtypeStruct((BAND, rows + 8, BAND * units), jnp.float32),
-        in_specs=[SMEM] + [VMEM] * 5,
+        out_shape=jax.ShapeDtypeStruct((BAND, rows + 16, BAND * units), bf16),
+        in_specs=[SMEM] + [VMEM] * 8,
         out_specs=VMEM,
-    )(place_operand, gathered, *slabs)
+    )(place_operand, *features, *slabs)
     sums = lax.all_to_all(sums, "tensor", 0, 0, tiled=True, axis_index_groups=band_groups)
     parts = pl.pallas_call(
         down_kernel,
-        out_shape=jax.ShapeDtypeStruct((bands, rows, width), bf16),
+        out_shape=jax.ShapeDtypeStruct((2, bands, rows, width), bf16),
         in_specs=[SMEM] + [VMEM] * 5,
         out_specs=VMEM,
     )(place_operand, sums, *slabs)
-    parts = lax.all_to_all(parts, "tensor", 0, 0, tiled=True, axis_index_groups=member_groups)
-    decoded = (middle_home + jnp.sum(parts.astype(jnp.float32), axis=0)).astype(bf16)
-    decoded = decoded.reshape(row_count, steps, width)
-    returned = lax.ppermute(decoded, "role", [(0, 1)])
-    decoded = jnp.where(role_index == 0, decoded, returned)
-    return (weights_after, decoded)
+    parts = parts.reshape(2 * bands, rows, width)
+    home_groups = [
+        [r * tensor + b * BAND + m for r in range(2) for b in range(bands)] for m in range(BAND)
+    ]
+    parts = lax.all_to_all(
+        parts, ("role", "tensor"), 0, 0, tiled=True, axis_index_groups=home_groups
+    )
+    decoded = (middle + jnp.sum(parts[:bands].astype(jnp.float32), axis=0)).astype(bf16)
+    return (weights_after, decoded.reshape(row_count, steps, width))
 
 
 def solution(mesh):

time: 132 us -> 139 us (1.053)
  the two profiles are of different devices: /device:TPU:38 before, /device:TPU:32 now
where the time goes in v2:
time: 139 us; the launch traced here: 138 us
  starting transfers between devices  51.1 us (37%)
  waiting for transfers between devices  49.9 us (36%)
  blocking collectives  13.2 us (9%)
  local copies, waits for them, and re-layouts  10.8 us (8%)
  Pallas kernels  10.2 us (7%)
  other arithmetic  1.47 us (1%)
    all_to_all x1, waiting for transfers between devices, body(): lax.all_to_all(parts, ('role', 'tensor'), 0, 0, tiled=True, axis_index_gr...  21.3 us
    ppermute x4, waiting for transfers between devices, body(): lax.ppermute(outgoing, ('role', 'dp', 'tensor'), to_holders(k))  16 us
    all_to_all x1, blocking collectives, body(): lax.all_to_all(blocks, 'tensor', 0, 0, tiled=True, axis_index_groups=band...  13.2 us
    ppermute x3, starting transfers between devices, body(): lax.ppermute(grad_quarter((place + k) % shards), ('role', 'dp'), learner_...  11.6 us
    all_to_all x1, starting transfers between devices, body(): squares = lax.all_to_all(squares, 'tensor', 0, 0, tiled=True)  9.65 us
    ppermute x3, starting transfers between devices, body(): lax.ppermute(own, ('role', 'dp'), learner_pairs(k))  9.08 us
    all_to_all x1, waiting for transfers between devices, body(): squares = lax.all_to_all(squares, 'tensor', 0, 0, tiled=True)  7.68 us
    ppermute x1, starting transfers between devices, body(): lax.ppermute(new_master, 'role', [(0, 1)]).astype(bf16).astype(jnp.float32)  6.43 us
  transfers between devices with their start and end apart: 15, of which 6 were waited for; matrix products, arithmetic and copies ran while one was open for 3% of the time, Pallas kernels for 5%

profile of v2, /device:TPU:32, one launch (start us, length us, event | category | flops | bytes accessed | tf_op | source)
XLA Modules:
  0.0 137.7 jit_solution(3227528447560608017)
XLA Ops:
  0.6 0.0 copy-start.13
  0.7 0.0 copy-start.7
  0.7 1.8 %dynamic-slice_bitcast_fusion = (bf16[16,2,4608]{2,1,0:T(2,128)(2,1)S(1)}, bf16[16,2,4608]{2,1,0:T(2,128)(2,1)S(1)}, bf16[16,2,4608]{2,1,0:T(2,128)(2,1)S(1)}) fusion(bf16[1,1,16,2,18432]{4,3,2,1,0:T(2,128)(2,1)} %param.9, s32[]{:T(128)S(6)} %select_n.55, s32[]{:T(128)S(6)} %select_n.51, s32[]{:T(128)S(6)} %select_n.53), kind=kLoop, calls=%fused_computation.2 | loop fusion | bytes 1769484 | tf_op jit(solution)/shard_map/dynamic_slice | solution.py:287
  2.5 3.5 %collective-permute-start = (bf16[16,2,4608]{2,1,0:T(2,128)(2,1)S(1)}, bf16[16,2,4608]{2,1,0:T(2,128)(2,1)S(1)}, u32[]{:S(2)}, u32[]{:S(2)}) collective-permute-start(bf16[16,2,4608]{2,1,0:T(2,128)(2,1)S(1)} %get-tuple-element.17), channel_id=1, source_target_pairs={{0,32},{32,64},{64,96},{96,0},{1,33},{33,65},{65,97},{97,1},{2,34}... | collective-permute-start | bytes 884744 | tf_op jit(solution)/shard_map/ppermute | solution.py:290
  6.0 4.8 %collective-permute-start.1 = (bf16[16,2,4608]{2,1,0:T(2,128)(2,1)S(1)}, bf16[16,2,4608]{2,1,0:T(2,128)(2,1)S(1)}, u32[]{:S(2)}, u32[]{:S(2)}) collective-permute-start(bf16[16,2,4608]{2,1,0:T(2,128)(2,1)S(1)} %get-tuple-element.18), channel_id=1, source_target_pairs={{0,64},{32,96},{64,0},{96,32},{1,65},{33,97},{65,1},{97,33},{2,66}... | collective-permute-start | bytes 884744 | tf_op jit(solution)/shard_map/ppermute | solution.py:290
  10.8 3.3 %collective-permute-start.2 = (bf16[16,2,4608]{2,1,0:T(2,128)(2,1)S(1)}, bf16[16,2,4608]{2,1,0:T(2,128)(2,1)S(1)}, u32[]{:S(2)}, u32[]{:S(2)}) collective-permute-start(bf16[16,2,4608]{2,1,0:T(2,128)(2,1)S(1)} %get-tuple-element.16), channel_id=1, source_target_pairs={{0,96},{32,0},{64,32},{96,64},{1,97},{33,1},{65,33},{97,65},{2,98}... | collective-permute-start | bytes 884744 | tf_op jit(solution)/shard_map/ppermute | solution.py:290
  14.0 0.0 copy-done.13
  14.0 0.7 reshape.23.hidden_ref
  14.7 1.7 %shard_map.104 = f32[32,8,128]{2,1,0:T(8,128)} custom-call(f32[64,576]{1,0:T(8,128)} %reshape.23.hidden_ref), custom_call_target="tpu_custom_call" | custom-call | tf_op jit(solution)/shard_map/pallas_call | solution.py:297
  16.4 9.7 %all-to-all-start = ((f32[32,8,128]{2,1,0:T(8,128)}), f32[32,8,128]{2,1,0:T(8,128)S(1)}, u32[]{:S(2)}, u32[]{:S(2)}) async-start(f32[32,8,128]{2,1,0:T(8,128)} %shard_map.104), calls=%async_computation | async-start | bytes 262144 | tf_op jit(solution)/shard_map/all_to_all | solution.py:303
  26.1 0.8 dynamic_slice.27
  26.9 0.8 dynamic_slice.28
  27.6 0.1 pad_add_fusion.place_ref
  27.7 7.7 %all-to-all-done.squares_ref = f32[32,8,128]{2,1,0:T(8,128)S(1)} async-done(((f32[32,8,128]{2,1,0:T(8,128)}), f32[32,8,128]{2,1,0:T(8,128)S(1)}, u32[]{:S(2)}, u32[]{:S(2)}) %all-to-all-start) | async-done | bytes 131104 | tf_op jit(solution)/shard_map/all_to_all | solution.py:303
  35.4 0.0 copy-done.7
  35.4 1.9 %copy-done.1 = bf16[1,16,1,256,384]{4,3,2,1,0:T(8,128)(2,1)S(1)} copy-done((bf16[1,16,1,256,384]{4,3,2,1,0:T(8,128)(2,1)S(1)}, bf16[1,16,1,256,384]{4,3,2,1,0:T(8,128)(2,1)}, u32[]{:S(2)}) %copy-start.1) | copy-done | bytes 3145752
  37.3 0.9 copy-done.2
  38.2 0.7 shard_map.105
  38.9 0.0 collective-permute-done.g1_ref
  38.9 0.0 collective-permute-done.1.g2_ref
  38.9 0.0 collective-permute-done.2.g3_ref
  38.9 0.0 copy-done.6
  38.9 0.5 copy-done
  39.5 0.1 copy-done.3
  39.6 0.2 copy-done.4
  39.8 0.2 copy-done.5
  40.0 2.9 %shard_map.106 = (f32[16,2,4608]{2,1,0:T(2,128)S(1)}, bf16[8,2,16,576]{3,2,1,0:T(8,128)(2,1)S(1)}) custom-call(s32[2]{0:T(128)S(1)} %pad_add_fusion.place_ref, bf16[16,2,18432]{2,1,0:T(2,128)(2,1)S(1)} %bitcast.17, bf16[16,2,4608]{2,1,0:T(2,128)(2,1)S(1)} %collective-permute-done.g1_ref, bf16[16,2,4608]{2,1,0:T(2,128)(2,1)S(1)} %collective-permute-done.1.g2_ref, ...), custom_call_target="tpu_custom_call" | custom-call | tf_op jit(solution)/shard_map/pallas_call | solution.py:337
  42.9 13.2 %all_to_all.20.w0_ref = bf16[8,2,16,576]{3,2,1,0:T(8,128)(2,1)S(1)} all-to-all(bf16[8,2,16,576]{3,2,1,0:T(8,128)(2,1)S(1)} %get-tuple-element.15), channel_id=1, replica_groups={{0,1,2,3,4,5,6,7},{8,9,10,11,12,13,14,15},{16,17,18,19,20,21,22,23},{24..., dimensions={0} | all-to-all | bytes 589824 | tf_op jit(solution)/shard_map/all_to_all | solution.py:358
  56.1 2.6 %collective-permute-start.9 = (bf16[8,2,16,576]{3,2,1,0:T(8,128)(2,1)S(1)}, bf16[8,2,16,576]{3,2,1,0:T(8,128)(2,1)S(1)}, u32[]{:S(2)}, u32[]{:S(2)}) collective-permute-start(bf16[8,2,16,576]{3,2,1,0:T(8,128)(2,1)S(1)} %all_to_all.20.w0_ref), channel_id=1, source_target_pairs={{0,32},{32,64},{64,96},{96,0},{1,33},{33,65},{65,97},{97,1},{2,34}... | collective-permute-start | bytes 884744 | tf_op jit(solution)/shard_map/ppermute | solution.py:360
  58.7 2.7 %collective-permute-start.10 = (bf16[8,2,16,576]{3,2,1,0:T(8,128)(2,1)S(1)}, bf16[8,2,16,576]{3,2,1,0:T(8,128)(2,1)S(1)}, u32[]{:S(2)}, u32[]{:S(2)}) collective-permute-start(bf16[8,2,16,576]{3,2,1,0:T(8,128)(2,1)S(1)} %all_to_all.20.w0_ref), channel_id=1, source_target_pairs={{0,64},{32,96},{64,0},{96,32},{1,65},{33,97},{65,1},{97,33},{2,66}... | collective-permute-start | bytes 884744 | tf_op jit(solution)/shard_map/ppermute | solution.py:360
  61.4 3.8 %collective-permute-start.11 = (bf16[8,2,16,576]{3,2,1,0:T(8,128)(2,1)S(1)}, bf16[8,2,16,576]{3,2,1,0:T(8,128)(2,1)S(1)}, u32[]{:S(2)}, u32[]{:S(2)}) collective-permute-start(bf16[8,2,16,576]{3,2,1,0:T(8,128)(2,1)S(1)} %all_to_all.20.w0_ref), channel_id=1, source_target_pairs={{0,96},{32,0},{64,32},{96,64},{1,97},{33,1},{65,33},{97,65},{2,98}... | collective-permute-start | bytes 884744 | tf_op jit(solution)/shard_map/ppermute | solution.py:360
  65.2 1.3 collective-permute-start.5
  66.5 1.3 collective-permute-start.6
  67.8 5.2 %collective-permute-done.5.x0_ref = bf16[64,640]{1,0:T(8,128)(2,1)S(1)} collective-permute-done((bf16[64,640]{1,0:T(8,128)(2,1)S(1)}, bf16[64,640]{1,0:T(8,128)(2,1)S(1)}, u32[]{:S(2)}, u32[]{:S(2)}) %collective-permute-start.5) | collective-permute-done | bytes 81952 | tf_op jit(solution)/shard_map/ppermute | solution.py:328
  73.1 1.3 collective-permute-start.7
  74.4 5.8 %collective-permute-done.6.x1_ref = bf16[64,640]{1,0:T(8,128)(2,1)S(1)} collective-permute-done((bf16[64,640]{1,0:T(8,128)(2,1)S(1)}, bf16[64,640]{1,0:T(8,128)(2,1)S(1)}, u32[]{:S(2)}, u32[]{:S(2)}) %collective-permute-start.6) | collective-permute-done | bytes 81952 | tf_op jit(solution)/shard_map/ppermute | solution.py:328
  80.2 1.3 collective-permute-start.8
  81.5 0.2 convert.1
  81.7 0.0 collective-permute-done.7.x2_ref
  81.7 0.0 copy-start.16
  81.7 6.4 %collective-permute-start.3 = (bf16[16,2,4608]{2,1,0:T(2,128)(2,1)S(1)}, bf16[16,2,4608]{2,1,0:T(2,128)(2,1)S(1)}, u32[]{:S(2)}, u32[]{:S(2)}) collective-permute-start(bf16[16,2,4608]{2,1,0:T(2,128)(2,1)S(1)} %convert.1), channel_id=1, source_target_pairs={{0,128},{1,129},{2,130},{3,131},{4,132},{5,133},{6,134},{7,135},{8... | collective-permute-start | bytes 884744 | tf_op jit(solution)/shard_map/ppermute | solution.py:355
  88.1 4.9 %collective-permute-done.8.x3_ref = bf16[64,640]{1,0:T(8,128)(2,1)S(1)} collective-permute-done((bf16[64,640]{1,0:T(8,128)(2,1)S(1)}, bf16[64,640]{1,0:T(8,128)(2,1)S(1)}, u32[]{:S(2)}, u32[]{:S(2)}) %collective-permute-start.8) | collective-permute-done | bytes 81952 | tf_op jit(solution)/shard_map/ppermute | solution.py:328
  93.1 0.0 collective-permute-done.9.w1_ref
  93.1 0.0 collective-permute-done.10.w2_ref
  93.1 0.0 copy-start.10
  93.1 0.0 collective-permute-done.11.w3_ref
  93.1 0.0 copy-done.8
  93.1 0.0 copy-done.14
  93.1 0.6 copy-done.17
  93.7 0.1 copy-done.9
  93.8 0.1 copy-done.10
  94.0 0.7 copy-done.11
  94.7 2.5 %shard_map.107 = bf16[8,80,128]{2,1,0:T(8,128)(2,1)} custom-call(s32[2]{0:T(128)} %copy-done.6, bf16[64,640]{1,0:T(8,128)(2,1)} %copy-done.14, bf16[64,640]{1,0:T(8,128)(2,1)} %copy-done.15, bf16[64,640]{1,0:T(8,128)(2,1)} %copy-done.16, bf16[64,640]{1,0:T(8,128)(2,1)} %copy-done.17, bf16[8,2,16,576]{3,2,1,0:T(8,128)(2,1)} %copy-done.8, ...), custom_call_target="tpu_custom_call" | custom-call | tf_op jit(solution)/shard_map/pallas_call | solution.py:362
  97.2 4.4 %all-to-all-start.2 = ((bf16[8,80,128]{2,1,0:T(8,128)(2,1)}), bf16[8,80,128]{2,1,0:T(8,128)(2,1)S(1)}, u32[]{:S(2)}, u32[]{:S(2)}) async-start(bf16[8,80,128]{2,1,0:T(8,128)(2,1)} %shard_map.107), calls=%async_computation.2 | async-start | bytes 327680 | tf_op jit(solution)/shard_map/all_to_all | solution.py:368
  101.6 1.3 collective-permute-start.4
  102.9 4.9 %all-to-all-done.2.sums_ref = bf16[8,80,128]{2,1,0:T(8,128)(2,1)S(1)} async-done(((bf16[8,80,128]{2,1,0:T(8,128)(2,1)}), bf16[8,80,128]{2,1,0:T(8,128)(2,1)S(1)}, u32[]{:S(2)}, u32[]{:S(2)}) %all-to-all-start.2) | async-done | bytes 163872 | tf_op jit(solution)/shard_map/all_to_all | solution.py:368
  107.8 0.7 copy-done.12
  108.5 2.5 %shard_map.108 = bf16[2,4,64,576]{3,2,1,0:T(8,128)(2,1)} custom-call(s32[2]{0:T(128)} %copy-done.6, bf16[8,80,128]{2,1,0:T(8,128)(2,1)} %copy-done.12, bf16[8,2,16,576]{3,2,1,0:T(8,128)(2,1)} %copy-done.8, bf16[8,2,16,576]{3,2,1,0:T(8,128)(2,1)} %copy-done.9, bf16[8,2,16,576]{3,2,1,0:T(8,128)(2,1)} %copy-done.10, bf16[8,2,16,576]{3,2,1,0:T(8,128)(2,1)} %copy-done.11), custom_call_target="tpu_custom_call" | custom-call | tf_op jit(solution)/shard_map/pallas_call | solution.py:369
  111.0 3.5 %all-to-all-start.3 = ((bf16[8,64,576]{2,1,0:T(8,128)(2,1)}), bf16[8,64,576]{2,1,0:T(8,128)(2,1)S(1)}, u32[]{:S(2)}, u32[]{:S(2)}) async-start(bf16[8,64,576]{2,1,0:T(8,128)(2,1)} %bitcast.22), calls=%async_computation.3 | async-start | bytes 1310720 | tf_op jit(solution)/shard_map/all_to_all | solution.py:379
  114.6 0.0 collective-permute-done.3
  114.6 1.1 select_bitcast_fusion
  115.7 21.3 %all-to-all-done.3 = bf16[8,64,576]{2,1,0:T(8,128)(2,1)S(1)} async-done(((bf16[8,64,576]{2,1,0:T(8,128)(2,1)}), bf16[8,64,576]{2,1,0:T(8,128)(2,1)S(1)}, u32[]{:S(2)}, u32[]{:S(2)}) %all-to-all-start.3) | async-done | bytes 589856 | tf_op jit(solution)/shard_map/all_to_all | solution.py:379
  137.0 0.0 collective-permute-done.4
  137.1 0.7 reshape.21
  (20 shorter events, 0.1 us)
Async XLA Ops:
  0.6 13.4 %copy-start.13 = (bf16[16,4,576]{2,1,0:T(4,128)(2,1)S(1)}, bf16[16,4,576]{2,1,0:T(4,128)(2,1)}, u32[]{:S(2)}) copy-start(bf16[16,4,576]{2,1,0:T(4,128)(2,1)} %param.14) | copy-start | bytes 221188
  0.7 34.7 %copy-start.7 = (s32[16]{0:T(128)S(1)}, s32[16]{0:T(128)}, u32[]{:S(2)}) copy-start(s32[16]{0:T(128)} %len_ref.1) | copy-start | bytes 196
  2.5 36.4 %collective-permute-start = (bf16[16,2,4608]{2,1,0:T(2,128)(2,1)S(1)}, bf16[16,2,4608]{2,1,0:T(2,128)(2,1)S(1)}, u32[]{:S(2)}, u32[]{:S(2)}) collective-permute-start(bf16[16,2,4608]{2,1,0:T(2,128)(2,1)S(1)} %get-tuple-element.17), channel_id=1, source_target_pairs={{0,32},{32,64},{64,96},{96,0},{1,33},{33,65},{65,97},{97,1},{2,34}... | collective-permute-start | bytes 884744 | tf_op jit(solution)/shard_map/ppermute | solution.py:290
  6.0 33.0 %collective-permute-start.1 = (bf16[16,2,4608]{2,1,0:T(2,128)(2,1)S(1)}, bf16[16,2,4608]{2,1,0:T(2,128)(2,1)S(1)}, u32[]{:S(2)}, u32[]{:S(2)}) collective-permute-start(bf16[16,2,4608]{2,1,0:T(2,128)(2,1)S(1)} %get-tuple-element.18), channel_id=1, source_target_pairs={{0,64},{32,96},{64,0},{96,32},{1,65},{33,97},{65,1},{97,33},{2,66}... | collective-permute-start | bytes 884744 | tf_op jit(solution)/shard_map/ppermute | solution.py:290
  10.8 28.2 %collective-permute-start.2 = (bf16[16,2,4608]{2,1,0:T(2,128)(2,1)S(1)}, bf16[16,2,4608]{2,1,0:T(2,128)(2,1)S(1)}, u32[]{:S(2)}, u32[]{:S(2)}) collective-permute-start(bf16[16,2,4608]{2,1,0:T(2,128)(2,1)S(1)} %get-tuple-element.16), channel_id=1, source_target_pairs={{0,96},{32,0},{64,32},{96,64},{1,97},{33,1},{65,33},{97,65},{2,98}... | collective-permute-start | bytes 884744 | tf_op jit(solution)/shard_map/ppermute | solution.py:290
  16.4 19.0 %all-to-all-start = ((f32[32,8,128]{2,1,0:T(8,128)}), f32[32,8,128]{2,1,0:T(8,128)S(1)}, u32[]{:S(2)}, u32[]{:S(2)}) async-start(f32[32,8,128]{2,1,0:T(8,128)} %shard_map.104), calls=%async_computation | async-start | bytes 262144 | tf_op jit(solution)/shard_map/all_to_all | solution.py:303
  27.7 11.2 %copy-start.6 = (s32[2]{0:T(128)}, s32[2]{0:T(128)S(1)}, u32[]{:S(2)}) copy-start(s32[2]{0:T(128)S(1)} %pad_add_fusion.place_ref) | copy-start | bytes 28
  35.4 1.9 %copy-start.1 = (bf16[1,16,1,256,384]{4,3,2,1,0:T(8,128)(2,1)S(1)}, bf16[1,16,1,256,384]{4,3,2,1,0:T(8,128)(2,1)}, u32[]{:S(2)}) copy-start(bf16[1,16,1,256,384]{4,3,2,1,0:T(8,128)(2,1)} %param.13) | copy-start | bytes 9437188
  37.3 0.9 copy-start.2
  38.2 1.3 copy-start
  38.2 1.4 %copy-start.3 = (f32[1,16,2,4608]{3,2,1,0:T(2,128)S(1)}, f32[1,16,2,4608]{3,2,1,0:T(2,128)}, u32[]{:S(2)}) copy-start(f32[1,16,2,4608]{3,2,1,0:T(2,128)} %param.10) | copy-start | bytes 1769476
  38.2 1.6 %copy-start.4 = (f32[1,16,2,4608]{3,2,1,0:T(2,128)S(1)}, f32[1,16,2,4608]{3,2,1,0:T(2,128)}, u32[]{:S(2)}) copy-start(f32[1,16,2,4608]{3,2,1,0:T(2,128)} %param.11) | copy-start | bytes 1769476
  38.2 1.8 %copy-start.5 = (f32[1,16,2,4608]{3,2,1,0:T(2,128)S(1)}, f32[1,16,2,4608]{3,2,1,0:T(2,128)}, u32[]{:S(2)}) copy-start(f32[1,16,2,4608]{3,2,1,0:T(2,128)} %param.12) | copy-start | bytes 1769476
  56.1 37.0 %copy-start.8 = (bf16[8,2,16,576]{3,2,1,0:T(8,128)(2,1)}, bf16[8,2,16,576]{3,2,1,0:T(8,128)(2,1)S(1)}, u32[]{:S(2)}) copy-start(bf16[8,2,16,576]{3,2,1,0:T(8,128)(2,1)S(1)} %all_to_all.20.w0_ref) | copy-start | bytes 884740
  56.1 36.9 %collective-permute-start.9 = (bf16[8,2,16,576]{3,2,1,0:T(8,128)(2,1)S(1)}, bf16[8,2,16,576]{3,2,1,0:T(8,128)(2,1)S(1)}, u32[]{:S(2)}, u32[]{:S(2)}) collective-permute-start(bf16[8,2,16,576]{3,2,1,0:T(8,128)(2,1)S(1)} %all_to_all.20.w0_ref), channel_id=1, source_target_pairs={{0,32},{32,64},{64,96},{96,0},{1,33},{33,65},{65,97},{97,1},{2,34}... | collective-permute-start | bytes 884744 | tf_op jit(solution)/shard_map/ppermute | solution.py:360
  58.7 34.4 %collective-permute-start.10 = (bf16[8,2,16,576]{3,2,1,0:T(8,128)(2,1)S(1)}, bf16[8,2,16,576]{3,2,1,0:T(8,128)(2,1)S(1)}, u32[]{:S(2)}, u32[]{:S(2)}) collective-permute-start(bf16[8,2,16,576]{3,2,1,0:T(8,128)(2,1)S(1)} %all_to_all.20.w0_ref), channel_id=1, source_target_pairs={{0,64},{32,96},{64,0},{96,32},{1,65},{33,97},{65,1},{97,33},{2,66}... | collective-permute-start | bytes 884744 | tf_op jit(solution)/shard_map/ppermute | solution.py:360
  61.4 31.7 %collective-permute-start.11 = (bf16[8,2,16,576]{3,2,1,0:T(8,128)(2,1)S(1)}, bf16[8,2,16,576]{3,2,1,0:T(8,128)(2,1)S(1)}, u32[]{:S(2)}, u32[]{:S(2)}) collective-permute-start(bf16[8,2,16,576]{3,2,1,0:T(8,128)(2,1)S(1)} %all_to_all.20.w0_ref), channel_id=1, source_target_pairs={{0,96},{32,0},{64,32},{96,64},{1,97},{33,1},{65,33},{97,65},{2,98}... | collective-permute-start | bytes 884744 | tf_op jit(solution)/shard_map/ppermute | solution.py:360
  65.2 7.8 %collective-permute-start.5 = (bf16[64,640]{1,0:T(8,128)(2,1)S(1)}, bf16[64,640]{1,0:T(8,128)(2,1)S(1)}, u32[]{:S(2)}, u32[]{:S(2)}) collective-permute-start(bf16[64,640]{1,0:T(8,128)(2,1)S(1)} %get-tuple-element.9), channel_id=1, source_target_pairs={{128,0},{129,1},{130,2},{131,3},{132,4},{133,5},{134,6},{135,7},{1... | collective-permute-start | bytes 245768 | tf_op jit(solution)/shard_map/ppermute | solution.py:328
  66.5 13.6 %collective-permute-start.6 = (bf16[64,640]{1,0:T(8,128)(2,1)S(1)}, bf16[64,640]{1,0:T(8,128)(2,1)S(1)}, u32[]{:S(2)}, u32[]{:S(2)}) collective-permute-start(bf16[64,640]{1,0:T(8,128)(2,1)S(1)} %get-tuple-element.9), channel_id=1, source_target_pairs={{128,8},{129,9},{130,10},{131,11},{132,12},{133,13},{134,14},{135,... | collective-permute-start | bytes 245768 | tf_op jit(solution)/shard_map/ppermute | solution.py:328
  73.1 20.0 %copy-start.14 = (bf16[64,640]{1,0:T(8,128)(2,1)}, bf16[64,640]{1,0:T(8,128)(2,1)S(1)}, u32[]{:S(2)}) copy-start(bf16[64,640]{1,0:T(8,128)(2,1)S(1)} %collective-permute-done.5.x0_ref) | copy-start | bytes 245764
  73.1 8.6 %collective-permute-start.7 = (bf16[64,640]{1,0:T(8,128)(2,1)S(1)}, bf16[64,640]{1,0:T(8,128)(2,1)S(1)}, u32[]{:S(2)}, u32[]{:S(2)}) collective-permute-start(bf16[64,640]{1,0:T(8,128)(2,1)S(1)} %get-tuple-element.9), channel_id=1, source_target_pairs={{128,16},{129,17},{130,18},{131,19},{132,20},{133,21},{134,22},{13... | collective-permute-start | bytes 245768 | tf_op jit(solution)/shard_map/ppermute | solution.py:328
  80.2 12.9 %copy-start.15 = (bf16[64,640]{1,0:T(8,128)(2,1)}, bf16[64,640]{1,0:T(8,128)(2,1)S(1)}, u32[]{:S(2)}) copy-start(bf16[64,640]{1,0:T(8,128)(2,1)S(1)} %collective-permute-done.6.x1_ref) | copy-start | bytes 245764
  80.2 12.9 %collective-permute-start.8 = (bf16[64,640]{1,0:T(8,128)(2,1)S(1)}, bf16[64,640]{1,0:T(8,128)(2,1)S(1)}, u32[]{:S(2)}, u32[]{:S(2)}) collective-permute-start(bf16[64,640]{1,0:T(8,128)(2,1)S(1)} %get-tuple-element.9), channel_id=1, source_target_pairs={{128,24},{129,25},{130,26},{131,27},{132,28},{133,29},{134,30},{13... | collective-permute-start | bytes 245768 | tf_op jit(solution)/shard_map/ppermute | solution.py:328
  81.7 11.4 %copy-start.16 = (bf16[64,640]{1,0:T(8,128)(2,1)}, bf16[64,640]{1,0:T(8,128)(2,1)S(1)}, u32[]{:S(2)}) copy-start(bf16[64,640]{1,0:T(8,128)(2,1)S(1)} %collective-permute-done.7.x2_ref) | copy-start | bytes 245764
  81.7 32.9 %collective-permute-start.3 = (bf16[16,2,4608]{2,1,0:T(2,128)(2,1)S(1)}, bf16[16,2,4608]{2,1,0:T(2,128)(2,1)S(1)}, u32[]{:S(2)}, u32[]{:S(2)}) collective-permute-start(bf16[16,2,4608]{2,1,0:T(2,128)(2,1)S(1)} %convert.1), channel_id=1, source_target_pairs={{0,128},{1,129},{2,130},{3,131},{4,132},{5,133},{6,134},{7,135},{8... | collective-permute-start | bytes 884744 | tf_op jit(solution)/shard_map/ppermute | solution.py:355
  93.1 0.6 copy-start.17
  93.1 0.8 copy-start.9
  93.1 0.9 copy-start.10
  94.0 0.7 copy-start.11
  97.2 10.6 %all-to-all-start.2 = ((bf16[8,80,128]{2,1,0:T(8,128)(2,1)}), bf16[8,80,128]{2,1,0:T(8,128)(2,1)S(1)}, u32[]{:S(2)}, u32[]{:S(2)}) async-start(bf16[8,80,128]{2,1,0:T(8,128)(2,1)} %shard_map.107), calls=%async_computation.2 | async-start | bytes 327680 | tf_op jit(solution)/shard_map/all_to_all | solution.py:368
  101.6 35.4 %collective-permute-start.4 = (f32[64,576]{1,0:T(8,128)S(1)}, f32[64,576]{1,0:T(8,128)S(1)}, u32[]{:S(2)}, u32[]{:S(2)}) collective-permute-start(f32[64,576]{1,0:T(8,128)S(1)} %get-tuple-element.14), channel_id=1, source_target_pairs={{128,0},{129,1},{130,2},{131,3},{132,4},{133,5},{134,6},{135,7},{1... | collective-permute-start | bytes 442376 | tf_op jit(solution)/shard_map/ppermute | solution.py:330
  107.8 0.7 copy-start.12
  111.0 25.9 %all-to-all-start.3 = ((bf16[8,64,576]{2,1,0:T(8,128)(2,1)}), bf16[8,64,576]{2,1,0:T(8,128)(2,1)S(1)}, u32[]{:S(2)}, u32[]{:S(2)}) async-start(bf16[8,64,576]{2,1,0:T(8,128)(2,1)} %bitcast.22), calls=%async_computation.3 | async-start | bytes 1310720 | tf_op jit(solution)/shard_map/all_to_all | solution.py:379

commit v3 on v2

v3 whole, which is shorter than its diff:
```python
import functools
import math

import jax
import jax.numpy as jnp
from jax import lax
from jax.experimental import pallas as pl
from jax.experimental.pallas import tpu as pltpu
from jax.sharding import PartitionSpec as P

D = 18432
HEAD = 192
STEPS = 4
BAND = 8


beta_one = 0.9
beta_two = 0.95
rate_factor = 0.5
decay_rate = 0.1
adam_eps = 1e-08
norm_eps = 1e-05
step_count = 10


def adam_update(grad_sum, weights, first, second):
    learn_rate = rate_factor / math.sqrt(D)
    first_new = beta_one * first + (1.0 - beta_one) * grad_sum
    second_new = beta_two * second + (1.0 - beta_two) * grad_sum * grad_sum
    corr_one = 1.0 - beta_one**step_count
    corr_two = 1.0 - beta_two**step_count
    ratio = first_new / corr_one / (jnp.sqrt(second_new / corr_two) + adam_eps)
    return weights - learn_rate * (ratio + decay_rate * weights)


def to_lanes(column, lanes):
    rows = column.shape[0]
    here = lax.broadcasted_iota(jnp.int32, (rows, lanes), 0)
    lane = lax.broadcasted_iota(jnp.int32, (rows, lanes), 1)
    return jnp.sum(jnp.where(here == lane, column, 0.0), axis=0, keepdims=True)


def to_rows(line, rows):
    lanes = line.shape[1]
    here = lax.broadcasted_iota(jnp.int32, (rows, lanes), 0)
    lane = lax.broadcasted_iota(jnp.int32, (rows, lanes), 1)
    return jnp.sum(jnp.where(here == lane, line, 0.0), axis=1, keepdims=True)


def three_terms(values):
    high = values.astype(jnp.bfloat16).astype(jnp.float32)
    middle = (values - high).astype(jnp.bfloat16).astype(jnp.float32)
    return high, middle, values - high - middle


def squares_kernel(hidden_ref, out_ref):
    hidden = hidden_ref[...]
    line = to_lanes(jnp.sum(hidden * hidden, axis=1, keepdims=True), 128)
    out_ref[...] = jnp.broadcast_to(line[None], out_ref.shape)


def attend_kernel(
    pairs,
    len_ref,
    hidden_ref,
    squares_ref,
    gain_ref,
    out_gain_ref,
    kv_ref,
    middle_ref,
    sent_ref,
    normed_ref,
    hidden_parts_ref,
    flip_normed_ref,
):
    step = pl.program_id(0)
    groups = normed_ref.shape[0]
    rows = hidden_ref.shape[0]
    scale = 1.0 / math.sqrt(HEAD)

    @pl.when(step == 0)
    def _():
        total = jnp.sum(squares_ref[...], axis=0)[0:1]
        factor = lax.rsqrt(to_rows(total, rows) / D + norm_eps)
        hidden = hidden_ref[...]
        normed = hidden * factor * gain_ref[...]
        for q in range(groups):
            part = slice(q * HEAD, (q + 1) * HEAD)
            normed_ref[q] = normed[:, part]
            hidden_parts_ref[q] = hidden[:, part]
        across = lax.broadcasted_iota(jnp.int32, (HEAD, HEAD), 0)
        down = lax.broadcasted_iota(jnp.int32, (HEAD, HEAD), 1)
        reverse = jnp.where(across + down == HEAD - 1, 1.0, 0.0).astype(jnp.bfloat16)
        flip_normed_ref[...] = jnp.dot(
            normed_ref[0].astype(jnp.bfloat16), reverse, preferred_element_type=jnp.float32
        )

    high = lax.broadcasted_iota(jnp.int32, (groups * 8, 1), 0) % 8 >= 4
    row_id = lax.broadcasted_iota(jnp.int32, (groups * 8, 8), 0) % 8
    col_id = lax.broadcasted_iota(jnp.int32, (groups * 8, 8), 1)
    fresh_ok = (row_id // 4 == col_id // 4) & (col_id % 4 <= row_id % 4)
    context = kv_ref.shape[1]
    position = lax.broadcasted_iota(jnp.int32, (groups * 8, context), 1)
    for p in range(pairs):
        pair = step * pairs + p
        first = pl.multiple_of(pair * 8, 8)
        query = jnp.concatenate(
            [normed_ref[q, pl.ds(first, 8), :] for q in range(groups)], axis=0
        ).astype(jnp.bfloat16)
        new_keys = flip_normed_ref[pl.ds(first, 8), :].astype(jnp.bfloat16)
        new_values = normed_ref[1, pl.ds(first, 8), :].astype(jnp.bfloat16)
        contract = (((1,), (1,)), ((), ()))
        scores = []
        for half in range(2):
            keys = kv_ref[2 * p + half, :, :HEAD]
            scores.append(
                lax.dot_general(query, keys, contract, preferred_element_type=jnp.float32)
            )
        cache = jnp.where(high, scores[1], scores[0]) * scale
        length = jnp.where(high, len_ref[2 * pair + 1], len_ref[2 * pair])
        cache = jnp.where(position < length, cache, -jnp.inf)
        fresh = (
            lax.dot_general(query, new_keys, contract, preferred_element_type=jnp.float32)
            * scale
        )
        fresh = jnp.where(fresh_ok, fresh, -jnp.inf)
        top = jnp.maximum(
            jnp.max(cache, axis=1, keepdims=True), jnp.max(fresh, axis=1, keepdims=True)
        )
        cache = jnp.exp(cache - top)
        fresh = jnp.exp(fresh - top)
        total = jnp.sum(cache, axis=1, keepdims=True) + jnp.sum(fresh, axis=1, keepdims=True)
        cache = (cache / total).astype(jnp.bfloat16)
        fresh = (fresh / total).astype(jnp.bfloat16)
        weighed = []
        for half in range(2):
            values = kv_ref[2 * p + half, :, HEAD:]
            weighed.append(jnp.dot(cache, values, preferred_element_type=jnp.float32))
        attended = jnp.where(high, weighed[1], weighed[0]) + jnp.dot(
            fresh, new_values, preferred_element_type=jnp.float32
        )
        for q in range(groups):
            middle_ref[pl.ds(first, 8), q * HEAD : (q + 1) * HEAD] = (
                hidden_parts_ref[q, pl.ds(first, 8), :] + attended[q * 8 : (q + 1) * 8]
            )

    @pl.when(step == pl.num_programs(0) - 1)
    def _():
        middle = middle_ref[...]
        width = middle.shape[1]
        squares = jnp.sum(middle * middle, axis=1, keepdims=True)
        lane = lax.broadcasted_iota(jnp.int32, (rows, sent_ref.shape[1] - width), 1)
        tail = jnp.zeros(lane.shape, jnp.float32)
        for i, term in enumerate(three_terms(squares)):
            tail = jnp.where(lane == i, term, tail)
        sent_ref[:, :width] = (middle * out_gain_ref[...]).astype(jnp.bfloat16)
        sent_ref[:, width:] = tail.astype(jnp.bfloat16)


def adam_kernel(place_ref, grad_ref, g1_ref, g2_ref, g3_ref, w_ref, m1_ref, m2_ref, new_ref, blocks_ref):
    members, halves, units, width = blocks_ref.shape
    step = 2 * width
    for half in range(halves):
        for i in range(members // 2):
            cut = slice(i * step, (i + 1) * step)
            grad_sum = grad_ref[:, half, cut].astype(jnp.float32)
            for ref in (g1_ref, g2_ref, g3_ref):
                grad_sum = grad_sum + ref[:, half, cut].astype(jnp.float32)
            new = adam_update(
                grad_sum, w_ref[:, half, cut], m1_ref[:, half, cut], m2_ref[:, half, cut]
            )
            new_ref[:, half, cut] = new
            blocks_ref[2 * i, half] = new[:, :width].astype(jnp.bfloat16)
            blocks_ref[2 * i + 1, half] = new[:, width:].astype(jnp.bfloat16)


def up_kernel(place_ref, x_ref, w0_ref, w1_ref, w2_ref, w3_ref, out_ref):
    copies, height, units = out_ref.shape
    bands, rows, _ = x_ref.shape
    width = w0_ref.shape[3]
    total = jnp.zeros((rows, units), jnp.float32)
    squares = jnp.zeros((rows, 1), jnp.float32)
    for k, w_ref in enumerate((w0_ref, w1_ref, w2_ref, w3_ref)):
        x = x_ref[lax.rem(place_ref[0] + bands - k, bands)]
        total += lax.dot_general(
            x[:, :width],
            w_ref[:, 0].reshape(units, width),
            (((1,), (1,)), ((), ())),
            preferred_element_type=jnp.float32,
        )
        squares += jnp.sum(x[:, width:].astype(jnp.float32), axis=1, keepdims=True)
    line = to_lanes(squares, units)
    row = lax.broadcasted_iota(jnp.int32, (height - rows, units), 0)
    tail = jnp.zeros((height - rows, units), jnp.float32)
    for i, term in enumerate(three_terms(line)):
        tail = jnp.where(row == i, term, tail)
    total = total.astype(out_ref.dtype)
    tail = tail.astype(out_ref.dtype)
    for copy in range(copies):
        out_ref[copy, :rows] = total
        out_ref[copy, rows:] = tail


def down_kernel(place_ref, sums_ref, w0_ref, w1_ref, w2_ref, w3_ref, out_ref):
    roles, bands, rows, width = out_ref.shape
    total = jnp.sum(sums_ref[...].astype(jnp.float32), axis=0)
    squares = jnp.sum(total[rows : rows + 8], axis=0, keepdims=True)
    factor = lax.rsqrt(to_rows(squares, rows) / D + norm_eps)
    upper = jnp.maximum(total[:rows] * factor, 0.0)
    active = (upper * upper).astype(jnp.bfloat16)
    for k, w_ref in enumerate((w0_ref, w1_ref, w2_ref, w3_ref)):
        weights = w_ref[:, 1].reshape(active.shape[1], width)
        band = lax.rem(place_ref[0] + bands - k, bands)
        part = jnp.dot(active, weights, preferred_element_type=jnp.float32).astype(jnp.bfloat16)
        for role in range(roles):
            out_ref[role, band] = part


VMEM = pl.BlockSpec(memory_space=pltpu.VMEM)
SMEM = pl.BlockSpec(memory_space=pltpu.SMEM)


def whole(shape):
    return pl.BlockSpec(shape, lambda i: (0,) * len(shape))


def attend(lengths, hidden, squares, gain, out_gain, kv):
    rows, width = hidden.shape
    count = kv.shape[0]
    groups = width // HEAD
    pairs = 2
    block = (2 * pairs,) + kv.shape[1:]
    return pl.pallas_call(
        functools.partial(attend_kernel, pairs),
        grid=(count // (2 * pairs),),
        out_shape=(
            jax.ShapeDtypeStruct((rows, width), jnp.float32),
            jax.ShapeDtypeStruct((rows, 640), jnp.bfloat16),
        ),
        in_specs=[
            SMEM,
            whole(hidden.shape),
            whole(squares.shape),
            whole(gain.shape),
            whole(out_gain.shape),
            pl.BlockSpec(block, lambda i: (i, 0, 0)),
        ],
        out_specs=(whole((rows, width)), whole((rows, 640))),
        scratch_shapes=[
            pltpu.VMEM((groups, rows, HEAD), jnp.float32),
            pltpu.VMEM((groups, rows, HEAD), jnp.float32),
            pltpu.VMEM((rows, HEAD), jnp.float32),
        ],
        compiler_params=pltpu.CompilerParams(vmem_limit_bytes=24 * 1024 * 1024),
    )(lengths, hidden, squares, gain, out_gain, kv)


def body(grad_parts, master, moment1, moment2, kv_cache, hidden_in, attn_gain, ffn_gain, lengths):
    role_index = lax.axis_index("role")
    place = lax.axis_index("dp")
    shards = lax.axis_size("dp")
    tensor = lax.axis_size("tensor")
    bands = tensor // BAND
    bf16 = jnp.bfloat16
    band_groups = [[b * BAND + m for m in range(BAND)] for b in range(bands)]
    member_groups = [[b * BAND + m for b in range(bands)] for m in range(BAND)]
    quarter = master.shape[3]

    grads = grad_parts[0, 0]
    row_count, steps, width = hidden_in.shape
    rows = row_count * steps
    units = master.shape[1]
    place_operand = place.astype(jnp.int32)[None]
    wide = 640

    def learner_pairs(by):
        return [(i, (i + by) % shards) for i in range(shards)]

    def grad_quarter(owner):
        return lax.dynamic_slice_in_dim(grads, owner * quarter, quarter, 2)

    def learn():
        arriving = [
            lax.ppermute(grad_quarter((place + k) % shards), ("role", "dp"), learner_pairs(k))
            for k in range(1, shards)
        ]
        flat = pl.BlockSpec((units, 2, quarter), lambda i, place_ref: (0, 0, 0))
        new_master, blocks = pl.pallas_call(
            adam_kernel,
            out_shape=(
                jax.ShapeDtypeStruct((units, 2, quarter), jnp.float32),
                jax.ShapeDtypeStruct((BAND, 2, units, width), bf16),
            ),
            grid_spec=pltpu.PrefetchScalarGridSpec(
                num_scalar_prefetch=1,
                grid=(1,),
                in_specs=[
                    pl.BlockSpec((units, 2, quarter), lambda i, place_ref: (0, 0, place_ref[0]))
                ]
                + [flat] * 6,
                out_specs=(
                    flat,
                    pl.BlockSpec((BAND, 2, units, width), lambda i, place_ref: (0, 0, 0, 0)),
                ),
            ),
            compiler_params=pltpu.CompilerParams(vmem_limit_bytes=24 * 1024 * 1024),
        )(place_operand, grads, *arriving, master[0], moment1[0], moment2[0])
        own = lax.all_to_all(blocks, "tensor", 0, 0, tiled=True, axis_index_groups=band_groups)
        return (
            new_master,
            own,
            jnp.zeros((bands, rows, wide), bf16),
            jnp.zeros((rows, width), jnp.float32),
        )

    def roll_out():
        hidden = hidden_in.astype(jnp.float32).reshape(rows, width)
        squares = pl.pallas_call(
            squares_kernel,
            out_shape=jax.ShapeDtypeStruct((tensor, 8, 128), jnp.float32),
            in_specs=[VMEM],
            out_specs=VMEM,
        )(hidden)
        squares = lax.all_to_all(squares, "tensor", 0, 0, tiled=True)
        feature_start = lax.axis_index("tensor") * width
        middle, outgoing = attend(
            lengths,
            hidden,
            squares,
            lax.dynamic_slice_in_dim(attn_gain, feature_start, width)[None],
            lax.dynamic_slice_in_dim(ffn_gain, feature_start, width)[None],
            kv_cache[0, :, 0],
        )
        features = lax.all_to_all(
            jnp.broadcast_to(outgoing[None], (bands, rows, wide)),
            "tensor",
            0,
            0,
            tiled=True,
            axis_index_groups=member_groups,
        )
        return (
            jnp.zeros((units, 2, quarter), jnp.float32),
            jnp.zeros((BAND, 2, units, width), bf16),
            features,
            middle,
        )

    new_master, own, features, middle = lax.cond(role_index == 0, learn, roll_out)
    features = lax.ppermute(features, "role", [(1, 0)])
    slabs = [own] + [
        lax.ppermute(own, ("role", "dp"), learner_pairs(k)) for k in range(1, shards)
    ]
    middle_home = lax.ppermute(middle, "role", [(1, 0)])
    middle = jnp.where(role_index == 0, middle_home, middle)
    copied = lax.ppermute(new_master, "role", [(0, 1)]).astype(bf16).astype(jnp.float32)
    weights_after = jnp.where(role_index == 0, new_master, copied)[None]

    sums = pl.pallas_call(
        up_kernel,
        out_shape=jax.ShapeDtypeStruct((BAND, rows + 16, BAND * units), bf16),
        in_specs=[SMEM] + [VMEM] * 5,
        out_specs=VMEM,
    )(place_operand, features, *slabs)
    sums = lax.all_to_all(sums, "tensor", 0, 0, tiled=True, axis_index_groups=band_groups)
    parts = pl.pallas_call(
        down_kernel,
        out_shape=jax.ShapeDtypeStruct((2, bands, rows, width), bf16),
        in_specs=[SMEM] + [VMEM] * 5,
        out_specs=VMEM,
    )(place_operand, sums, *slabs)
    parts = parts.reshape(2 * bands, rows, width)
    home_groups = [
        [r * tensor + b * BAND + m for r in range(2) for b in range(bands)] for m in range(BAND)
    ]
    parts = lax.all_to_all(
        parts, ("role", "tensor"), 0, 0, tiled=True, axis_index_groups=home_groups
    )
    decoded = (middle + jnp.sum(parts[:bands].astype(jnp.float32), axis=0)).astype(bf16)
    return (weights_after, decoded.reshape(row_count, steps, width))


def solution(mesh):
    in_specs = (
        P("role", "dp", "tensor", None, None),
        P("role", "tensor", None, "dp"),
        P("role", "tensor", None, "dp"),
        P("role", "tensor", None, "dp"),
        P("role", "dp", "tensor", None, None),
        P("dp", None, "tensor"),
        P(),
        P(),
        P("dp"),
    )
    out_specs = (P("role", "tensor", None, "dp"), P("dp", None, "tensor"))
    return jax.shard_map(body, mesh=mesh, in_specs=in_specs, out_specs=out_specs, check_vma=False)
```

time: 139 us -> 115 us (0.83)
  the two profiles are of different devices: /device:TPU:32 before, /device:TPU:40 now
where the time goes in v3:
time: 115 us; the launch traced here: 114 us
  waiting for transfers between devices  48.1 us (42%)
  starting transfers between devices  35.6 us (31%)
  blocking collectives  15.3 us (13%)
  Pallas kernels  8.37 us (7%)
  local copies, waits for them, and re-layouts  4.71 us (4%)
  other arithmetic  1.4 us (1%)
    all_to_all x1, waiting for transfers between devices, body(): lax.all_to_all(parts, ('role', 'tensor'), 0, 0, tiled=True, axis_index_gr...  21.1 us
    all_to_all x1, blocking collectives, learn(): lax.all_to_all(blocks, 'tensor', 0, 0, tiled=True, axis_index_groups=band...  15.3 us
    ppermute x3, waiting for transfers between devices, body(): lax.ppermute(own, ('role', 'dp'), learner_pairs(k))  11.1 us
    ppermute x3, waiting for transfers between devices, learn(): lax.ppermute(grad_quarter((place + k) % shards), ('role', 'dp'), learner_...  11 us
    ppermute x3, starting transfers between devices, learn(): lax.ppermute(grad_quarter((place + k) % shards), ('role', 'dp'), learner_...  10.7 us
    ppermute x3, starting transfers between devices, body(): lax.ppermute(own, ('role', 'dp'), learner_pairs(k))  9.37 us
    all_to_all x1, starting transfers between devices, body(): lax.all_to_all(parts, ('role', 'tensor'), 0, 0, tiled=True, axis_index_gr...  6.7 us
    all_to_all x1, starting transfers between devices, body(): lax.all_to_all(sums, 'tensor', 0, 0, tiled=True, axis_index_groups=band_g...  4.96 us
  transfers between devices with their start and end apart: 11, of which 8 were waited for; matrix products, arithmetic and copies ran while one was open for 1% of the time, Pallas kernels for 4%

profile of v3, /device:TPU:40, one launch (start us, length us, event | category | flops | bytes accessed | tf_op | source)
XLA Modules:
  0.0 114.3 jit_solution(14982619325552103772)
XLA Ops:
  0.6 42.6 %conditional.1 = (f32[16,2,4608]{2,1,0:T(2,128)S(1)}, bf16[8,2,16,576]{3,2,1,0:T(8,128)(2,1)S(1)}, bf16[4,64,640]{2,1,0:T(8,128)(2,1)S(1)}, f32[64,576]{1,0:T(8,128)S(1)}) conditional(s32[]{:T(128)} %convert_element_type.16, (bf16[16,4,576]{2,1,0:T(4,128)(2,1)}, f32[18432]{0:T(1024)}, f32[18432]{0:T(1024)}, bf16[1,16,1,256,384]{4,3,2,1,0:T(8,128)(2,1)}, ...), branch_computations={%region_0.0_spmd, %region_1.2_spmd} | conditional | flops 48 | bytes 13451991 | solution.py:349
  0.7 0.0 copy-start.1
  0.7 0.0 copy-start.6
  0.7 1.9 %dynamic-slice_bitcast_fusion = (bf16[16,2,4608]{2,1,0:T(2,128)(2,1)S(1)}, bf16[16,2,4608]{2,1,0:T(2,128)(2,1)S(1)}, bf16[16,2,4608]{2,1,0:T(2,128)(2,1)S(1)}) fusion(bf16[1,1,16,2,18432]{4,3,2,1,0:T(2,128)(2,1)} %get-tuple-element.62, s32[]{:T(128)S(6)} %select_n.39, s32[]{:T(128)S(6)} %select_n.37, s32[]{:T(128)S(6)} %select_n.35), kind=kLoop, calls=%fused_computation | loop fusion | bytes 1769484 | tf_op jit(solution)/shard_map/cond/branch_1_fun/dynamic_slice | solution.py:280
  2.6 3.5 %collective-permute-start = (bf16[16,2,4608]{2,1,0:T(2,128)(2,1)S(1)}, bf16[16,2,4608]{2,1,0:T(2,128)(2,1)S(1)}, u32[]{:S(2)}, u32[]{:S(2)}) collective-permute-start(bf16[16,2,4608]{2,1,0:T(2,128)(2,1)S(1)} %get-tuple-element.73), channel_id=1, source_target_pairs={{0,32},{32,64},{64,96},{96,0},{1,33},{33,65},{65,97},{97,1},{2,34}... | collective-permute-start | bytes 884744 | tf_op jit(solution)/shard_map/cond/branch_1_fun/ppermute | solution.py:284
  6.1 2.8 %collective-permute-start.1 = (bf16[16,2,4608]{2,1,0:T(2,128)(2,1)S(1)}, bf16[16,2,4608]{2,1,0:T(2,128)(2,1)S(1)}, u32[]{:S(2)}, u32[]{:S(2)}) collective-permute-start(bf16[16,2,4608]{2,1,0:T(2,128)(2,1)S(1)} %get-tuple-element.72), channel_id=1, source_target_pairs={{0,64},{32,96},{64,0},{96,32},{1,65},{33,97},{65,1},{97,33},{2,66}... | collective-permute-start | bytes 884744 | tf_op jit(solution)/shard_map/cond/branch_1_fun/ppermute | solution.py:284
  9.0 4.3 %collective-permute-start.2 = (bf16[16,2,4608]{2,1,0:T(2,128)(2,1)S(1)}, bf16[16,2,4608]{2,1,0:T(2,128)(2,1)S(1)}, u32[]{:S(2)}, u32[]{:S(2)}) collective-permute-start(bf16[16,2,4608]{2,1,0:T(2,128)(2,1)S(1)} %get-tuple-element.71), channel_id=1, source_target_pairs={{0,96},{32,0},{64,32},{96,64},{1,97},{33,1},{65,33},{97,65},{2,98}... | collective-permute-start | bytes 884744 | tf_op jit(solution)/shard_map/cond/branch_1_fun/ppermute | solution.py:284
  13.3 1.1 collective-permute-done.g1_ref
  14.4 5.1 %collective-permute-done.1.g2_ref = bf16[16,2,4608]{2,1,0:T(2,128)(2,1)S(1)} collective-permute-done((bf16[16,2,4608]{2,1,0:T(2,128)(2,1)S(1)}, bf16[16,2,4608]{2,1,0:T(2,128)(2,1)S(1)}, u32[]{:S(2)}, u32[]{:S(2)}) %collective-permute-start.1) | collective-permute-done | bytes 294944 | tf_op jit(solution)/shard_map/cond/branch_1_fun/ppermute | solution.py:284
  19.5 4.8 %collective-permute-done.2.g3_ref = bf16[16,2,4608]{2,1,0:T(2,128)(2,1)S(1)} collective-permute-done((bf16[16,2,4608]{2,1,0:T(2,128)(2,1)S(1)}, bf16[16,2,4608]{2,1,0:T(2,128)(2,1)S(1)}, u32[]{:S(2)}, u32[]{:S(2)}) %collective-permute-start.2) | collective-permute-done | bytes 294944 | tf_op jit(solution)/shard_map/cond/branch_1_fun/ppermute | solution.py:284
  24.3 0.0 copy-done.1
  24.3 0.0 copy-done.6
  24.3 3.6 %branch_1_fun.1 = (f32[16,2,4608]{2,1,0:T(2,128)S(1)}, bf16[8,2,16,576]{3,2,1,0:T(8,128)(2,1)S(1)}) custom-call(s32[1]{0:T(128)} %get-tuple-element.30.place_ref, bf16[16,2,18432]{2,1,0:T(2,128)(2,1)S(1)} %bitcast.17, bf16[16,2,4608]{2,1,0:T(2,128)(2,1)S(1)} %collective-permute-done.g1_ref, bf16[16,2,4608]{2,1,0:T(2,128)(2,1)S(1)} %collective-permute-done.1.g2_ref, ...), custom_call_target="tpu_custom_call" | custom-call | tf_op jit(solution)/shard_map/cond/branch_1_fun/pallas_call | solution.py:288
  27.9 15.3 %all_to_all.23 = bf16[8,2,16,576]{3,2,1,0:T(8,128)(2,1)S(1)} all-to-all(bf16[8,2,16,576]{3,2,1,0:T(8,128)(2,1)S(1)} %get-tuple-element.37), channel_id=1, replica_groups={{0,1,2,3,4,5,6,7},{8,9,10,11,12,13,14,15},{16,17,18,19,20,21,22,23},{24..., dimensions={0} | all-to-all | bytes 589824 | tf_op jit(solution)/shard_map/cond/branch_1_fun/all_to_all | solution.py:308
  43.3 1.3 %collective-permute-start.5 = (bf16[4,64,640]{2,1,0:T(8,128)(2,1)S(1)}, bf16[4,64,640]{2,1,0:T(8,128)(2,1)S(1)}, u32[]{:S(2)}, u32[]{:S(2)}) collective-permute-start(bf16[4,64,640]{2,1,0:T(8,128)(2,1)S(1)} %get-tuple-element.46), channel_id=1, source_target_pairs={{128,0},{129,1},{130,2},{131,3},{132,4},{133,5},{134,6},{135,7},{1... | collective-permute-start | bytes 983048 | tf_op jit(solution)/shard_map/ppermute | solution.py:350
  44.6 2.5 %collective-permute-start.6 = (bf16[8,2,16,576]{3,2,1,0:T(8,128)(2,1)S(1)}, bf16[8,2,16,576]{3,2,1,0:T(8,128)(2,1)S(1)}, u32[]{:S(2)}, u32[]{:S(2)}) collective-permute-start(bf16[8,2,16,576]{3,2,1,0:T(8,128)(2,1)S(1)} %get-tuple-element.47.w0_ref), channel_id=1, source_target_pairs={{0,32},{32,64},{64,96},{96,0},{1,33},{33,65},{65,97},{97,1},{2,34}... | collective-permute-start | bytes 884744 | tf_op jit(solution)/shard_map/ppermute | solution.py:352
  47.1 2.9 %collective-permute-start.7 = (bf16[8,2,16,576]{3,2,1,0:T(8,128)(2,1)S(1)}, bf16[8,2,16,576]{3,2,1,0:T(8,128)(2,1)S(1)}, u32[]{:S(2)}, u32[]{:S(2)}) collective-permute-start(bf16[8,2,16,576]{3,2,1,0:T(8,128)(2,1)S(1)} %get-tuple-element.47.w0_ref), channel_id=1, source_target_pairs={{0,64},{32,96},{64,0},{96,32},{1,65},{33,97},{65,1},{97,33},{2,66}... | collective-permute-start | bytes 884744 | tf_op jit(solution)/shard_map/ppermute | solution.py:352
  50.0 4.0 %collective-permute-start.8 = (bf16[8,2,16,576]{3,2,1,0:T(8,128)(2,1)S(1)}, bf16[8,2,16,576]{3,2,1,0:T(8,128)(2,1)S(1)}, u32[]{:S(2)}, u32[]{:S(2)}) collective-permute-start(bf16[8,2,16,576]{3,2,1,0:T(8,128)(2,1)S(1)} %get-tuple-element.47.w0_ref), channel_id=1, source_target_pairs={{0,96},{32,0},{64,32},{96,64},{1,97},{33,1},{65,33},{97,65},{2,98}... | collective-permute-start | bytes 884744 | tf_op jit(solution)/shard_map/ppermute | solution.py:352
  54.0 0.2 convert.1
  54.2 1.3 %collective-permute-start.3 = (bf16[16,2,4608]{2,1,0:T(2,128)(2,1)S(1)}, bf16[16,2,4608]{2,1,0:T(2,128)(2,1)S(1)}, u32[]{:S(2)}, u32[]{:S(2)}) collective-permute-start(bf16[16,2,4608]{2,1,0:T(2,128)(2,1)S(1)} %convert.1), channel_id=1, source_target_pairs={{0,128},{1,129},{2,130},{3,131},{4,132},{5,133},{6,134},{7,135},{8... | collective-permute-start | bytes 884744 | tf_op jit(solution)/shard_map/ppermute | solution.py:356
  55.5 1.6 %collective-permute-done.6.w1_ref = bf16[8,2,16,576]{3,2,1,0:T(8,128)(2,1)S(1)} collective-permute-done((bf16[8,2,16,576]{3,2,1,0:T(8,128)(2,1)S(1)}, bf16[8,2,16,576]{3,2,1,0:T(8,128)(2,1)S(1)}, u32[]{:S(2)}, u32[]{:S(2)}) %collective-permute-start.6) | collective-permute-done | bytes 294944 | tf_op jit(solution)/shard_map/ppermute | solution.py:352
  57.1 0.0 copy-start.2
  57.1 4.1 %collective-permute-done.7.w2_ref = bf16[8,2,16,576]{3,2,1,0:T(8,128)(2,1)S(1)} collective-permute-done((bf16[8,2,16,576]{3,2,1,0:T(8,128)(2,1)S(1)}, bf16[8,2,16,576]{3,2,1,0:T(8,128)(2,1)S(1)}, u32[]{:S(2)}, u32[]{:S(2)}) %collective-permute-start.7) | collective-permute-done | bytes 294944 | tf_op jit(solution)/shard_map/ppermute | solution.py:352
  61.2 0.0 copy-start.3
  61.2 5.4 %collective-permute-done.8.w3_ref = bf16[8,2,16,576]{3,2,1,0:T(8,128)(2,1)S(1)} collective-permute-done((bf16[8,2,16,576]{3,2,1,0:T(8,128)(2,1)S(1)}, bf16[8,2,16,576]{3,2,1,0:T(8,128)(2,1)S(1)}, u32[]{:S(2)}, u32[]{:S(2)}) %collective-permute-start.8) | collective-permute-done | bytes 294944 | tf_op jit(solution)/shard_map/ppermute | solution.py:352
  66.6 0.0 copy-start.4
  66.6 0.0 collective-permute-done.5.x_ref
  66.6 0.0 copy-done.2
  66.6 0.0 copy-done.3
  66.6 0.7 copy-done.4
  67.3 0.0 copy-start.7
  67.3 0.7 copy-done.7
  68.0 2.3 %shard_map.113 = bf16[8,80,128]{2,1,0:T(8,128)(2,1)} custom-call(s32[1]{0:T(128)} %bitcast.10.place_ref, bf16[4,64,640]{2,1,0:T(8,128)(2,1)} %copy-done.7, bf16[8,2,16,576]{3,2,1,0:T(8,128)(2,1)S(1)} %get-tuple-element.47.w0_ref, bf16[8,2,16,576]{3,2,1,0:T(8,128)(2,1)} %copy-done.2, bf16[8,2,16,576]{3,2,1,0:T(8,128)(2,1)} %copy-done.3, ...), custom_call_target="tpu_custom_call" | custom-call | tf_op jit(solution)/shard_map/pallas_call | solution.py:359
  70.4 5.0 %all-to-all-start.3 = ((bf16[8,80,128]{2,1,0:T(8,128)(2,1)}), bf16[8,80,128]{2,1,0:T(8,128)(2,1)S(1)}, u32[]{:S(2)}, u32[]{:S(2)}) async-start(bf16[8,80,128]{2,1,0:T(8,128)(2,1)} %shard_map.113), calls=%async_computation.3 | async-start | bytes 327680 | tf_op jit(solution)/shard_map/all_to_all | solution.py:365
  75.3 1.3 %collective-permute-start.4 = (f32[64,576]{1,0:T(8,128)S(1)}, f32[64,576]{1,0:T(8,128)S(1)}, u32[]{:S(2)}, u32[]{:S(2)}) collective-permute-start(f32[64,576]{1,0:T(8,128)S(1)} %get-tuple-element.45), channel_id=1, source_target_pairs={{128,0},{129,1},{130,2},{131,3},{132,4},{133,5},{134,6},{135,7},{1... | collective-permute-start | bytes 442376 | tf_op jit(solution)/shard_map/ppermute | solution.py:354
  76.6 4.9 %all-to-all-done.3.sums_ref = bf16[8,80,128]{2,1,0:T(8,128)(2,1)S(1)} async-done(((bf16[8,80,128]{2,1,0:T(8,128)(2,1)}), bf16[8,80,128]{2,1,0:T(8,128)(2,1)S(1)}, u32[]{:S(2)}, u32[]{:S(2)}) %all-to-all-start.3) | async-done | bytes 163872 | tf_op jit(solution)/shard_map/all_to_all | solution.py:365
  81.6 0.0 copy-start.5
  81.6 0.7 copy-done.5
  82.2 2.4 %shard_map.114 = bf16[2,4,64,576]{3,2,1,0:T(8,128)(2,1)} custom-call(s32[1]{0:T(128)} %bitcast.10.place_ref, bf16[8,80,128]{2,1,0:T(8,128)(2,1)} %copy-done.5, bf16[8,2,16,576]{3,2,1,0:T(8,128)(2,1)S(1)} %get-tuple-element.47.w0_ref, bf16[8,2,16,576]{3,2,1,0:T(8,128)(2,1)} %copy-done.2, bf16[8,2,16,576]{3,2,1,0:T(8,128)(2,1)} %copy-done.3, ...), custom_call_target="tpu_custom_call" | custom-call | tf_op jit(solution)/shard_map/pallas_call | solution.py:366
  84.7 6.7 %all-to-all-start.4 = ((bf16[8,64,576]{2,1,0:T(8,128)(2,1)}), bf16[8,64,576]{2,1,0:T(8,128)(2,1)S(1)}, u32[]{:S(2)}, u32[]{:S(2)}) async-start(bf16[8,64,576]{2,1,0:T(8,128)(2,1)} %bitcast.19), calls=%async_computation.4 | async-start | bytes 1310720 | tf_op jit(solution)/shard_map/all_to_all | solution.py:376
  91.4 0.0 collective-permute-done.3
  91.4 1.1 select_bitcast_fusion
  92.5 21.1 %all-to-all-done.4 = bf16[8,64,576]{2,1,0:T(8,128)(2,1)S(1)} async-done(((bf16[8,64,576]{2,1,0:T(8,128)(2,1)}), bf16[8,64,576]{2,1,0:T(8,128)(2,1)S(1)}, u32[]{:S(2)}, u32[]{:S(2)}) %all-to-all-start.4) | async-done | bytes 589856 | tf_op jit(solution)/shard_map/all_to_all | solution.py:376
  113.6 0.0 collective-permute-done.4
  113.6 0.7 reshape.20
  (4 shorter events, 0.1 us)
Async XLA Ops:
  0.7 23.6 %copy-start.1 = (bf16[1,1,16,2,18432]{4,3,2,1,0:T(2,128)(2,1)S(1)}, bf16[1,1,16,2,18432]{4,3,2,1,0:T(2,128)(2,1)}, u32[]{:S(2)}) copy-start(bf16[1,1,16,2,18432]{4,3,2,1,0:T(2,128)(2,1)} %get-tuple-element.62) | copy-start | bytes 3538948 | tf_op jit(solution)/shard_map/cond
  0.7 23.6 %copy-start.6 = (f32[1,16,2,4608]{3,2,1,0:T(2,128)S(1)}, f32[1,16,2,4608]{3,2,1,0:T(2,128)}, u32[]{:S(2)}) copy-start(f32[1,16,2,4608]{3,2,1,0:T(2,128)} %get-tuple-element.63) | copy-start | bytes 1769476 | tf_op jit(solution)/shard_map/cond
  2.6 11.8 %collective-permute-start = (bf16[16,2,4608]{2,1,0:T(2,128)(2,1)S(1)}, bf16[16,2,4608]{2,1,0:T(2,128)(2,1)S(1)}, u32[]{:S(2)}, u32[]{:S(2)}) collective-permute-start(bf16[16,2,4608]{2,1,0:T(2,128)(2,1)S(1)} %get-tuple-element.73), channel_id=1, source_target_pairs={{0,32},{32,64},{64,96},{96,0},{1,33},{33,65},{65,97},{97,1},{2,34}... | collective-permute-start | bytes 884744 | tf_op jit(solution)/shard_map/cond/branch_1_fun/ppermute | solution.py:284
  6.1 13.4 %collective-permute-start.1 = (bf16[16,2,4608]{2,1,0:T(2,128)(2,1)S(1)}, bf16[16,2,4608]{2,1,0:T(2,128)(2,1)S(1)}, u32[]{:S(2)}, u32[]{:S(2)}) collective-permute-start(bf16[16,2,4608]{2,1,0:T(2,128)(2,1)S(1)} %get-tuple-element.72), channel_id=1, source_target_pairs={{0,64},{32,96},{64,0},{96,32},{1,65},{33,97},{65,1},{97,33},{2,66}... | collective-permute-start | bytes 884744 | tf_op jit(solution)/shard_map/cond/branch_1_fun/ppermute | solution.py:284
  9.0 15.3 %collective-permute-start.2 = (bf16[16,2,4608]{2,1,0:T(2,128)(2,1)S(1)}, bf16[16,2,4608]{2,1,0:T(2,128)(2,1)S(1)}, u32[]{:S(2)}, u32[]{:S(2)}) collective-permute-start(bf16[16,2,4608]{2,1,0:T(2,128)(2,1)S(1)} %get-tuple-element.71), channel_id=1, source_target_pairs={{0,96},{32,0},{64,32},{96,64},{1,97},{33,1},{65,33},{97,65},{2,98}... | collective-permute-start | bytes 884744 | tf_op jit(solution)/shard_map/cond/branch_1_fun/ppermute | solution.py:284
  43.3 23.3 %collective-permute-start.5 = (bf16[4,64,640]{2,1,0:T(8,128)(2,1)S(1)}, bf16[4,64,640]{2,1,0:T(8,128)(2,1)S(1)}, u32[]{:S(2)}, u32[]{:S(2)}) collective-permute-start(bf16[4,64,640]{2,1,0:T(8,128)(2,1)S(1)} %get-tuple-element.46), channel_id=1, source_target_pairs={{128,0},{129,1},{130,2},{131,3},{132,4},{133,5},{134,6},{135,7},{1... | collective-permute-start | bytes 983048 | tf_op jit(solution)/shard_map/ppermute | solution.py:350
  44.6 12.5 %collective-permute-start.6 = (bf16[8,2,16,576]{3,2,1,0:T(8,128)(2,1)S(1)}, bf16[8,2,16,576]{3,2,1,0:T(8,128)(2,1)S(1)}, u32[]{:S(2)}, u32[]{:S(2)}) collective-permute-start(bf16[8,2,16,576]{3,2,1,0:T(8,128)(2,1)S(1)} %get-tuple-element.47.w0_ref), channel_id=1, source_target_pairs={{0,32},{32,64},{64,96},{96,0},{1,33},{33,65},{65,97},{97,1},{2,34}... | collective-permute-start | bytes 884744 | tf_op jit(solution)/shard_map/ppermute | solution.py:352
  47.1 14.1 %collective-permute-start.7 = (bf16[8,2,16,576]{3,2,1,0:T(8,128)(2,1)S(1)}, bf16[8,2,16,576]{3,2,1,0:T(8,128)(2,1)S(1)}, u32[]{:S(2)}, u32[]{:S(2)}) collective-permute-start(bf16[8,2,16,576]{3,2,1,0:T(8,128)(2,1)S(1)} %get-tuple-element.47.w0_ref), channel_id=1, source_target_pairs={{0,64},{32,96},{64,0},{96,32},{1,65},{33,97},{65,1},{97,33},{2,66}... | collective-permute-start | bytes 884744 | tf_op jit(solution)/shard_map/ppermute | solution.py:352
  50.0 16.6 %collective-permute-start.8 = (bf16[8,2,16,576]{3,2,1,0:T(8,128)(2,1)S(1)}, bf16[8,2,16,576]{3,2,1,0:T(8,128)(2,1)S(1)}, u32[]{:S(2)}, u32[]{:S(2)}) collective-permute-start(bf16[8,2,16,576]{3,2,1,0:T(8,128)(2,1)S(1)} %get-tuple-element.47.w0_ref), channel_id=1, source_target_pairs={{0,96},{32,0},{64,32},{96,64},{1,97},{33,1},{65,33},{97,65},{2,98}... | collective-permute-start | bytes 884744 | tf_op jit(solution)/shard_map/ppermute | solution.py:352
  54.2 37.2 %collective-permute-start.3 = (bf16[16,2,4608]{2,1,0:T(2,128)(2,1)S(1)}, bf16[16,2,4608]{2,1,0:T(2,128)(2,1)S(1)}, u32[]{:S(2)}, u32[]{:S(2)}) collective-permute-start(bf16[16,2,4608]{2,1,0:T(2,128)(2,1)S(1)} %convert.1), channel_id=1, source_target_pairs={{0,128},{1,129},{2,130},{3,131},{4,132},{5,133},{6,134},{7,135},{8... | collective-permute-start | bytes 884744 | tf_op jit(solution)/shard_map/ppermute | solution.py:356
  57.1 9.5 %copy-start.2 = (bf16[8,2,16,576]{3,2,1,0:T(8,128)(2,1)}, bf16[8,2,16,576]{3,2,1,0:T(8,128)(2,1)S(1)}, u32[]{:S(2)}) copy-start(bf16[8,2,16,576]{3,2,1,0:T(8,128)(2,1)S(1)} %collective-permute-done.6.w1_ref) | copy-start | bytes 884740
  61.2 5.4 %copy-start.3 = (bf16[8,2,16,576]{3,2,1,0:T(8,128)(2,1)}, bf16[8,2,16,576]{3,2,1,0:T(8,128)(2,1)S(1)}, u32[]{:S(2)}) copy-start(bf16[8,2,16,576]{3,2,1,0:T(8,128)(2,1)S(1)} %collective-permute-done.7.w2_ref) | copy-start | bytes 884740
  66.6 0.7 copy-start.4
  67.3 0.7 copy-start.7
  70.4 11.2 %all-to-all-start.3 = ((bf16[8,80,128]{2,1,0:T(8,128)(2,1)}), bf16[8,80,128]{2,1,0:T(8,128)(2,1)S(1)}, u32[]{:S(2)}, u32[]{:S(2)}) async-start(bf16[8,80,128]{2,1,0:T(8,128)(2,1)} %shard_map.113), calls=%async_computation.3 | async-start | bytes 327680 | tf_op jit(solution)/shard_map/all_to_all | solution.py:365
  75.3 38.3 %collective-permute-start.4 = (f32[64,576]{1,0:T(8,128)S(1)}, f32[64,576]{1,0:T(8,128)S(1)}, u32[]{:S(2)}, u32[]{:S(2)}) collective-permute-start(f32[64,576]{1,0:T(8,128)S(1)} %get-tuple-element.45), channel_id=1, source_target_pairs={{128,0},{129,1},{130,2},{131,3},{132,4},{133,5},{134,6},{135,7},{1... | collective-permute-start | bytes 442376 | tf_op jit(solution)/shard_map/ppermute | solution.py:354
  81.6 0.7 copy-start.5
  84.7 28.9 %all-to-all-start.4 = ((bf16[8,64,576]{2,1,0:T(8,128)(2,1)}), bf16[8,64,576]{2,1,0:T(8,128)(2,1)S(1)}, u32[]{:S(2)}, u32[]{:S(2)}) async-start(bf16[8,64,576]{2,1,0:T(8,128)(2,1)} %bitcast.19), calls=%async_computation.4 | async-start | bytes 1310720 | tf_op jit(solution)/shard_map/all_to_all | solution.py:376

commit v4 on v3

--- a/solution.py
+++ b/solution.py
@@ -54,9 +54,14 @@
 
 
 def squares_kernel(hidden_ref, out_ref):
-    hidden = hidden_ref[...]
-    line = to_lanes(jnp.sum(hidden * hidden, axis=1, keepdims=True), 128)
-    out_ref[...] = jnp.broadcast_to(line[None], out_ref.shape)
+    hidden = hidden_ref[...].astype(jnp.float32)
+    squares = jnp.sum(hidden * hidden, axis=2, keepdims=True)
+    shape = hidden.shape[:2] + (out_ref.shape[2],)
+    row = lax.broadcasted_iota(jnp.int32, shape, 0) * shape[1]
+    row = row + lax.broadcasted_iota(jnp.int32, shape, 1)
+    lane = lax.broadcasted_iota(jnp.int32, shape, 2)
+    line = jnp.sum(jnp.where(lane == row, squares, 0.0), axis=(0, 1))
+    out_ref[...] = jnp.broadcast_to(line[None, None], out_ref.shape)
 
 
 def attend_kernel(
@@ -67,8 +72,9 @@
     gain_ref,
     out_gain_ref,
     kv_ref,
+    sent_ref,
+    halves_ref,
     middle_ref,
-    sent_ref,
     normed_ref,
     hidden_parts_ref,
     flip_normed_ref,
@@ -155,17 +161,33 @@
             tail = jnp.where(lane == i, term, tail)
         sent_ref[:, :width] = (middle * out_gain_ref[...]).astype(jnp.bfloat16)
         sent_ref[:, width:] = tail.astype(jnp.bfloat16)
-
-
-def adam_kernel(place_ref, grad_ref, g1_ref, g2_ref, g3_ref, w_ref, m1_ref, m2_ref, new_ref, blocks_ref):
+        rounded = middle.astype(jnp.bfloat16)
+        halves_ref[0, :, :width] = rounded
+        halves_ref[1, :, :width] = (middle - rounded.astype(jnp.float32)).astype(jnp.bfloat16)
+        halves_ref[:, :, width:] = jnp.zeros((2,) + lane.shape, jnp.bfloat16)
+
+
+def split_kernel(grads_ref, out_ref, sems):
+    quarter = out_ref.shape[3]
+    copies = [
+        pltpu.make_async_copy(
+            grads_ref.at[:, :, pl.ds(k * quarter, quarter)], out_ref.at[k], sems.at[k]
+        )
+        for k in range(out_ref.shape[0])
+    ]
+    for copy in copies:
+        copy.start()
+    for copy in copies:
+        copy.wait()
+
+
+def adam_kernel(grads_ref, w_ref, m1_ref, m2_ref, new_ref, blocks_ref):
     members, halves, units, width = blocks_ref.shape
     step = 2 * width
     for half in range(halves):
         for i in range(members // 2):
             cut = slice(i * step, (i + 1) * step)
-            grad_sum = grad_ref[:, half, cut].astype(jnp.float32)
-            for ref in (g1_ref, g2_ref, g3_ref):
-                grad_sum = grad_sum + ref[:, half, cut].astype(jnp.float32)
+            grad_sum = jnp.sum(grads_ref[:, :, half, cut].astype(jnp.float32), axis=0)
             new = adam_update(
                 grad_sum, w_ref[:, half, cut], m1_ref[:, half, cut], m2_ref[:, half, cut]
             )
@@ -174,17 +196,17 @@
             blocks_ref[2 * i + 1, half] = new[:, width:].astype(jnp.bfloat16)
 
 
-def up_kernel(place_ref, x_ref, w0_ref, w1_ref, w2_ref, w3_ref, out_ref):
+def up_kernel(x_ref, slab_ref, out_ref):
     copies, height, units = out_ref.shape
-    bands, rows, _ = x_ref.shape
-    width = w0_ref.shape[3]
+    rows = x_ref.shape[1]
+    bands, width = slab_ref.shape[0], slab_ref.shape[4]
     total = jnp.zeros((rows, units), jnp.float32)
     squares = jnp.zeros((rows, 1), jnp.float32)
-    for k, w_ref in enumerate((w0_ref, w1_ref, w2_ref, w3_ref)):
-        x = x_ref[lax.rem(place_ref[0] + bands - k, bands)]
+    for band in range(bands):
+        x = x_ref[band]
         total += lax.dot_general(
             x[:, :width],
-            w_ref[:, 0].reshape(units, width),
+            slab_ref[band, :, 0].reshape(units, width),
             (((1,), (1,)), ((), ())),
             preferred_element_type=jnp.float32,
         )
@@ -201,19 +223,18 @@
         out_ref[copy, rows:] = tail
 
 
-def down_kernel(place_ref, sums_ref, w0_ref, w1_ref, w2_ref, w3_ref, out_ref):
-    roles, bands, rows, width = out_ref.shape
+def down_kernel(sums_ref, slab_ref, out_ref):
+    bands, rows, width = out_ref.shape
     total = jnp.sum(sums_ref[...].astype(jnp.float32), axis=0)
     squares = jnp.sum(total[rows : rows + 8], axis=0, keepdims=True)
     factor = lax.rsqrt(to_rows(squares, rows) / D + norm_eps)
     upper = jnp.maximum(total[:rows] * factor, 0.0)
     active = (upper * upper).astype(jnp.bfloat16)
-    for k, w_ref in enumerate((w0_ref, w1_ref, w2_ref, w3_ref)):
-        weights = w_ref[:, 1].reshape(active.shape[1], width)
-        band = lax.rem(place_ref[0] + bands - k, bands)
-        part = jnp.dot(active, weights, preferred_element_type=jnp.float32).astype(jnp.bfloat16)
-        for role in range(roles):
-            out_ref[role, band] = part
+    for band in range(bands):
+        weights = slab_ref[band, :, 1].reshape(active.shape[1], width)
+        out_ref[band] = jnp.dot(active, weights, preferred_element_type=jnp.float32).astype(
+            out_ref.dtype
+        )
 
 
 VMEM = pl.BlockSpec(memory_space=pltpu.VMEM)
@@ -234,8 +255,8 @@
         functools.partial(attend_kernel, pairs),
         grid=(count // (2 * pairs),),
         out_shape=(
-            jax.ShapeDtypeStruct((rows, width), jnp.float32),
             jax.ShapeDtypeStruct((rows, 640), jnp.bfloat16),
+            jax.ShapeDtypeStruct((2, rows, 640), jnp.bfloat16),
         ),
         in_specs=[
             SMEM,
@@ -245,8 +266,9 @@
             whole(out_gain.shape),
             pl.BlockSpec(block, lambda i: (i, 0, 0)),
         ],
-        out_specs=(whole((rows, width)), whole((rows, 640))),
+        out_specs=(whole((rows, 640)), whole((2, rows, 640))),
         scratch_shapes=[
+            pltpu.VMEM((rows, width), jnp.float32),
             pltpu.VMEM((groups, rows, HEAD), jnp.float32),
             pltpu.VMEM((groups, rows, HEAD), jnp.float32),
             pltpu.VMEM((rows, HEAD), jnp.float32),
@@ -257,7 +279,6 @@
 
 def body(grad_parts, master, moment1, moment2, kv_cache, hidden_in, attn_gain, ffn_gain, lengths):
     role_index = lax.axis_index("role")
-    place = lax.axis_index("dp")
     shards = lax.axis_size("dp")
     tensor = lax.axis_size("tensor")
     bands = tensor // BAND
@@ -270,60 +291,45 @@
     row_count, steps, width = hidden_in.shape
     rows = row_count * steps
     units = master.shape[1]
-    place_operand = place.astype(jnp.int32)[None]
     wide = 640
 
-    def learner_pairs(by):
-        return [(i, (i + by) % shards) for i in range(shards)]
-
-    def grad_quarter(owner):
-        return lax.dynamic_slice_in_dim(grads, owner * quarter, quarter, 2)
-
     def learn():
-        arriving = [
-            lax.ppermute(grad_quarter((place + k) % shards), ("role", "dp"), learner_pairs(k))
-            for k in range(1, shards)
-        ]
-        flat = pl.BlockSpec((units, 2, quarter), lambda i, place_ref: (0, 0, 0))
+        split = pl.pallas_call(
+            split_kernel,
+            out_shape=jax.ShapeDtypeStruct((shards, units, 2, quarter), bf16),
+            in_specs=[pl.BlockSpec(memory_space=pl.ANY)],
+            out_specs=VMEM,
+            scratch_shapes=[pltpu.SemaphoreType.DMA((shards,))],
+        )(grads)
+        arriving = lax.all_to_all(split, "dp", 0, 0, tiled=True)
         new_master, blocks = pl.pallas_call(
             adam_kernel,
             out_shape=(
                 jax.ShapeDtypeStruct((units, 2, quarter), jnp.float32),
                 jax.ShapeDtypeStruct((BAND, 2, units, width), bf16),
             ),
-            grid_spec=pltpu.PrefetchScalarGridSpec(
-                num_scalar_prefetch=1,
-                grid=(1,),
-                in_specs=[
-                    pl.BlockSpec((units, 2, quarter), lambda i, place_ref: (0, 0, place_ref[0]))
-                ]
-                + [flat] * 6,
-                out_specs=(
-                    flat,
-                    pl.BlockSpec((BAND, 2, units, width), lambda i, place_ref: (0, 0, 0, 0)),
-                ),
-            ),
+            in_specs=[VMEM] * 4,
+            out_specs=(VMEM, VMEM),
             compiler_params=pltpu.CompilerParams(vmem_limit_bytes=24 * 1024 * 1024),
-        )(place_operand, grads, *arriving, master[0], moment1[0], moment2[0])
+        )(arriving, master[0], moment1[0], moment2[0])
         own = lax.all_to_all(blocks, "tensor", 0, 0, tiled=True, axis_index_groups=band_groups)
         return (
             new_master,
             own,
-            jnp.zeros((bands, rows, wide), bf16),
-            jnp.zeros((rows, width), jnp.float32),
+            jnp.zeros((bands + 2, rows, wide), bf16),
         )
 
     def roll_out():
-        hidden = hidden_in.astype(jnp.float32).reshape(rows, width)
         squares = pl.pallas_call(
             squares_kernel,
             out_shape=jax.ShapeDtypeStruct((tensor, 8, 128), jnp.float32),
             in_specs=[VMEM],
             out_specs=VMEM,
-        )(hidden)
+        )(hidden_in)
         squares = lax.all_to_all(squares, "tensor", 0, 0, tiled=True)
+        hidden = hidden_in.astype(jnp.float32).reshape(rows, width)
         feature_start = lax.axis_index("tensor") * width
-        middle, outgoing = attend(
+        outgoing, halves = attend(
             lengths,
             hidden,
             squares,
@@ -342,42 +348,45 @@
         return (
             jnp.zeros((units, 2, quarter), jnp.float32),
             jnp.zeros((BAND, 2, units, width), bf16),
-            features,
-            middle,
-        )
-
-    new_master, own, features, middle = lax.cond(role_index == 0, learn, roll_out)
+            jnp.concatenate([features, halves]),
+        )
+
+    new_master, own, features = lax.cond(role_index == 0, learn, roll_out)
     features = lax.ppermute(features, "role", [(1, 0)])
-    slabs = [own] + [
-        lax.ppermute(own, ("role", "dp"), learner_pairs(k)) for k in range(1, shards)
-    ]
-    middle_home = lax.ppermute(middle, "role", [(1, 0)])
-    middle = jnp.where(role_index == 0, middle_home, middle)
+
+    def gather_slabs():
+        return lax.all_to_all(
+            jnp.broadcast_to(own[None], (shards,) + own.shape), "dp", 0, 0, tiled=True
+        )
+
+    def no_slabs():
+        return jnp.zeros((shards,) + own.shape, bf16)
+
+    slabs = lax.cond(role_index == 0, gather_slabs, no_slabs)
+    slabs, new_master = lax.optimization_barrier((slabs, new_master))
     copied = lax.ppermute(new_master, "role", [(0, 1)]).astype(bf16).astype(jnp.float32)
     weights_after = jnp.where(role_index == 0, new_master, copied)[None]
 
     sums = pl.pallas_call(
         up_kernel,
         out_shape=jax.ShapeDtypeStruct((BAND, rows + 16, BAND * units), bf16),
-        in_specs=[SMEM] + [VMEM] * 5,
+        in_specs=[VMEM, VMEM],
         out_specs=VMEM,
-    )(place_operand, features, *slabs)
+    )(features, slabs)
     sums = lax.all_to_all(sums, "tensor", 0, 0, tiled=True, axis_index_groups=band_groups)
+    sums, weights_after = lax.optimization_barrier((sums, weights_after))
     parts = pl.pallas_call(
         down_kernel,
-        out_shape=jax.ShapeDtypeStruct((2, bands, rows, width), bf16),
-        in_specs=[SMEM] + [VMEM] * 5,
+        out_shape=jax.ShapeDtypeStruct((bands, rows, width), bf16),
+        in_specs=[VMEM, VMEM],
         out_specs=VMEM,
-    )(place_operand, sums, *slabs)
-    parts = parts.reshape(2 * bands, rows, width)
-    home_groups = [
-        [r * tensor + b * BAND + m for r in range(2) for b in range(bands)] for m in range(BAND)
-    ]
-    parts = lax.all_to_all(
-        parts, ("role", "tensor"), 0, 0, tiled=True, axis_index_groups=home_groups
-    )
-    decoded = (middle + jnp.sum(parts[:bands].astype(jnp.float32), axis=0)).astype(bf16)
-    return (weights_after, decoded.reshape(row_count, steps, width))
+    )(sums, slabs)
+    parts = lax.all_to_all(parts, "tensor", 0, 0, tiled=True, axis_index_groups=member_groups)
+    middle = jnp.sum(features[bands:, :, :width].astype(jnp.float32), axis=0)
+    decoded = (middle + jnp.sum(parts.astype(jnp.float32), axis=0)).astype(bf16)
+    decoded = decoded.reshape(row_count, steps, width)
+    returned = lax.ppermute(decoded, "role", [(0, 1)])
+    return (weights_after, jnp.where(role_index == 0, decoded, returned))
 
 
 def solution(mesh):

time: 115 us -> 108 us (0.939)
  the two profiles are of different devices: /device:TPU:40 before, /device:TPU:38 now
where the time goes in v4:
time: 108 us
  waiting for transfers between devices  44.8 us (41%)
  starting transfers between devices  26.4 us (24%)
  blocking collectives  16.8 us (16%)
  Pallas kernels  11.5 us (11%)
  local copies, waits for them, and re-layouts  4.28 us (4%)
  other arithmetic  3.06 us (3%)
    all_to_all x1, blocking collectives, roll_out(): lax.all_to_all(jnp.broadcast_to(outgoing[None], (bands, rows, wide)), 'te...  16.8 us
    ppermute x1, waiting for transfers between devices, body(): returned = lax.ppermute(decoded, 'role', [(0, 1)])  12.2 us
    all_to_all x1, starting transfers between devices, roll_out(): squares = lax.all_to_all(squares, 'tensor', 0, 0, tiled=True)  9.64 us
    ppermute x1, waiting for transfers between devices, body(): lax.ppermute(new_master, 'role', [(0, 1)]).astype(bf16).astype(jnp.float32)  9.09 us
    all_to_all x1, waiting for transfers between devices, body(): lax.all_to_all(parts, 'tensor', 0, 0, tiled=True, axis_index_groups=membe...  8.96 us
    ppermute x1, waiting for transfers between devices, body(): features = lax.ppermute(features, 'role', [(1, 0)])  8.67 us
    all_to_all x1, starting transfers between devices, body(): lax.all_to_all(parts, 'tensor', 0, 0, tiled=True, axis_index_groups=membe...  7.22 us
    all_to_all x1, waiting for transfers between devices, roll_out(): squares = lax.all_to_all(squares, 'tensor', 0, 0, tiled=True)  5.88 us
  transfers between devices with their start and end apart: 6, of which 5 were waited for; matrix products, arithmetic and copies ran while one was open for 5% of the time, Pallas kernels for 2%

profile of v4, /device:TPU:38, one launch (start us, length us, event | category | flops | bytes accessed | tf_op | source)
XLA Modules:
  0.0 107.7 jit_solution(1746993030565477139)
XLA Ops:
  0.6 42.6 %conditional.2 = (f32[16,2,4608]{2,1,0:T(2,128)S(1)}, bf16[6,64,640]{2,1,0:T(8,128)(2,1)S(1)}, bf16[8,2,16,576]{3,2,1,0:T(8,128)(2,1)S(1)}) conditional(s32[]{:T(128)} %convert_element_type.24, (bf16[16,4,576]{2,1,0:T(4,128)(2,1)}, f32[18432]{0:T(1024)}, f32[18432]{0:T(1024)}, bf16[1,16,1,256,384]{4,3,2,1,0:T(8,128)(2,1)}, s32[16]{0:T(128)}) %tuple.28, ...), branch_computations={%region_0.0_spmd, %region_1.0_spmd} | conditional | flops 245766 | bytes 10518638 | solution.py:354
  0.6 1.7 %branch_0_fun.2 = f32[32,8,128]{2,1,0:T(8,128)} custom-call(bf16[16,4,576]{2,1,0:T(4,128)(2,1)} %get-tuple-element.58.hidden_ref), custom_call_target="tpu_custom_call" | custom-call | tf_op jit(solution)/shard_map/cond/branch_0_fun/pallas_call | solution.py:323
  2.3 9.6 %all-to-all-start.3 = ((f32[32,8,128]{2,1,0:T(8,128)}), f32[32,8,128]{2,1,0:T(8,128)S(1)}, u32[]{:S(2)}, u32[]{:S(2)}) async-start(f32[32,8,128]{2,1,0:T(8,128)} %branch_0_fun.2), calls=%async_computation.3 | async-start | bytes 262144 | tf_op jit(solution)/shard_map/cond/branch_0_fun/all_to_all | solution.py:329
  12.0 0.9 reshape.17.hidden_ref
  12.9 0.8 dynamic_slice.5
  13.7 0.8 dynamic_slice.4
  14.5 5.9 %all-to-all-done.3.squares_ref = f32[32,8,128]{2,1,0:T(8,128)S(1)} async-done(((f32[32,8,128]{2,1,0:T(8,128)}), f32[32,8,128]{2,1,0:T(8,128)S(1)}, u32[]{:S(2)}, u32[]{:S(2)}) %all-to-all-start.3) | async-done | bytes 131104 | tf_op jit(solution)/shard_map/cond/branch_0_fun/all_to_all | solution.py:329
  20.3 5.8 %branch_0_fun.3 = (bf16[64,640]{1,0:T(8,128)(2,1)S(1)}, bf16[2,64,640]{2,1,0:T(8,128)(2,1)S(1)}) custom-call(s32[16]{0:T(128)} %get-tuple-element.62.len_ref, f32[64,576]{1,0:T(8,128)S(1)} %reshape.17.hidden_ref, f32[32,8,128]{2,1,0:T(8,128)S(1)} %all-to-all-done.3.squares_ref, f32[1,576]{1,0:T(1,128)S(1)} %broadcast_in_dim.2.gain_ref, ...), custom_call_target="tpu_custom_call" | custom-call | tf_op jit(solution)/shard_map/cond/branch_0_fun/pallas_call | solution.py:254
  26.1 16.8 %all_to_all.30 = bf16[4,64,640]{2,1,0:T(8,128)(2,1)S(1)} all-to-all(bf16[4,64,640]{2,1,0:T(8,128)(2,1)S(1)} %broadcast_in_dim.13), channel_id=1, replica_groups={{0,8,16,24},{1,9,17,25},{2,10,18,26},{3,11,19,27},{4,12,20,28},{5,13,21..., dimensions={0} | all-to-all | bytes 655360 | tf_op jit(solution)/shard_map/cond/branch_0_fun/all_to_all | solution.py:340
  42.9 0.1 pad_maximum_fusion
  43.0 0.2 broadcast.10
  43.2 2.0 %collective-permute-start = (bf16[6,64,640]{2,1,0:T(8,128)(2,1)S(1)}, bf16[6,64,640]{2,1,0:T(8,128)(2,1)S(1)}, u32[]{:S(2)}, u32[]{:S(2)}) collective-permute-start(bf16[6,64,640]{2,1,0:T(8,128)(2,1)S(1)} %get-tuple-element.46), channel_id=1, source_target_pairs={{128,0},{129,1},{130,2},{131,3},{132,4},{133,5},{134,6},{135,7},{1... | collective-permute-start | bytes 1474568 | tf_op jit(solution)/shard_map/ppermute | solution.py:355
  45.3 0.1 conditional.3
  45.3 0.1 broadcast.13
  45.4 0.2 convert.1
  45.6 1.3 %collective-permute-start.1 = (bf16[16,2,4608]{2,1,0:T(2,128)(2,1)S(1)}, bf16[16,2,4608]{2,1,0:T(2,128)(2,1)S(1)}, u32[]{:S(2)}, u32[]{:S(2)}) collective-permute-start(bf16[16,2,4608]{2,1,0:T(2,128)(2,1)S(1)} %convert.1), channel_id=1, source_target_pairs={{0,128},{1,129},{2,130},{3,131},{4,132},{5,133},{6,134},{7,135},{8... | collective-permute-start | bytes 884744 | tf_op jit(solution)/shard_map/ppermute | solution.py:367
  46.9 8.7 %collective-permute-done.x_ref = bf16[6,64,640]{2,1,0:T(8,128)(2,1)S(1)} collective-permute-done((bf16[6,64,640]{2,1,0:T(8,128)(2,1)S(1)}, bf16[6,64,640]{2,1,0:T(8,128)(2,1)S(1)}, u32[]{:S(2)}, u32[]{:S(2)}) %collective-permute-start) | collective-permute-done | bytes 491552 | tf_op jit(solution)/shard_map/ppermute | solution.py:355
  55.6 0.0 copy-start
  55.6 0.8 copy-done
  56.4 2.1 %shard_map.113 = bf16[8,80,128]{2,1,0:T(8,128)(2,1)} custom-call(bf16[6,64,640]{2,1,0:T(8,128)(2,1)} %copy-done, bf16[4,8,2,16,576]{4,3,2,1,0:T(8,128)(2,1)S(1)} %get-tuple-element.82.slab_ref), custom_call_target="tpu_custom_call" | custom-call | tf_op jit(solution)/shard_map/pallas_call | solution.py:370
  58.5 5.0 %all-to-all-start.5 = ((bf16[8,80,128]{2,1,0:T(8,128)(2,1)}), bf16[8,80,128]{2,1,0:T(8,128)(2,1)S(1)}, u32[]{:S(2)}, u32[]{:S(2)}) async-start(bf16[8,80,128]{2,1,0:T(8,128)(2,1)} %shard_map.113), calls=%async_computation.5 | async-start | bytes 327680 | tf_op jit(solution)/shard_map/all_to_all | solution.py:376
  63.4 9.1 %collective-permute-done.1 = bf16[16,2,4608]{2,1,0:T(2,128)(2,1)S(1)} collective-permute-done((bf16[16,2,4608]{2,1,0:T(2,128)(2,1)S(1)}, bf16[16,2,4608]{2,1,0:T(2,128)(2,1)S(1)}, u32[]{:S(2)}, u32[]{:S(2)}) %collective-permute-start.1) | collective-permute-done | bytes 294944 | tf_op jit(solution)/shard_map/ppermute | solution.py:367
  72.5 1.1 %select_bitcast_fusion = f32[1,16,2,4608]{3,2,1,0:T(2,128)} fusion(f32[16,2,4608]{2,1,0:T(2,128)S(1)} %get-tuple-element.50, pred[]{:T(512)S(6)} %eq.2, bf16[16,2,4608]{2,1,0:T(2,128)(2,1)S(1)} %collective-permute-done.1), kind=kLoop, calls=%fused_computation.2 | loop fusion | flops 294912 | bytes 1474561 | tf_op jit(solution)/shard_map/broadcast_in_dim | solution.py:368
  73.6 0.0 all-to-all-done.5.sums_ref
  73.6 0.0 copy-start.1
  73.6 0.7 copy-done.1
  74.3 2.0 %shard_map.114 = bf16[4,64,576]{2,1,0:T(8,128)(2,1)} custom-call(bf16[8,80,128]{2,1,0:T(8,128)(2,1)} %copy-done.1, bf16[4,8,2,16,576]{4,3,2,1,0:T(8,128)(2,1)S(1)} %get-tuple-element.82.slab_ref), custom_call_target="tpu_custom_call" | custom-call | tf_op jit(solution)/shard_map/pallas_call | solution.py:378
  76.3 7.2 %all-to-all-start.6 = ((bf16[4,64,576]{2,1,0:T(8,128)(2,1)}), bf16[4,64,576]{2,1,0:T(8,128)(2,1)S(1)}, u32[]{:S(2)}, u32[]{:S(2)}) async-start(bf16[4,64,576]{2,1,0:T(8,128)(2,1)} %shard_map.114), calls=%async_computation.6 | async-start | bytes 655360 | tf_op jit(solution)/shard_map/all_to_all | solution.py:384
  83.5 1.0 convert_reduce_fusion.1
  84.5 9.0 %all-to-all-done.6 = bf16[4,64,576]{2,1,0:T(8,128)(2,1)S(1)} async-done(((bf16[4,64,576]{2,1,0:T(8,128)(2,1)}), bf16[4,64,576]{2,1,0:T(8,128)(2,1)S(1)}, u32[]{:S(2)}, u32[]{:S(2)}) %all-to-all-start.6) | async-done | bytes 294944 | tf_op jit(solution)/shard_map/all_to_all | solution.py:384
  93.5 1.3 %collective-permute-start.2 = (bf16[16,4,576]{2,1,0:T(4,128)(2,1)S(1)}, bf16[16,4,576]{2,1,0:T(4,128)(2,1)S(1)}, u32[]{:S(2)}, u32[]{:S(2)}) collective-permute-start(bf16[16,4,576]{2,1,0:T(4,128)(2,1)S(1)} %convert_element_type.30), channel_id=1, source_target_pairs={{0,128},{1,129},{2,130},{3,131},{4,132},{5,133},{6,134},{7,135},{8... | collective-permute-start | bytes 221192 | tf_op jit(solution)/shard_map/ppermute | solution.py:388
  94.8 12.2 %collective-permute-done.2 = bf16[16,4,576]{2,1,0:T(4,128)(2,1)S(1)} collective-permute-done((bf16[16,4,576]{2,1,0:T(4,128)(2,1)S(1)}, bf16[16,4,576]{2,1,0:T(4,128)(2,1)S(1)}, u32[]{:S(2)}, u32[]{:S(2)}) %collective-permute-start.2) | collective-permute-done | bytes 73760 | tf_op jit(solution)/shard_map/ppermute | solution.py:388
  107.0 0.7 broadcast_select_fusion
  (7 shorter events, 0.2 us)
Async XLA Ops:
  2.3 18.0 %all-to-all-start.3 = ((f32[32,8,128]{2,1,0:T(8,128)}), f32[32,8,128]{2,1,0:T(8,128)S(1)}, u32[]{:S(2)}, u32[]{:S(2)}) async-start(f32[32,8,128]{2,1,0:T(8,128)} %branch_0_fun.2), calls=%async_computation.3 | async-start | bytes 262144 | tf_op jit(solution)/shard_map/cond/branch_0_fun/all_to_all | solution.py:329
  43.2 12.4 %collective-permute-start = (bf16[6,64,640]{2,1,0:T(8,128)(2,1)S(1)}, bf16[6,64,640]{2,1,0:T(8,128)(2,1)S(1)}, u32[]{:S(2)}, u32[]{:S(2)}) collective-permute-start(bf16[6,64,640]{2,1,0:T(8,128)(2,1)S(1)} %get-tuple-element.46), channel_id=1, source_target_pairs={{128,0},{129,1},{130,2},{131,3},{132,4},{133,5},{134,6},{135,7},{1... | collective-permute-start | bytes 1474568 | tf_op jit(solution)/shard_map/ppermute | solution.py:355
  45.6 26.9 %collective-permute-start.1 = (bf16[16,2,4608]{2,1,0:T(2,128)(2,1)S(1)}, bf16[16,2,4608]{2,1,0:T(2,128)(2,1)S(1)}, u32[]{:S(2)}, u32[]{:S(2)}) collective-permute-start(bf16[16,2,4608]{2,1,0:T(2,128)(2,1)S(1)} %convert.1), channel_id=1, source_target_pairs={{0,128},{1,129},{2,130},{3,131},{4,132},{5,133},{6,134},{7,135},{8... | collective-permute-start | bytes 884744 | tf_op jit(solution)/shard_map/ppermute | solution.py:367
  55.6 0.8 copy-start
  58.5 15.2 %all-to-all-start.5 = ((bf16[8,80,128]{2,1,0:T(8,128)(2,1)}), bf16[8,80,128]{2,1,0:T(8,128)(2,1)S(1)}, u32[]{:S(2)}, u32[]{:S(2)}) async-start(bf16[8,80,128]{2,1,0:T(8,128)(2,1)} %shard_map.113), calls=%async_computation.5 | async-start | bytes 327680 | tf_op jit(solution)/shard_map/all_to_all | solution.py:376
  73.6 0.7 copy-start.1
  76.3 17.1 %all-to-all-start.6 = ((bf16[4,64,576]{2,1,0:T(8,128)(2,1)}), bf16[4,64,576]{2,1,0:T(8,128)(2,1)S(1)}, u32[]{:S(2)}, u32[]{:S(2)}) async-start(bf16[4,64,576]{2,1,0:T(8,128)(2,1)} %shard_map.114), calls=%async_computation.6 | async-start | bytes 655360 | tf_op jit(solution)/shard_map/all_to_all | solution.py:384
  93.5 13.5 %collective-permute-start.2 = (bf16[16,4,576]{2,1,0:T(4,128)(2,1)S(1)}, bf16[16,4,576]{2,1,0:T(4,128)(2,1)S(1)}, u32[]{:S(2)}, u32[]{:S(2)}) collective-permute-start(bf16[16,4,576]{2,1,0:T(4,128)(2,1)S(1)} %convert_element_type.30), channel_id=1, source_target_pairs={{0,128},{1,129},{2,130},{3,131},{4,132},{5,133},{6,134},{7,135},{8... | collective-permute-start | bytes 221192 | tf_op jit(solution)/shard_map/ppermute | solution.py:388

commit v5 on v4

--- a/solution.py
+++ b/solution.py
@@ -300,6 +300,7 @@
             in_specs=[pl.BlockSpec(memory_space=pl.ANY)],
             out_specs=VMEM,
             scratch_shapes=[pltpu.SemaphoreType.DMA((shards,))],
+            compiler_params=pltpu.CompilerParams(vmem_limit_bytes=16 * 1024 * 1024),
         )(grads)
         arriving = lax.all_to_all(split, "dp", 0, 0, tiled=True)
         new_master, blocks = pl.pallas_call(
@@ -325,6 +326,7 @@
             out_shape=jax.ShapeDtypeStruct((tensor, 8, 128), jnp.float32),
             in_specs=[VMEM],
             out_specs=VMEM,
+            compiler_params=pltpu.CompilerParams(vmem_limit_bytes=16 * 1024 * 1024),
         )(hidden_in)
         squares = lax.all_to_all(squares, "tensor", 0, 0, tiled=True)
         hidden = hidden_in.astype(jnp.float32).reshape(rows, width)
@@ -372,6 +374,7 @@
         out_shape=jax.ShapeDtypeStruct((BAND, rows + 16, BAND * units), bf16),
         in_specs=[VMEM, VMEM],
         out_specs=VMEM,
+        compiler_params=pltpu.CompilerParams(vmem_limit_bytes=16 * 1024 * 1024),
     )(features, slabs)
     sums = lax.all_to_all(sums, "tensor", 0, 0, tiled=True, axis_index_groups=band_groups)
     sums, weights_after = lax.optimization_barrier((sums, weights_after))
@@ -380,6 +383,7 @@
         out_shape=jax.ShapeDtypeStruct((bands, rows, width), bf16),
         in_specs=[VMEM, VMEM],
         out_specs=VMEM,
+        compiler_params=pltpu.CompilerParams(vmem_limit_bytes=16 * 1024 * 1024),
     )(sums, slabs)
     parts = lax.all_to_all(parts, "tensor", 0, 0, tiled=True, axis_index_groups=member_groups)
     middle = jnp.sum(features[bands:, :, :width].astype(jnp.float32), axis=0)

time: 108 us -> 104 us (0.963)
  Pallas kernels: 11.5 us -> 9.54 us
  local copies, waits for them, and re-layouts: 4.28 us -> 2.83 us
    ppermute x1, waiting for transfers between devices: 12.2 us -> 10 us  [body(): returned = lax.ppermute(decoded, 'role', [(0, 1)])]
    ppermute x1, waiting for transfers between devices: 9.09 us -> 10.6 us  [body(): lax.ppermute(new_master, 'role', [(0, 1)]).astype(bf16).astype(jnp.float32)]
    unnamed x4 -> x0, local copies, waits for them, and re-layouts: 1.44 us -> none
  transfers between devices with their start and end apart: 6 -> 6, of which waited for: 5 -> 5; matrix products, arithmetic and copies ran while one was open for 5% -> 5% of each run, Pallas kernels for 2% -> 1%
where the time goes in v5:
time: 104 us
  waiting for transfers between devices  44.5 us (43%)
  starting transfers between devices  26.2 us (25%)
  blocking collectives  16.8 us (16%)
  Pallas kernels  9.54 us (9%)
  other arithmetic  3.08 us (3%)
  local copies, waits for them, and re-layouts  2.83 us (3%)
    all_to_all x1, blocking collectives, roll_out(): lax.all_to_all(jnp.broadcast_to(outgoing[None], (bands, rows, wide)), 'te...  16.8 us
    ppermute x1, waiting for transfers between devices, body(): lax.ppermute(new_master, 'role', [(0, 1)]).astype(bf16).astype(jnp.float32)  10.6 us
    ppermute x1, waiting for transfers between devices, body(): returned = lax.ppermute(decoded, 'role', [(0, 1)])  10 us
    all_to_all x1, waiting for transfers between devices, body(): lax.all_to_all(parts, 'tensor', 0, 0, tiled=True, axis_index_groups=membe...  9.89 us
    all_to_all x1, starting transfers between devices, roll_out(): squares = lax.all_to_all(squares, 'tensor', 0, 0, tiled=True)  9.64 us
    ppermute x1, waiting for transfers between devices, body(): features = lax.ppermute(features, 'role', [(1, 0)])  8.15 us
    all_to_all x1, starting transfers between devices, body(): lax.all_to_all(parts, 'tensor', 0, 0, tiled=True, axis_index_groups=membe...  7.22 us
    all_to_all x1, waiting for transfers between devices, roll_out(): squares = lax.all_to_all(squares, 'tensor', 0, 0, tiled=True)  5.88 us
  transfers between devices with their start and end apart: 6, of which 5 were waited for; matrix products, arithmetic and copies ran while one was open for 5% of the time, Pallas kernels for 1%

profile of v5, /device:TPU:38, one launch (start us, length us, event | category | flops | bytes accessed | tf_op | source)
XLA Modules:
  0.0 103.8 jit_solution(1884698745615291463)
XLA Ops:
  0.6 42.6 %conditional.2 = (f32[16,2,4608]{2,1,0:T(2,128)S(1)}, bf16[6,64,640]{2,1,0:T(8,128)(2,1)S(1)}, bf16[8,2,16,576]{3,2,1,0:T(8,128)(2,1)S(1)}) conditional(s32[]{:T(128)} %convert_element_type.24, (bf16[16,4,576]{2,1,0:T(4,128)(2,1)}, f32[18432]{0:T(1024)}, f32[18432]{0:T(1024)}, bf16[1,16,1,256,384]{4,3,2,1,0:T(8,128)(2,1)}, s32[16]{0:T(128)}) %tuple.28, ...), branch_computations={%region_0.0_spmd, %region_1.0_spmd} | conditional | flops 245766 | bytes 10518638 | solution.py:356
  0.6 1.7 %branch_0_fun.2 = f32[32,8,128]{2,1,0:T(8,128)} custom-call(bf16[16,4,576]{2,1,0:T(4,128)(2,1)} %get-tuple-element.58.hidden_ref), custom_call_target="tpu_custom_call" | custom-call | tf_op jit(solution)/shard_map/cond/branch_0_fun/pallas_call | solution.py:324
  2.3 9.6 %all-to-all-start.3 = ((f32[32,8,128]{2,1,0:T(8,128)}), f32[32,8,128]{2,1,0:T(8,128)S(1)}, u32[]{:S(2)}, u32[]{:S(2)}) async-start(f32[32,8,128]{2,1,0:T(8,128)} %branch_0_fun.2), calls=%async_computation.3 | async-start | bytes 262144 | tf_op jit(solution)/shard_map/cond/branch_0_fun/all_to_all | solution.py:331
  12.0 0.9 reshape.17.hidden_ref
  12.9 0.8 dynamic_slice.5
  13.7 0.8 dynamic_slice.4
  14.5 5.9 %all-to-all-done.3.squares_ref = f32[32,8,128]{2,1,0:T(8,128)S(1)} async-done(((f32[32,8,128]{2,1,0:T(8,128)}), f32[32,8,128]{2,1,0:T(8,128)S(1)}, u32[]{:S(2)}, u32[]{:S(2)}) %all-to-all-start.3) | async-done | bytes 131104 | tf_op jit(solution)/shard_map/cond/branch_0_fun/all_to_all | solution.py:331
  20.3 5.8 %branch_0_fun.3 = (bf16[64,640]{1,0:T(8,128)(2,1)S(1)}, bf16[2,64,640]{2,1,0:T(8,128)(2,1)S(1)}) custom-call(s32[16]{0:T(128)} %get-tuple-element.62.len_ref, f32[64,576]{1,0:T(8,128)S(1)} %reshape.17.hidden_ref, f32[32,8,128]{2,1,0:T(8,128)S(1)} %all-to-all-done.3.squares_ref, f32[1,576]{1,0:T(1,128)S(1)} %broadcast_in_dim.2.gain_ref, ...), custom_call_target="tpu_custom_call" | custom-call | tf_op jit(solution)/shard_map/cond/branch_0_fun/pallas_call | solution.py:254
  26.1 16.8 %all_to_all.30 = bf16[4,64,640]{2,1,0:T(8,128)(2,1)S(1)} all-to-all(bf16[4,64,640]{2,1,0:T(8,128)(2,1)S(1)} %broadcast_in_dim.13), channel_id=1, replica_groups={{0,8,16,24},{1,9,17,25},{2,10,18,26},{3,11,19,27},{4,12,20,28},{5,13,21..., dimensions={0} | all-to-all | bytes 655360 | tf_op jit(solution)/shard_map/cond/branch_0_fun/all_to_all | solution.py:342
  42.9 0.1 pad_maximum_fusion
  43.0 0.2 broadcast.10
  43.2 1.3 %collective-permute-start = (bf16[6,64,640]{2,1,0:T(8,128)(2,1)S(1)}, bf16[6,64,640]{2,1,0:T(8,128)(2,1)S(1)}, u32[]{:S(2)}, u32[]{:S(2)}) collective-permute-start(bf16[6,64,640]{2,1,0:T(8,128)(2,1)S(1)} %get-tuple-element.46), channel_id=1, source_target_pairs={{128,0},{129,1},{130,2},{131,3},{132,4},{133,5},{134,6},{135,7},{1... | collective-permute-start | bytes 1474568 | tf_op jit(solution)/shard_map/ppermute | solution.py:357
  44.5 0.1 conditional.3
  44.6 0.1 broadcast.13
  44.7 0.2 convert.1
  44.9 1.3 %collective-permute-start.1 = (bf16[16,2,4608]{2,1,0:T(2,128)(2,1)S(1)}, bf16[16,2,4608]{2,1,0:T(2,128)(2,1)}, u32[]{:S(2)}, u32[]{:S(2)}) collective-permute-start(bf16[16,2,4608]{2,1,0:T(2,128)(2,1)S(1)} %convert.1), channel_id=1, source_target_pairs={{0,128},{1,129},{2,130},{3,131},{4,132},{5,133},{6,134},{7,135},{8... | collective-permute-start | bytes 884744 | tf_op jit(solution)/shard_map/ppermute | solution.py:369
  46.2 8.1 %collective-permute-done.x_ref = bf16[6,64,640]{2,1,0:T(8,128)(2,1)S(1)} collective-permute-done((bf16[6,64,640]{2,1,0:T(8,128)(2,1)S(1)}, bf16[6,64,640]{2,1,0:T(8,128)(2,1)S(1)}, u32[]{:S(2)}, u32[]{:S(2)}) %collective-permute-start) | collective-permute-done | bytes 491552 | tf_op jit(solution)/shard_map/ppermute | solution.py:357
  54.3 1.1 %shard_map.113 = bf16[8,80,128]{2,1,0:T(8,128)(2,1)} custom-call(bf16[6,64,640]{2,1,0:T(8,128)(2,1)S(1)} %collective-permute-done.x_ref, bf16[4,8,2,16,576]{4,3,2,1,0:T(8,128)(2,1)S(1)} %get-tuple-element.82.slab_ref), custom_call_target="tpu_custom_call" | custom-call | tf_op jit(solution)/shard_map/pallas_call | solution.py:372
  55.4 5.4 %all-to-all-start.5 = ((bf16[8,80,128]{2,1,0:T(8,128)(2,1)}), bf16[8,80,128]{2,1,0:T(8,128)(2,1)S(1)}, u32[]{:S(2)}, u32[]{:S(2)}) async-start(bf16[8,80,128]{2,1,0:T(8,128)(2,1)} %shard_map.113), calls=%async_computation.5 | async-start | bytes 327680 | tf_op jit(solution)/shard_map/all_to_all | solution.py:379
  60.8 10.6 %collective-permute-done.1 = bf16[16,2,4608]{2,1,0:T(2,128)(2,1)} collective-permute-done((bf16[16,2,4608]{2,1,0:T(2,128)(2,1)S(1)}, bf16[16,2,4608]{2,1,0:T(2,128)(2,1)}, u32[]{:S(2)}, u32[]{:S(2)}) %collective-permute-start.1) | collective-permute-done | bytes 294944 | tf_op jit(solution)/shard_map/ppermute | solution.py:369
  71.4 2.1 %select_bitcast_fusion = f32[1,16,2,4608]{3,2,1,0:T(2,128)} fusion(f32[16,2,4608]{2,1,0:T(2,128)S(1)} %get-tuple-element.50, pred[]{:T(512)S(6)} %eq.2, bf16[16,2,4608]{2,1,0:T(2,128)(2,1)} %collective-permute-done.1), kind=kLoop, calls=%fused_computation.2 | loop fusion | flops 294912 | bytes 1474561 | tf_op jit(solution)/shard_map/broadcast_in_dim | solution.py:370
  73.5 0.0 all-to-all-done.5.sums_ref
  73.5 1.1 %shard_map.114 = bf16[4,64,576]{2,1,0:T(8,128)(2,1)} custom-call(bf16[8,80,128]{2,1,0:T(8,128)(2,1)S(1)} %all-to-all-done.5.sums_ref, bf16[4,8,2,16,576]{4,3,2,1,0:T(8,128)(2,1)S(1)} %get-tuple-element.82.slab_ref), custom_call_target="tpu_custom_call" | custom-call | tf_op jit(solution)/shard_map/pallas_call | solution.py:381
  74.5 7.2 %all-to-all-start.6 = ((bf16[4,64,576]{2,1,0:T(8,128)(2,1)}), bf16[4,64,576]{2,1,0:T(8,128)(2,1)S(1)}, u32[]{:S(2)}, u32[]{:S(2)}) async-start(bf16[4,64,576]{2,1,0:T(8,128)(2,1)} %shard_map.114), calls=%async_computation.6 | async-start | bytes 655360 | tf_op jit(solution)/shard_map/all_to_all | solution.py:388
  81.8 9.9 %all-to-all-done.6 = bf16[4,64,576]{2,1,0:T(8,128)(2,1)S(1)} async-done(((bf16[4,64,576]{2,1,0:T(8,128)(2,1)}), bf16[4,64,576]{2,1,0:T(8,128)(2,1)S(1)}, u32[]{:S(2)}, u32[]{:S(2)}) %all-to-all-start.6) | async-done | bytes 294944 | tf_op jit(solution)/shard_map/all_to_all | solution.py:388
  91.8 1.3 %collective-permute-start.2 = (bf16[16,4,576]{2,1,0:T(4,128)(2,1)S(1)}, bf16[16,4,576]{2,1,0:T(4,128)(2,1)S(1)}, u32[]{:S(2)}, u32[]{:S(2)}) collective-permute-start(bf16[16,4,576]{2,1,0:T(4,128)(2,1)S(1)} %convert_element_type.30), channel_id=1, source_target_pairs={{0,128},{1,129},{2,130},{3,131},{4,132},{5,133},{6,134},{7,135},{8... | collective-permute-start | bytes 221192 | tf_op jit(solution)/shard_map/ppermute | solution.py:392
  93.1 10.0 %collective-permute-done.2 = bf16[16,4,576]{2,1,0:T(4,128)(2,1)S(1)} collective-permute-done((bf16[16,4,576]{2,1,0:T(4,128)(2,1)S(1)}, bf16[16,4,576]{2,1,0:T(4,128)(2,1)S(1)}, u32[]{:S(2)}, u32[]{:S(2)}) %collective-permute-start.2) | collective-permute-done | bytes 73760 | tf_op jit(solution)/shard_map/ppermute | solution.py:392
  103.1 0.7 broadcast_select_fusion
  (8 shorter events, 0.2 us)
Async XLA Ops:
  2.3 18.0 %all-to-all-start.3 = ((f32[32,8,128]{2,1,0:T(8,128)}), f32[32,8,128]{2,1,0:T(8,128)S(1)}, u32[]{:S(2)}, u32[]{:S(2)}) async-start(f32[32,8,128]{2,1,0:T(8,128)} %branch_0_fun.2), calls=%async_computation.3 | async-start | bytes 262144 | tf_op jit(solution)/shard_map/cond/branch_0_fun/all_to_all | solution.py:331
  43.2 11.1 %collective-permute-start = (bf16[6,64,640]{2,1,0:T(8,128)(2,1)S(1)}, bf16[6,64,640]{2,1,0:T(8,128)(2,1)S(1)}, u32[]{:S(2)}, u32[]{:S(2)}) collective-permute-start(bf16[6,64,640]{2,1,0:T(8,128)(2,1)S(1)} %get-tuple-element.46), channel_id=1, source_target_pairs={{128,0},{129,1},{130,2},{131,3},{132,4},{133,5},{134,6},{135,7},{1... | collective-permute-start | bytes 1474568 | tf_op jit(solution)/shard_map/ppermute | solution.py:357
  44.9 26.5 %collective-permute-start.1 = (bf16[16,2,4608]{2,1,0:T(2,128)(2,1)S(1)}, bf16[16,2,4608]{2,1,0:T(2,128)(2,1)}, u32[]{:S(2)}, u32[]{:S(2)}) collective-permute-start(bf16[16,2,4608]{2,1,0:T(2,128)(2,1)S(1)} %convert.1), channel_id=1, source_target_pairs={{0,128},{1,129},{2,130},{3,131},{4,132},{5,133},{6,134},{7,135},{8... | collective-permute-start | bytes 884744 | tf_op jit(solution)/shard_map/ppermute | solution.py:369
  55.4 18.1 %all-to-all-start.5 = ((bf16[8,80,128]{2,1,0:T(8,128)(2,1)}), bf16[8,80,128]{2,1,0:T(8,128)(2,1)S(1)}, u32[]{:S(2)}, u32[]{:S(2)}) async-start(bf16[8,80,128]{2,1,0:T(8,128)(2,1)} %shard_map.113), calls=%async_computation.5 | async-start | bytes 327680 | tf_op jit(solution)/shard_map/all_to_all | solution.py:379
  74.5 17.1 %all-to-all-start.6 = ((bf16[4,64,576]{2,1,0:T(8,128)(2,1)}), bf16[4,64,576]{2,1,0:T(8,128)(2,1)S(1)}, u32[]{:S(2)}, u32[]{:S(2)}) async-start(bf16[4,64,576]{2,1,0:T(8,128)(2,1)} %shard_map.114), calls=%async_computation.6 | async-start | bytes 655360 | tf_op jit(solution)/shard_map/all_to_all | solution.py:388
  91.8 11.3 %collective-permute-start.2 = (bf16[16,4,576]{2,1,0:T(4,128)(2,1)S(1)}, bf16[16,4,576]{2,1,0:T(4,128)(2,1)S(1)}, u32[]{:S(2)}, u32[]{:S(2)}) collective-permute-start(bf16[16,4,576]{2,1,0:T(4,128)(2,1)S(1)} %convert_element_type.30), channel_id=1, source_target_pairs={{0,128},{1,129},{2,130},{3,131},{4,132},{5,133},{6,134},{7,135},{8... | collective-permute-start | bytes 221192 | tf_op jit(solution)/shard_map/ppermute | solution.py:392

commit v6 on v5

--- a/solution.py
+++ b/solution.py
@@ -182,31 +182,32 @@
 
 
 def adam_kernel(grads_ref, w_ref, m1_ref, m2_ref, new_ref, blocks_ref):
-    members, halves, units, width = blocks_ref.shape
-    step = 2 * width
-    for half in range(halves):
+    members, _, double = blocks_ref.shape
+    width = double // 2
+    for half in range(2):
         for i in range(members // 2):
-            cut = slice(i * step, (i + 1) * step)
+            cut = slice(i * double, (i + 1) * double)
             grad_sum = jnp.sum(grads_ref[:, :, half, cut].astype(jnp.float32), axis=0)
             new = adam_update(
                 grad_sum, w_ref[:, half, cut], m1_ref[:, half, cut], m2_ref[:, half, cut]
             )
             new_ref[:, half, cut] = new
-            blocks_ref[2 * i, half] = new[:, :width].astype(jnp.bfloat16)
-            blocks_ref[2 * i + 1, half] = new[:, width:].astype(jnp.bfloat16)
+            place = slice(half * width, (half + 1) * width)
+            blocks_ref[2 * i, :, place] = new[:, :width].astype(jnp.bfloat16)
+            blocks_ref[2 * i + 1, :, place] = new[:, width:].astype(jnp.bfloat16)
 
 
 def up_kernel(x_ref, slab_ref, out_ref):
     copies, height, units = out_ref.shape
     rows = x_ref.shape[1]
-    bands, width = slab_ref.shape[0], slab_ref.shape[4]
+    bands, width = slab_ref.shape[0], slab_ref.shape[3] // 2
     total = jnp.zeros((rows, units), jnp.float32)
     squares = jnp.zeros((rows, 1), jnp.float32)
     for band in range(bands):
         x = x_ref[band]
         total += lax.dot_general(
             x[:, :width],
-            slab_ref[band, :, 0].reshape(units, width),
+            slab_ref[band, :, :, :width].reshape(units, width),
             (((1,), (1,)), ((), ())),
             preferred_element_type=jnp.float32,
         )
@@ -231,7 +232,7 @@
     upper = jnp.maximum(total[:rows] * factor, 0.0)
     active = (upper * upper).astype(jnp.bfloat16)
     for band in range(bands):
-        weights = slab_ref[band, :, 1].reshape(active.shape[1], width)
+        weights = slab_ref[band, :, :, width:].reshape(active.shape[1], width)
         out_ref[band] = jnp.dot(active, weights, preferred_element_type=jnp.float32).astype(
             out_ref.dtype
         )
@@ -307,7 +308,7 @@
             adam_kernel,
             out_shape=(
                 jax.ShapeDtypeStruct((units, 2, quarter), jnp.float32),
-                jax.ShapeDtypeStruct((BAND, 2, units, width), bf16),
+                jax.ShapeDtypeStruct((BAND, units, 2 * width), bf16),
             ),
             in_specs=[VMEM] * 4,
             out_specs=(VMEM, VMEM),
@@ -349,7 +350,7 @@
         )
         return (
             jnp.zeros((units, 2, quarter), jnp.float32),
-            jnp.zeros((BAND, 2, units, width), bf16),
+            jnp.zeros((BAND, units, 2 * width), bf16),
             jnp.concatenate([features, halves]),
         )
 
@@ -365,10 +366,6 @@
         return jnp.zeros((shards,) + own.shape, bf16)
 
     slabs = lax.cond(role_index == 0, gather_slabs, no_slabs)
-    slabs, new_master = lax.optimization_barrier((slabs, new_master))
-    copied = lax.ppermute(new_master, "role", [(0, 1)]).astype(bf16).astype(jnp.float32)
-    weights_after = jnp.where(role_index == 0, new_master, copied)[None]
-
     sums = pl.pallas_call(
         up_kernel,
         out_shape=jax.ShapeDtypeStruct((BAND, rows + 16, BAND * units), bf16),
@@ -376,6 +373,9 @@
         out_specs=VMEM,
         compiler_params=pltpu.CompilerParams(vmem_limit_bytes=16 * 1024 * 1024),
     )(features, slabs)
+    sums, new_master = lax.optimization_barrier((sums, new_master))
+    copied = lax.ppermute(new_master, "role", [(0, 1)]).astype(bf16).astype(jnp.float32)
+    weights_after = jnp.where(role_index == 0, new_master, copied)[None]
     sums = lax.all_to_all(sums, "tensor", 0, 0, tiled=True, axis_index_groups=band_groups)
     sums, weights_after = lax.optimization_barrier((sums, weights_after))
     parts = pl.pallas_call(

time: 104 us -> 102 us (0.981)
  waiting for transfers between devices: 44.5 us -> 42.8 us
    ppermute x1, waiting for transfers between devices: 10.6 us -> 8.08 us  [body(): lax.ppermute(new_master, 'role', [(0, 1)]).astype(bf16).astype(jnp.float32)]
    ppermute x1, waiting for transfers between devices: 8.15 us -> 9.64 us  [body(): features = lax.ppermute(features, 'role', [(1, 0)])]
  transfers between devices with their start and end apart: 6 -> 6, of which waited for: 5 -> 5; matrix products, arithmetic and copies ran while one was open for 5% -> 4% of each run, Pallas kernels for 1% -> 0%
where the time goes in v6:
time: 102 us; the launch traced here: 101 us
  waiting for transfers between devices  42.8 us (42%)
  starting transfers between devices  26.2 us (26%)
  blocking collectives  16.8 us (16%)
  Pallas kernels  9.74 us (10%)
  local copies, waits for them, and re-layouts  2.8 us (3%)
  other arithmetic  2.12 us (2%)
    all_to_all x1, blocking collectives, roll_out(): lax.all_to_all(jnp.broadcast_to(outgoing[None], (bands, rows, wide)), 'te...  16.8 us
    all_to_all x1, waiting for transfers between devices, body(): lax.all_to_all(parts, 'tensor', 0, 0, tiled=True, axis_index_groups=membe...  9.94 us
    all_to_all x1, starting transfers between devices, roll_out(): squares = lax.all_to_all(squares, 'tensor', 0, 0, tiled=True)  9.64 us
    ppermute x1, waiting for transfers between devices, body(): features = lax.ppermute(features, 'role', [(1, 0)])  9.64 us
    ppermute x1, waiting for transfers between devices, body(): returned = lax.ppermute(decoded, 'role', [(0, 1)])  9.29 us
    ppermute x1, waiting for transfers between devices, body(): lax.ppermute(new_master, 'role', [(0, 1)]).astype(bf16).astype(jnp.float32)  8.08 us
    all_to_all x1, starting transfers between devices, body(): lax.all_to_all(parts, 'tensor', 0, 0, tiled=True, axis_index_groups=membe...  7.22 us
    all_to_all x1, waiting for transfers between devices, roll_out(): squares = lax.all_to_all(squares, 'tensor', 0, 0, tiled=True)  5.88 us
  transfers between devices with their start and end apart: 6, of which 5 were waited for; matrix products, arithmetic and copies ran while one was open for 4% of the time, Pallas kernels for 0%

profile of v6, /device:TPU:38, one launch (start us, length us, event | category | flops | bytes accessed | tf_op | source)
XLA Modules:
  0.0 101.3 jit_solution(12339262734778907007)
XLA Ops:
  0.6 42.6 %conditional.2 = (f32[16,2,4608]{2,1,0:T(2,128)S(1)}, bf16[6,64,640]{2,1,0:T(8,128)(2,1)S(1)}, bf16[8,16,1152]{2,1,0:T(8,128)(2,1)S(1)}) conditional(s32[]{:T(128)} %convert_element_type.24, (bf16[16,4,576]{2,1,0:T(4,128)(2,1)}, f32[18432]{0:T(1024)}, f32[18432]{0:T(1024)}, bf16[1,16,1,256,384]{4,3,2,1,0:T(8,128)(2,1)}, s32[16]{0:T(128)}) %tuple.28, ...), branch_computations={%region_0.0_spmd, %region_1.0_spmd} | conditional | flops 245766 | bytes 10518638 | solution.py:357
  0.6 1.7 %branch_0_fun.2 = f32[32,8,128]{2,1,0:T(8,128)} custom-call(bf16[16,4,576]{2,1,0:T(4,128)(2,1)} %get-tuple-element.58.hidden_ref), custom_call_target="tpu_custom_call" | custom-call | tf_op jit(solution)/shard_map/cond/branch_0_fun/pallas_call | solution.py:325
  2.3 9.6 %all-to-all-start.3 = ((f32[32,8,128]{2,1,0:T(8,128)}), f32[32,8,128]{2,1,0:T(8,128)S(1)}, u32[]{:S(2)}, u32[]{:S(2)}) async-start(f32[32,8,128]{2,1,0:T(8,128)} %branch_0_fun.2), calls=%async_computation.3 | async-start | bytes 262144 | tf_op jit(solution)/shard_map/cond/branch_0_fun/all_to_all | solution.py:332
  12.0 0.9 reshape.17.hidden_ref
  12.9 0.8 dynamic_slice.5
  13.7 0.8 dynamic_slice.4
  14.5 5.9 %all-to-all-done.3.squares_ref = f32[32,8,128]{2,1,0:T(8,128)S(1)} async-done(((f32[32,8,128]{2,1,0:T(8,128)}), f32[32,8,128]{2,1,0:T(8,128)S(1)}, u32[]{:S(2)}, u32[]{:S(2)}) %all-to-all-start.3) | async-done | bytes 131104 | tf_op jit(solution)/shard_map/cond/branch_0_fun/all_to_all | solution.py:332
  20.3 5.8 %branch_0_fun.3 = (bf16[64,640]{1,0:T(8,128)(2,1)S(1)}, bf16[2,64,640]{2,1,0:T(8,128)(2,1)S(1)}) custom-call(s32[16]{0:T(128)} %get-tuple-element.62.len_ref, f32[64,576]{1,0:T(8,128)S(1)} %reshape.17.hidden_ref, f32[32,8,128]{2,1,0:T(8,128)S(1)} %all-to-all-done.3.squares_ref, f32[1,576]{1,0:T(1,128)S(1)} %broadcast_in_dim.2.gain_ref, ...), custom_call_target="tpu_custom_call" | custom-call | tf_op jit(solution)/shard_map/cond/branch_0_fun/pallas_call | solution.py:255
  26.1 16.8 %all_to_all.30 = bf16[4,64,640]{2,1,0:T(8,128)(2,1)S(1)} all-to-all(bf16[4,64,640]{2,1,0:T(8,128)(2,1)S(1)} %broadcast_in_dim.13), channel_id=1, replica_groups={{0,8,16,24},{1,9,17,25},{2,10,18,26},{3,11,19,27},{4,12,20,28},{5,13,21..., dimensions={0} | all-to-all | bytes 655360 | tf_op jit(solution)/shard_map/cond/branch_0_fun/all_to_all | solution.py:343
  42.9 0.1 pad_maximum_fusion
  43.0 0.2 broadcast.10
  43.2 1.3 %collective-permute-start = (bf16[6,64,640]{2,1,0:T(8,128)(2,1)S(1)}, bf16[6,64,640]{2,1,0:T(8,128)(2,1)S(1)}, u32[]{:S(2)}, u32[]{:S(2)}) collective-permute-start(bf16[6,64,640]{2,1,0:T(8,128)(2,1)S(1)} %get-tuple-element.46), channel_id=1, source_target_pairs={{128,0},{129,1},{130,2},{131,3},{132,4},{133,5},{134,6},{135,7},{1... | collective-permute-start | bytes 1474568 | tf_op jit(solution)/shard_map/ppermute | solution.py:358
  44.5 0.1 conditional.3
  44.6 0.1 broadcast.13
  44.7 9.6 %collective-permute-done.x_ref = bf16[6,64,640]{2,1,0:T(8,128)(2,1)S(1)} collective-permute-done((bf16[6,64,640]{2,1,0:T(8,128)(2,1)S(1)}, bf16[6,64,640]{2,1,0:T(8,128)(2,1)S(1)}, u32[]{:S(2)}, u32[]{:S(2)}) %collective-permute-start) | collective-permute-done | bytes 491552 | tf_op jit(solution)/shard_map/ppermute | solution.py:358
  54.3 1.1 %shard_map.113 = bf16[8,80,128]{2,1,0:T(8,128)(2,1)} custom-call(bf16[6,64,640]{2,1,0:T(8,128)(2,1)S(1)} %collective-permute-done.x_ref, bf16[4,8,16,1152]{3,2,1,0:T(8,128)(2,1)S(1)} %get-tuple-element.82.slab_ref), custom_call_target="tpu_custom_call" | custom-call | tf_op jit(solution)/shard_map/pallas_call | solution.py:369
  55.4 0.2 convert.1
  55.6 1.3 %collective-permute-start.1 = (bf16[16,2,4608]{2,1,0:T(2,128)(2,1)S(1)}, bf16[16,2,4608]{2,1,0:T(2,128)(2,1)S(1)}, u32[]{:S(2)}, u32[]{:S(2)}) collective-permute-start(bf16[16,2,4608]{2,1,0:T(2,128)(2,1)S(1)} %convert.1), channel_id=1, source_target_pairs={{0,128},{1,129},{2,130},{3,131},{4,132},{5,133},{6,134},{7,135},{8... | collective-permute-start | bytes 884744 | tf_op jit(solution)/shard_map/ppermute | solution.py:377
  56.9 5.4 %all-to-all-start.5 = ((bf16[8,80,128]{2,1,0:T(8,128)(2,1)}), bf16[8,80,128]{2,1,0:T(8,128)(2,1)S(1)}, u32[]{:S(2)}, u32[]{:S(2)}) async-start(bf16[8,80,128]{2,1,0:T(8,128)(2,1)} %shard_map.113), calls=%async_computation.5 | async-start | bytes 327680 | tf_op jit(solution)/shard_map/all_to_all | solution.py:379
  62.3 8.1 %collective-permute-done.1 = bf16[16,2,4608]{2,1,0:T(2,128)(2,1)S(1)} collective-permute-done((bf16[16,2,4608]{2,1,0:T(2,128)(2,1)S(1)}, bf16[16,2,4608]{2,1,0:T(2,128)(2,1)S(1)}, u32[]{:S(2)}, u32[]{:S(2)}) %collective-permute-start.1) | collective-permute-done | bytes 294944 | tf_op jit(solution)/shard_map/ppermute | solution.py:377
  70.4 1.1 %select_bitcast_fusion = f32[1,16,2,4608]{3,2,1,0:T(2,128)} fusion(f32[16,2,4608]{2,1,0:T(2,128)S(1)} %get-tuple-element.50, pred[]{:T(512)S(6)} %eq.2, bf16[16,2,4608]{2,1,0:T(2,128)(2,1)S(1)} %collective-permute-done.1), kind=kLoop, calls=%fused_computation.2 | loop fusion | flops 294912 | bytes 1474561 | tf_op jit(solution)/shard_map/broadcast_in_dim | solution.py:378
  71.5 0.0 all-to-all-done.5.sums_ref
  71.5 1.2 %shard_map.114 = bf16[4,64,576]{2,1,0:T(8,128)(2,1)} custom-call(bf16[8,80,128]{2,1,0:T(8,128)(2,1)S(1)} %all-to-all-done.5.sums_ref, bf16[4,8,16,1152]{3,2,1,0:T(8,128)(2,1)S(1)} %get-tuple-element.82.slab_ref), custom_call_target="tpu_custom_call" | custom-call | tf_op jit(solution)/shard_map/pallas_call | solution.py:381
  72.7 7.2 %all-to-all-start.6 = ((bf16[4,64,576]{2,1,0:T(8,128)(2,1)}), bf16[4,64,576]{2,1,0:T(8,128)(2,1)S(1)}, u32[]{:S(2)}, u32[]{:S(2)}) async-start(bf16[4,64,576]{2,1,0:T(8,128)(2,1)} %shard_map.114), calls=%async_computation.6 | async-start | bytes 655360 | tf_op jit(solution)/shard_map/all_to_all | solution.py:388
  80.0 9.9 %all-to-all-done.6 = bf16[4,64,576]{2,1,0:T(8,128)(2,1)S(1)} async-done(((bf16[4,64,576]{2,1,0:T(8,128)(2,1)}), bf16[4,64,576]{2,1,0:T(8,128)(2,1)S(1)}, u32[]{:S(2)}, u32[]{:S(2)}) %all-to-all-start.6) | async-done | bytes 294944 | tf_op jit(solution)/shard_map/all_to_all | solution.py:388
  90.0 1.3 %collective-permute-start.2 = (bf16[16,4,576]{2,1,0:T(4,128)(2,1)S(1)}, bf16[16,4,576]{2,1,0:T(4,128)(2,1)S(1)}, u32[]{:S(2)}, u32[]{:S(2)}) collective-permute-start(bf16[16,4,576]{2,1,0:T(4,128)(2,1)S(1)} %convert_element_type.30), channel_id=1, source_target_pairs={{0,128},{1,129},{2,130},{3,131},{4,132},{5,133},{6,134},{7,135},{8... | collective-permute-start | bytes 221192 | tf_op jit(solution)/shard_map/ppermute | solution.py:392
  91.3 9.3 %collective-permute-done.2 = bf16[16,4,576]{2,1,0:T(4,128)(2,1)S(1)} collective-permute-done((bf16[16,4,576]{2,1,0:T(4,128)(2,1)S(1)}, bf16[16,4,576]{2,1,0:T(4,128)(2,1)S(1)}, u32[]{:S(2)}, u32[]{:S(2)}) %collective-permute-start.2) | collective-permute-done | bytes 73760 | tf_op jit(solution)/shard_map/ppermute | solution.py:392
  100.6 0.7 broadcast_select_fusion
  (8 shorter events, 0.2 us)
Async XLA Ops:
  2.3 18.0 %all-to-all-start.3 = ((f32[32,8,128]{2,1,0:T(8,128)}), f32[32,8,128]{2,1,0:T(8,128)S(1)}, u32[]{:S(2)}, u32[]{:S(2)}) async-start(f32[32,8,128]{2,1,0:T(8,128)} %branch_0_fun.2), calls=%async_computation.3 | async-start | bytes 262144 | tf_op jit(solution)/shard_map/cond/branch_0_fun/all_to_all | solution.py:332
  43.2 11.1 %collective-permute-start = (bf16[6,64,640]{2,1,0:T(8,128)(2,1)S(1)}, bf16[6,64,640]{2,1,0:T(8,128)(2,1)S(1)}, u32[]{:S(2)}, u32[]{:S(2)}) collective-permute-start(bf16[6,64,640]{2,1,0:T(8,128)(2,1)S(1)} %get-tuple-element.46), channel_id=1, source_target_pairs={{128,0},{129,1},{130,2},{131,3},{132,4},{133,5},{134,6},{135,7},{1... | collective-permute-start | bytes 1474568 | tf_op jit(solution)/shard_map/ppermute | solution.py:358
  55.6 14.8 %collective-permute-start.1 = (bf16[16,2,4608]{2,1,0:T(2,128)(2,1)S(1)}, bf16[16,2,4608]{2,1,0:T(2,128)(2,1)S(1)}, u32[]{:S(2)}, u32[]{:S(2)}) collective-permute-start(bf16[16,2,4608]{2,1,0:T(2,128)(2,1)S(1)} %convert.1), channel_id=1, source_target_pairs={{0,128},{1,129},{2,130},{3,131},{4,132},{5,133},{6,134},{7,135},{8... | collective-permute-start | bytes 884744 | tf_op jit(solution)/shard_map/ppermute | solution.py:377
  56.9 14.6 %all-to-all-start.5 = ((bf16[8,80,128]{2,1,0:T(8,128)(2,1)}), bf16[8,80,128]{2,1,0:T(8,128)(2,1)S(1)}, u32[]{:S(2)}, u32[]{:S(2)}) async-start(bf16[8,80,128]{2,1,0:T(8,128)(2,1)} %shard_map.113), calls=%async_computation.5 | async-start | bytes 327680 | tf_op jit(solution)/shard_map/all_to_all | solution.py:379
  72.7 17.2 %all-to-all-start.6 = ((bf16[4,64,576]{2,1,0:T(8,128)(2,1)}), bf16[4,64,576]{2,1,0:T(8,128)(2,1)S(1)}, u32[]{:S(2)}, u32[]{:S(2)}) async-start(bf16[4,64,576]{2,1,0:T(8,128)(2,1)} %shard_map.114), calls=%async_computation.6 | async-start | bytes 655360 | tf_op jit(solution)/shard_map/all_to_all | solution.py:388
  90.0 10.6 %collective-permute-start.2 = (bf16[16,4,576]{2,1,0:T(4,128)(2,1)S(1)}, bf16[16,4,576]{2,1,0:T(4,128)(2,1)S(1)}, u32[]{:S(2)}, u32[]{:S(2)}) collective-permute-start(bf16[16,4,576]{2,1,0:T(4,128)(2,1)S(1)} %convert_element_type.30), channel_id=1, source_target_pairs={{0,128},{1,129},{2,130},{3,131},{4,132},{5,133},{6,134},{7,135},{8... | collective-permute-start | bytes 221192 | tf_op jit(solution)/shard_map/ppermute | solution.py:392

commit v7 on v6

--- a/solution.py
+++ b/solution.py
@@ -181,13 +181,19 @@
         copy.wait()
 
 
-def adam_kernel(grads_ref, w_ref, m1_ref, m2_ref, new_ref, blocks_ref):
+def adam_kernel(grads_ref, w_ref, m1_ref, m2_ref, new_ref, blocks_ref, grad_ref):
     members, _, double = blocks_ref.shape
     width = double // 2
+    for i in range(members // 2):
+        cut = slice(i * double, (i + 1) * double)
+        total = grads_ref[0, :, :, cut].astype(jnp.float32)
+        for shard in range(1, grads_ref.shape[0]):
+            total = total + grads_ref[shard, :, :, cut].astype(jnp.float32)
+        grad_ref[:, :, cut] = total
     for half in range(2):
         for i in range(members // 2):
             cut = slice(i * double, (i + 1) * double)
-            grad_sum = jnp.sum(grads_ref[:, :, half, cut].astype(jnp.float32), axis=0)
+            grad_sum = grad_ref[:, half, cut]
             new = adam_update(
                 grad_sum, w_ref[:, half, cut], m1_ref[:, half, cut], m2_ref[:, half, cut]
             )
@@ -225,7 +231,8 @@
 
 
 def down_kernel(sums_ref, slab_ref, out_ref):
-    bands, rows, width = out_ref.shape
+    bands, half, double = out_ref.shape
+    rows, width = 2 * half, double // 2
     total = jnp.sum(sums_ref[...].astype(jnp.float32), axis=0)
     squares = jnp.sum(total[rows : rows + 8], axis=0, keepdims=True)
     factor = lax.rsqrt(to_rows(squares, rows) / D + norm_eps)
@@ -233,7 +240,22 @@
     active = (upper * upper).astype(jnp.bfloat16)
     for band in range(bands):
         weights = slab_ref[band, :, :, width:].reshape(active.shape[1], width)
-        out_ref[band] = jnp.dot(active, weights, preferred_element_type=jnp.float32).astype(
+        part = jnp.dot(active, weights, preferred_element_type=jnp.float32).astype(out_ref.dtype)
+        out_ref[band, :, :width] = part[:half]
+        out_ref[band, :, width:] = part[half:]
+
+
+def finish_kernel(parts_ref, x_ref, out_ref):
+    bands, half, double = parts_ref.shape
+    width = double // 2
+    steps = out_ref.shape[1]
+    total = jnp.sum(parts_ref[...].astype(jnp.float32), axis=0)
+    middle = jnp.sum(x_ref[bands:, :, :width].astype(jnp.float32), axis=0)
+    for side in range(2):
+        rows = slice(side * half, (side + 1) * half)
+        done = middle[rows] + total[:, side * width : (side + 1) * width]
+        count = half // steps
+        out_ref[side * count : (side + 1) * count] = done.reshape(count, steps, width).astype(
             out_ref.dtype
         )
 
@@ -312,6 +334,7 @@
             ),
             in_specs=[VMEM] * 4,
             out_specs=(VMEM, VMEM),
+            scratch_shapes=[pltpu.VMEM((units, 2, quarter), jnp.float32)],
             compiler_params=pltpu.CompilerParams(vmem_limit_bytes=24 * 1024 * 1024),
         )(arriving, master[0], moment1[0], moment2[0])
         own = lax.all_to_all(blocks, "tensor", 0, 0, tiled=True, axis_index_groups=band_groups)
@@ -373,22 +396,25 @@
         out_specs=VMEM,
         compiler_params=pltpu.CompilerParams(vmem_limit_bytes=16 * 1024 * 1024),
     )(features, slabs)
+    sums = lax.all_to_all(sums, "tensor", 0, 0, tiled=True, axis_index_groups=band_groups)
     sums, new_master = lax.optimization_barrier((sums, new_master))
     copied = lax.ppermute(new_master, "role", [(0, 1)]).astype(bf16).astype(jnp.float32)
     weights_after = jnp.where(role_index == 0, new_master, copied)[None]
-    sums = lax.all_to_all(sums, "tensor", 0, 0, tiled=True, axis_index_groups=band_groups)
-    sums, weights_after = lax.optimization_barrier((sums, weights_after))
     parts = pl.pallas_call(
         down_kernel,
-        out_shape=jax.ShapeDtypeStruct((bands, rows, width), bf16),
+        out_shape=jax.ShapeDtypeStruct((bands, rows // 2, 2 * width), bf16),
         in_specs=[VMEM, VMEM],
         out_specs=VMEM,
         compiler_params=pltpu.CompilerParams(vmem_limit_bytes=16 * 1024 * 1024),
     )(sums, slabs)
     parts = lax.all_to_all(parts, "tensor", 0, 0, tiled=True, axis_index_groups=member_groups)
-    middle = jnp.sum(features[bands:, :, :width].astype(jnp.float32), axis=0)
-    decoded = (middle + jnp.sum(parts.astype(jnp.float32), axis=0)).astype(bf16)
-    decoded = decoded.reshape(row_count, steps, width)
+    decoded = pl.pallas_call(
+        finish_kernel,
+        out_shape=jax.ShapeDtypeStruct((row_count, steps, width), bf16),
+        in_specs=[VMEM, VMEM],
+        out_specs=VMEM,
+        compiler_params=pltpu.CompilerParams(vmem_limit_bytes=16 * 1024 * 1024),
+    )(parts, features)
     returned = lax.ppermute(decoded, "role", [(0, 1)])
     return (weights_after, jnp.where(role_index == 0, decoded, returned))
 

time: 102 us -> 98.7 us (0.968)
  blocking collectives: 16.8 us -> 28.2 us
  waiting for transfers between devices: 42.8 us -> 35.3 us
  starting transfers between devices: 26.2 us -> 18.9 us
    all_to_all x0 -> x1, blocking collectives: none -> 11.4 us  [body(): lax.all_to_all(sums, 'tensor', 0, 0, tiled=True, axis_index_groups=band_g...]
    all_to_all x1 -> x0, starting transfers between devices: 5.43 us -> none  [body(): lax.all_to_all(sums, 'tensor', 0, 0, tiled=True, axis_index_groups=band_g...]
    ppermute x1, waiting for transfers between devices: 8.08 us -> 3.98 us  [body(): lax.ppermute(new_master, 'role', [(0, 1)]).astype(bf16).astype(jnp.float32)]
    ppermute x1, waiting for transfers between devices: 9.29 us -> 5.23 us  [body(): returned = lax.ppermute(decoded, 'role', [(0, 1)])]
    all_to_all x1, starting transfers between devices: 7.22 us -> 5.4 us  [body(): lax.all_to_all(parts, 'tensor', 0, 0, tiled=True, axis_index_groups=membe...]
  transfers between devices with their start and end apart: 6 -> 5, of which waited for: 5 -> 5; matrix products, arithmetic and copies ran while one was open for 4% -> 4% of each run, Pallas kernels for 0% -> 0%
where the time goes in v7:
time: 98.7 us; the launch traced here: 98.1 us
  waiting for transfers between devices  35.3 us (36%)
  blocking collectives  28.2 us (29%)
  starting transfers between devices  18.9 us (19%)
  Pallas kernels  9.26 us (9%)
  other arithmetic  2.8 us (3%)
  local copies, waits for them, and re-layouts  2.77 us (3%)
    all_to_all x1, blocking collectives, roll_out(): lax.all_to_all(jnp.broadcast_to(outgoing[None], (bands, rows, wide)), 'te...  16.8 us
    all_to_all x1, blocking collectives, body(): lax.all_to_all(sums, 'tensor', 0, 0, tiled=True, axis_index_groups=band_g...  11.4 us
    all_to_all x1, waiting for transfers between devices, body(): lax.all_to_all(parts, 'tensor', 0, 0, tiled=True, axis_index_groups=membe...  10.3 us
    ppermute x1, waiting for transfers between devices, body(): features = lax.ppermute(features, 'role', [(1, 0)])  9.95 us
    all_to_all x1, starting transfers between devices, roll_out(): squares = lax.all_to_all(squares, 'tensor', 0, 0, tiled=True)  9.64 us
    all_to_all x1, waiting for transfers between devices, roll_out(): squares = lax.all_to_all(squares, 'tensor', 0, 0, tiled=True)  5.88 us
    pallas_call x1, Pallas kernels, attend(): pl.pallas_call(functools.partial(attend_kernel, pairs), grid=(count // (2...  5.75 us
    all_to_all x1, starting transfers between devices, body(): lax.all_to_all(parts, 'tensor', 0, 0, tiled=True, axis_index_groups=membe...  5.4 us
  transfers between devices with their start and end apart: 5, of which 5 were waited for; matrix products, arithmetic and copies ran while one was open for 4% of the time, Pallas kernels for 0%

profile of v7, /device:TPU:38, one launch (start us, length us, event | category | flops | bytes accessed | tf_op | source)
XLA Modules:
  0.0 98.1 jit_solution(9761169443689401440)
XLA Ops:
  0.6 43.3 %conditional.2 = (f32[16,2,4608]{2,1,0:T(2,128)S(1)}, bf16[6,64,640]{2,1,0:T(8,128)(2,1)}, bf16[8,16,1152]{2,1,0:T(8,128)(2,1)S(1)}) conditional(s32[]{:T(128)} %convert_element_type.11, (bf16[16,4,576]{2,1,0:T(4,128)(2,1)}, f32[18432]{0:T(1024)}, f32[18432]{0:T(1024)}, bf16[1,16,1,256,384]{4,3,2,1,0:T(8,128)(2,1)}, s32[16]{0:T(128)}) %tuple.27, ...), branch_computations={%region_0.0_spmd, %region_1.0_spmd} | conditional | flops 245766 | bytes 10518638 | solution.py:380
  0.6 1.7 %branch_0_fun.2 = f32[32,8,128]{2,1,0:T(8,128)} custom-call(bf16[16,4,576]{2,1,0:T(4,128)(2,1)} %get-tuple-element.54.hidden_ref), custom_call_target="tpu_custom_call" | custom-call | tf_op jit(solution)/shard_map/cond/branch_0_fun/pallas_call | solution.py:348
  2.3 9.6 %all-to-all-start.3 = ((f32[32,8,128]{2,1,0:T(8,128)}), f32[32,8,128]{2,1,0:T(8,128)S(1)}, u32[]{:S(2)}, u32[]{:S(2)}) async-start(f32[32,8,128]{2,1,0:T(8,128)} %branch_0_fun.2), calls=%async_computation.3 | async-start | bytes 262144 | tf_op jit(solution)/shard_map/cond/branch_0_fun/all_to_all | solution.py:355
  12.0 0.9 reshape.12.hidden_ref
  12.9 0.8 dynamic_slice.5
  13.7 0.8 dynamic_slice.4
  14.5 5.9 %all-to-all-done.3.squares_ref = f32[32,8,128]{2,1,0:T(8,128)S(1)} async-done(((f32[32,8,128]{2,1,0:T(8,128)}), f32[32,8,128]{2,1,0:T(8,128)S(1)}, u32[]{:S(2)}, u32[]{:S(2)}) %all-to-all-start.3) | async-done | bytes 131104 | tf_op jit(solution)/shard_map/cond/branch_0_fun/all_to_all | solution.py:355
  20.3 5.8 %branch_0_fun.3 = (bf16[64,640]{1,0:T(8,128)(2,1)S(1)}, bf16[2,64,640]{2,1,0:T(8,128)(2,1)S(1)}) custom-call(s32[16]{0:T(128)} %get-tuple-element.58.len_ref, f32[64,576]{1,0:T(8,128)S(1)} %reshape.12.hidden_ref, f32[32,8,128]{2,1,0:T(8,128)S(1)} %all-to-all-done.3.squares_ref, f32[1,576]{1,0:T(1,128)S(1)} %broadcast_in_dim.2.gain_ref, ...), custom_call_target="tpu_custom_call" | custom-call | tf_op jit(solution)/shard_map/cond/branch_0_fun/pallas_call | solution.py:277
  26.1 16.8 %all_to_all.30 = bf16[4,64,640]{2,1,0:T(8,128)(2,1)S(1)} all-to-all(bf16[4,64,640]{2,1,0:T(8,128)(2,1)S(1)} %broadcast_in_dim.13), channel_id=1, replica_groups={{0,8,16,24},{1,9,17,25},{2,10,18,26},{3,11,19,27},{4,12,20,28},{5,13,21..., dimensions={0} | all-to-all | bytes 655360 | tf_op jit(solution)/shard_map/cond/branch_0_fun/all_to_all | solution.py:366
  42.9 0.8 pad_maximum_fusion
  43.8 0.2 broadcast.10
  44.0 1.3 %collective-permute-start = (bf16[6,64,640]{2,1,0:T(8,128)(2,1)}, bf16[6,64,640]{2,1,0:T(8,128)(2,1)S(1)}, u32[]{:S(2)}, u32[]{:S(2)}) collective-permute-start(bf16[6,64,640]{2,1,0:T(8,128)(2,1)} %get-tuple-element.44), channel_id=1, source_target_pairs={{128,0},{129,1},{130,2},{131,3},{132,4},{133,5},{134,6},{135,7},{1... | collective-permute-start | bytes 1474568 | tf_op jit(solution)/shard_map/ppermute | solution.py:381
  45.3 0.1 conditional.3
  45.3 0.1 broadcast.13
  45.4 10.0 %collective-permute-done.x_ref = bf16[6,64,640]{2,1,0:T(8,128)(2,1)S(1)} collective-permute-done((bf16[6,64,640]{2,1,0:T(8,128)(2,1)}, bf16[6,64,640]{2,1,0:T(8,128)(2,1)S(1)}, u32[]{:S(2)}, u32[]{:S(2)}) %collective-permute-start) | collective-permute-done | bytes 491552 | tf_op jit(solution)/shard_map/ppermute | solution.py:381
  55.4 0.4 shard_map.113
  55.8 11.4 %all_to_all.34.sums_ref = bf16[8,80,128]{2,1,0:T(8,128)(2,1)S(1)} all-to-all(bf16[8,80,128]{2,1,0:T(8,128)(2,1)S(1)} %shard_map.113), channel_id=1, replica_groups={{0,1,2,3,4,5,6,7},{8,9,10,11,12,13,14,15},{16,17,18,19,20,21,22,23},{24..., dimensions={0} | all-to-all | bytes 327680 | tf_op jit(solution)/shard_map/all_to_all | solution.py:399
  67.2 1.3 %shard_map.114 = bf16[4,32,1152]{2,1,0:T(8,128)(2,1)} custom-call(bf16[8,80,128]{2,1,0:T(8,128)(2,1)S(1)} %all_to_all.34.sums_ref, bf16[4,8,16,1152]{3,2,1,0:T(8,128)(2,1)S(1)} %get-tuple-element.78.slab_ref), custom_call_target="tpu_custom_call" | custom-call | tf_op jit(solution)/shard_map/pallas_call | solution.py:403
  68.5 5.4 %all-to-all-start.6 = ((bf16[4,32,1152]{2,1,0:T(8,128)(2,1)}), bf16[4,32,1152]{2,1,0:T(8,128)(2,1)S(1)}, u32[]{:S(2)}, u32[]{:S(2)}) async-start(bf16[4,32,1152]{2,1,0:T(8,128)(2,1)} %shard_map.114), calls=%async_computation.6 | async-start | bytes 589824 | tf_op jit(solution)/shard_map/all_to_all | solution.py:410
  73.9 0.2 convert.1
  74.1 1.3 %collective-permute-start.1 = (bf16[16,2,4608]{2,1,0:T(2,128)(2,1)S(1)}, bf16[16,2,4608]{2,1,0:T(2,128)(2,1)S(1)}, u32[]{:S(2)}, u32[]{:S(2)}) collective-permute-start(bf16[16,2,4608]{2,1,0:T(2,128)(2,1)S(1)} %convert.1), channel_id=1, source_target_pairs={{0,128},{1,129},{2,130},{3,131},{4,132},{5,133},{6,134},{7,135},{8... | collective-permute-start | bytes 884744 | tf_op jit(solution)/shard_map/ppermute | solution.py:401
  75.4 10.3 %all-to-all-done.6.parts_ref = bf16[4,32,1152]{2,1,0:T(8,128)(2,1)S(1)} async-done(((bf16[4,32,1152]{2,1,0:T(8,128)(2,1)}), bf16[4,32,1152]{2,1,0:T(8,128)(2,1)S(1)}, u32[]{:S(2)}, u32[]{:S(2)}) %all-to-all-start.6) | async-done | bytes 294944 | tf_op jit(solution)/shard_map/all_to_all | solution.py:410
  85.7 0.1 shard_map.115
  85.8 1.3 %collective-permute-start.2 = (bf16[16,4,576]{2,1,0:T(4,128)(2,1)S(1)}, bf16[16,4,576]{2,1,0:T(4,128)(2,1)S(1)}, u32[]{:S(2)}, u32[]{:S(2)}) collective-permute-start(bf16[16,4,576]{2,1,0:T(4,128)(2,1)S(1)} %shard_map.115), channel_id=1, source_target_pairs={{0,128},{1,129},{2,130},{3,131},{4,132},{5,133},{6,134},{7,135},{8... | collective-permute-start | bytes 221192 | tf_op jit(solution)/shard_map/ppermute | solution.py:418
  87.1 4.0 %collective-permute-done.1 = bf16[16,2,4608]{2,1,0:T(2,128)(2,1)S(1)} collective-permute-done((bf16[16,2,4608]{2,1,0:T(2,128)(2,1)S(1)}, bf16[16,2,4608]{2,1,0:T(2,128)(2,1)S(1)}, u32[]{:S(2)}, u32[]{:S(2)}) %collective-permute-start.1) | collective-permute-done | bytes 294944 | tf_op jit(solution)/shard_map/ppermute | solution.py:401
  91.1 1.1 %select_bitcast_fusion = f32[1,16,2,4608]{3,2,1,0:T(2,128)} fusion(f32[16,2,4608]{2,1,0:T(2,128)S(1)} %get-tuple-element.47, pred[]{:T(512)S(6)} %eq.2, bf16[16,2,4608]{2,1,0:T(2,128)(2,1)S(1)} %collective-permute-done.1), kind=kLoop, calls=%fused_computation.1 | loop fusion | flops 294912 | bytes 1474561 | tf_op jit(solution)/shard_map/broadcast_in_dim | solution.py:402
  92.2 5.2 %collective-permute-done.2 = bf16[16,4,576]{2,1,0:T(4,128)(2,1)S(1)} collective-permute-done((bf16[16,4,576]{2,1,0:T(4,128)(2,1)S(1)}, bf16[16,4,576]{2,1,0:T(4,128)(2,1)S(1)}, u32[]{:S(2)}, u32[]{:S(2)}) %collective-permute-start.2) | collective-permute-done | bytes 73760 | tf_op jit(solution)/shard_map/ppermute | solution.py:418
  97.5 0.6 broadcast_select_fusion
  (4 shorter events, 0.1 us)
Async XLA Ops:
  2.3 18.0 %all-to-all-start.3 = ((f32[32,8,128]{2,1,0:T(8,128)}), f32[32,8,128]{2,1,0:T(8,128)S(1)}, u32[]{:S(2)}, u32[]{:S(2)}) async-start(f32[32,8,128]{2,1,0:T(8,128)} %branch_0_fun.2), calls=%async_computation.3 | async-start | bytes 262144 | tf_op jit(solution)/shard_map/cond/branch_0_fun/all_to_all | solution.py:355
  44.0 11.4 %collective-permute-start = (bf16[6,64,640]{2,1,0:T(8,128)(2,1)}, bf16[6,64,640]{2,1,0:T(8,128)(2,1)S(1)}, u32[]{:S(2)}, u32[]{:S(2)}) collective-permute-start(bf16[6,64,640]{2,1,0:T(8,128)(2,1)} %get-tuple-element.44), channel_id=1, source_target_pairs={{128,0},{129,1},{130,2},{131,3},{132,4},{133,5},{134,6},{135,7},{1... | collective-permute-start | bytes 1474568 | tf_op jit(solution)/shard_map/ppermute | solution.py:381
  68.5 17.2 %all-to-all-start.6 = ((bf16[4,32,1152]{2,1,0:T(8,128)(2,1)}), bf16[4,32,1152]{2,1,0:T(8,128)(2,1)S(1)}, u32[]{:S(2)}, u32[]{:S(2)}) async-start(bf16[4,32,1152]{2,1,0:T(8,128)(2,1)} %shard_map.114), calls=%async_computation.6 | async-start | bytes 589824 | tf_op jit(solution)/shard_map/all_to_all | solution.py:410
  74.1 17.0 %collective-permute-start.1 = (bf16[16,2,4608]{2,1,0:T(2,128)(2,1)S(1)}, bf16[16,2,4608]{2,1,0:T(2,128)(2,1)S(1)}, u32[]{:S(2)}, u32[]{:S(2)}) collective-permute-start(bf16[16,2,4608]{2,1,0:T(2,128)(2,1)S(1)} %convert.1), channel_id=1, source_target_pairs={{0,128},{1,129},{2,130},{3,131},{4,132},{5,133},{6,134},{7,135},{8... | collective-permute-start | bytes 884744 | tf_op jit(solution)/shard_map/ppermute | solution.py:401
  85.8 11.6 %collective-permute-start.2 = (bf16[16,4,576]{2,1,0:T(4,128)(2,1)S(1)}, bf16[16,4,576]{2,1,0:T(4,128)(2,1)S(1)}, u32[]{:S(2)}, u32[]{:S(2)}) collective-permute-start(bf16[16,4,576]{2,1,0:T(4,128)(2,1)S(1)} %shard_map.115), channel_id=1, source_target_pairs={{0,128},{1,129},{2,130},{3,131},{4,132},{5,133},{6,134},{7,135},{8... | collective-permute-start | bytes 221192 | tf_op jit(solution)/shard_map/ppermute | solution.py:418

commit v8 on v7

--- a/solution.py
+++ b/solution.py
@@ -167,7 +167,7 @@
         halves_ref[:, :, width:] = jnp.zeros((2,) + lane.shape, jnp.bfloat16)
 
 
-def split_kernel(grads_ref, out_ref, sems):
+def split_kernel(grads_ref, out_ref, blank_ref, sems):
     quarter = out_ref.shape[3]
     copies = [
         pltpu.make_async_copy(
@@ -177,6 +177,7 @@
     ]
     for copy in copies:
         copy.start()
+    del blank_ref
     for copy in copies:
         copy.wait()
 
@@ -317,11 +318,14 @@
     wide = 640
 
     def learn():
-        split = pl.pallas_call(
+        split, blank = pl.pallas_call(
             split_kernel,
-            out_shape=jax.ShapeDtypeStruct((shards, units, 2, quarter), bf16),
+            out_shape=(
+                jax.ShapeDtypeStruct((shards, units, 2, quarter), bf16),
+                jax.ShapeDtypeStruct((bands + 2, rows, wide), bf16),
+            ),
             in_specs=[pl.BlockSpec(memory_space=pl.ANY)],
-            out_specs=VMEM,
+            out_specs=(VMEM, pl.BlockSpec(memory_space=pl.ANY)),
             scratch_shapes=[pltpu.SemaphoreType.DMA((shards,))],
             compiler_params=pltpu.CompilerParams(vmem_limit_bytes=16 * 1024 * 1024),
         )(grads)
@@ -341,7 +345,7 @@
         return (
             new_master,
             own,
-            jnp.zeros((bands + 2, rows, wide), bf16),
+            blank,
         )
 
     def roll_out():

time: 98.7 us -> 97.9 us (level)
  no operation moved by 1% of the time
where the time goes in v8:
time: 97.9 us; the launch traced here: 97.3 us
  waiting for transfers between devices  35.3 us (36%)
  blocking collectives  28.2 us (29%)
  starting transfers between devices  18.1 us (18%)
  Pallas kernels  9.26 us (9%)
  other arithmetic  2.8 us (3%)
  local copies, waits for them, and re-layouts  2.77 us (3%)
    all_to_all x1, blocking collectives, roll_out(): lax.all_to_all(jnp.broadcast_to(outgoing[None], (bands, rows, wide)), 'te...  16.8 us
    all_to_all x1, blocking collectives, body(): lax.all_to_all(sums, 'tensor', 0, 0, tiled=True, axis_index_groups=band_g...  11.4 us
    all_to_all x1, waiting for transfers between devices, body(): lax.all_to_all(parts, 'tensor', 0, 0, tiled=True, axis_index_groups=membe...  10.5 us
    ppermute x1, waiting for transfers between devices, body(): features = lax.ppermute(features, 'role', [(1, 0)])  9.95 us
    all_to_all x1, starting transfers between devices, roll_out(): squares = lax.all_to_all(squares, 'tensor', 0, 0, tiled=True)  9.64 us
    all_to_all x1, waiting for transfers between devices, roll_out(): squares = lax.all_to_all(squares, 'tensor', 0, 0, tiled=True)  5.88 us
    pallas_call x1, Pallas kernels, attend(): pl.pallas_call(functools.partial(attend_kernel, pairs), grid=(count // (2...  5.75 us
    ppermute x1, waiting for transfers between devices, body(): returned = lax.ppermute(decoded, 'role', [(0, 1)])  5.23 us
  transfers between devices with their start and end apart: 5, of which 5 were waited for; matrix products, arithmetic and copies ran while one was open for 4% of the time, Pallas kernels for 0%

profile of v8, /device:TPU:38, one launch (start us, length us, event | category | flops | bytes accessed | tf_op | source)
XLA Modules:
  0.0 97.3 jit_solution(6677782238247776829)
XLA Ops:
  0.6 43.3 %conditional.2 = (f32[16,2,4608]{2,1,0:T(2,128)S(1)}, bf16[6,64,640]{2,1,0:T(8,128)(2,1)}, bf16[8,16,1152]{2,1,0:T(8,128)(2,1)S(1)}) conditional(s32[]{:T(128)} %convert_element_type.11, (bf16[16,4,576]{2,1,0:T(4,128)(2,1)}, f32[18432]{0:T(1024)}, f32[18432]{0:T(1024)}, bf16[1,16,1,256,384]{4,3,2,1,0:T(8,128)(2,1)}, s32[16]{0:T(128)}) %tuple.27, ...), branch_computations={%region_0.0_spmd, %region_1.0_spmd} | conditional | flops 245766 | bytes 10027116 | solution.py:384
  0.6 1.7 %branch_0_fun.2 = f32[32,8,128]{2,1,0:T(8,128)} custom-call(bf16[16,4,576]{2,1,0:T(4,128)(2,1)} %get-tuple-element.56.hidden_ref), custom_call_target="tpu_custom_call" | custom-call | tf_op jit(solution)/shard_map/cond/branch_0_fun/pallas_call | solution.py:352
  2.3 9.6 %all-to-all-start.3 = ((f32[32,8,128]{2,1,0:T(8,128)}), f32[32,8,128]{2,1,0:T(8,128)S(1)}, u32[]{:S(2)}, u32[]{:S(2)}) async-start(f32[32,8,128]{2,1,0:T(8,128)} %branch_0_fun.2), calls=%async_computation.3 | async-start | bytes 262144 | tf_op jit(solution)/shard_map/cond/branch_0_fun/all_to_all | solution.py:359
  12.0 0.9 reshape.12.hidden_ref
  12.9 0.8 dynamic_slice.5
  13.7 0.8 dynamic_slice.4
  14.5 5.9 %all-to-all-done.3.squares_ref = f32[32,8,128]{2,1,0:T(8,128)S(1)} async-done(((f32[32,8,128]{2,1,0:T(8,128)}), f32[32,8,128]{2,1,0:T(8,128)S(1)}, u32[]{:S(2)}, u32[]{:S(2)}) %all-to-all-start.3) | async-done | bytes 131104 | tf_op jit(solution)/shard_map/cond/branch_0_fun/all_to_all | solution.py:359
  20.3 5.8 %branch_0_fun.3 = (bf16[64,640]{1,0:T(8,128)(2,1)S(1)}, bf16[2,64,640]{2,1,0:T(8,128)(2,1)S(1)}) custom-call(s32[16]{0:T(128)} %get-tuple-element.60.len_ref, f32[64,576]{1,0:T(8,128)S(1)} %reshape.12.hidden_ref, f32[32,8,128]{2,1,0:T(8,128)S(1)} %all-to-all-done.3.squares_ref, f32[1,576]{1,0:T(1,128)S(1)} %broadcast_in_dim.2.gain_ref, ...), custom_call_target="tpu_custom_call" | custom-call | tf_op jit(solution)/shard_map/cond/branch_0_fun/pallas_call | solution.py:278
  26.1 16.8 %all_to_all.30 = bf16[4,64,640]{2,1,0:T(8,128)(2,1)S(1)} all-to-all(bf16[4,64,640]{2,1,0:T(8,128)(2,1)S(1)} %broadcast_in_dim.13), channel_id=1, replica_groups={{0,8,16,24},{1,9,17,25},{2,10,18,26},{3,11,19,27},{4,12,20,28},{5,13,21..., dimensions={0} | all-to-all | bytes 655360 | tf_op jit(solution)/shard_map/cond/branch_0_fun/all_to_all | solution.py:370
  42.9 0.8 pad_maximum_fusion
  43.8 0.2 broadcast.8
  44.0 1.3 %collective-permute-start = (bf16[6,64,640]{2,1,0:T(8,128)(2,1)}, bf16[6,64,640]{2,1,0:T(8,128)(2,1)S(1)}, u32[]{:S(2)}, u32[]{:S(2)}) collective-permute-start(bf16[6,64,640]{2,1,0:T(8,128)(2,1)} %get-tuple-element.46), channel_id=1, source_target_pairs={{128,0},{129,1},{130,2},{131,3},{132,4},{133,5},{134,6},{135,7},{1... | collective-permute-start | bytes 1474568 | tf_op jit(solution)/shard_map/ppermute | solution.py:385
  45.3 0.1 conditional.3
  45.3 0.1 broadcast.10
  45.4 10.0 %collective-permute-done.x_ref = bf16[6,64,640]{2,1,0:T(8,128)(2,1)S(1)} collective-permute-done((bf16[6,64,640]{2,1,0:T(8,128)(2,1)}, bf16[6,64,640]{2,1,0:T(8,128)(2,1)S(1)}, u32[]{:S(2)}, u32[]{:S(2)}) %collective-permute-start) | collective-permute-done | bytes 491552 | tf_op jit(solution)/shard_map/ppermute | solution.py:385
  55.4 0.4 shard_map.113
  55.8 11.4 %all_to_all.34.sums_ref = bf16[8,80,128]{2,1,0:T(8,128)(2,1)S(1)} all-to-all(bf16[8,80,128]{2,1,0:T(8,128)(2,1)S(1)} %shard_map.113), channel_id=1, replica_groups={{0,1,2,3,4,5,6,7},{8,9,10,11,12,13,14,15},{16,17,18,19,20,21,22,23},{24..., dimensions={0} | all-to-all | bytes 327680 | tf_op jit(solution)/shard_map/all_to_all | solution.py:403
  67.2 1.3 %shard_map.114 = bf16[4,32,1152]{2,1,0:T(8,128)(2,1)} custom-call(bf16[8,80,128]{2,1,0:T(8,128)(2,1)S(1)} %all_to_all.34.sums_ref, bf16[4,8,16,1152]{3,2,1,0:T(8,128)(2,1)S(1)} %get-tuple-element.80.slab_ref), custom_call_target="tpu_custom_call" | custom-call | tf_op jit(solution)/shard_map/pallas_call | solution.py:407
  68.5 4.6 %all-to-all-start.6 = ((bf16[4,32,1152]{2,1,0:T(8,128)(2,1)}), bf16[4,32,1152]{2,1,0:T(8,128)(2,1)S(1)}, u32[]{:S(2)}, u32[]{:S(2)}) async-start(bf16[4,32,1152]{2,1,0:T(8,128)(2,1)} %shard_map.114), calls=%async_computation.6 | async-start | bytes 589824 | tf_op jit(solution)/shard_map/all_to_all | solution.py:414
  73.1 0.2 convert.1
  73.3 1.3 %collective-permute-start.1 = (bf16[16,2,4608]{2,1,0:T(2,128)(2,1)S(1)}, bf16[16,2,4608]{2,1,0:T(2,128)(2,1)S(1)}, u32[]{:S(2)}, u32[]{:S(2)}) collective-permute-start(bf16[16,2,4608]{2,1,0:T(2,128)(2,1)S(1)} %convert.1), channel_id=1, source_target_pairs={{0,128},{1,129},{2,130},{3,131},{4,132},{5,133},{6,134},{7,135},{8... | collective-permute-start | bytes 884744 | tf_op jit(solution)/shard_map/ppermute | solution.py:405
  74.6 10.5 %all-to-all-done.6.parts_ref = bf16[4,32,1152]{2,1,0:T(8,128)(2,1)S(1)} async-done(((bf16[4,32,1152]{2,1,0:T(8,128)(2,1)}), bf16[4,32,1152]{2,1,0:T(8,128)(2,1)S(1)}, u32[]{:S(2)}, u32[]{:S(2)}) %all-to-all-start.6) | async-done | bytes 294944 | tf_op jit(solution)/shard_map/all_to_all | solution.py:414
  85.1 0.1 shard_map.115
  85.2 1.3 %collective-permute-start.2 = (bf16[16,4,576]{2,1,0:T(4,128)(2,1)S(1)}, bf16[16,4,576]{2,1,0:T(4,128)(2,1)S(1)}, u32[]{:S(2)}, u32[]{:S(2)}) collective-permute-start(bf16[16,4,576]{2,1,0:T(4,128)(2,1)S(1)} %shard_map.115), channel_id=1, source_target_pairs={{0,128},{1,129},{2,130},{3,131},{4,132},{5,133},{6,134},{7,135},{8... | collective-permute-start | bytes 221192 | tf_op jit(solution)/shard_map/ppermute | solution.py:422
  86.5 3.8 %collective-permute-done.1 = bf16[16,2,4608]{2,1,0:T(2,128)(2,1)S(1)} collective-permute-done((bf16[16,2,4608]{2,1,0:T(2,128)(2,1)S(1)}, bf16[16,2,4608]{2,1,0:T(2,128)(2,1)S(1)}, u32[]{:S(2)}, u32[]{:S(2)}) %collective-permute-start.1) | collective-permute-done | bytes 294944 | tf_op jit(solution)/shard_map/ppermute | solution.py:405
  90.3 1.1 %select_bitcast_fusion = f32[1,16,2,4608]{3,2,1,0:T(2,128)} fusion(f32[16,2,4608]{2,1,0:T(2,128)S(1)} %get-tuple-element.49, pred[]{:T(512)S(6)} %eq.2, bf16[16,2,4608]{2,1,0:T(2,128)(2,1)S(1)} %collective-permute-done.1), kind=kLoop, calls=%fused_computation.1 | loop fusion | flops 294912 | bytes 1474561 | tf_op jit(solution)/shard_map/broadcast_in_dim | solution.py:406
  91.4 5.2 %collective-permute-done.2 = bf16[16,4,576]{2,1,0:T(4,128)(2,1)S(1)} collective-permute-done((bf16[16,4,576]{2,1,0:T(4,128)(2,1)S(1)}, bf16[16,4,576]{2,1,0:T(4,128)(2,1)S(1)}, u32[]{:S(2)}, u32[]{:S(2)}) %collective-permute-start.2) | collective-permute-done | bytes 73760 | tf_op jit(solution)/shard_map/ppermute | solution.py:422
  96.6 0.6 broadcast_select_fusion
  (4 shorter events, 0.1 us)
Async XLA Ops:
  2.3 18.0 %all-to-all-start.3 = ((f32[32,8,128]{2,1,0:T(8,128)}), f32[32,8,128]{2,1,0:T(8,128)S(1)}, u32[]{:S(2)}, u32[]{:S(2)}) async-start(f32[32,8,128]{2,1,0:T(8,128)} %branch_0_fun.2), calls=%async_computation.3 | async-start | bytes 262144 | tf_op jit(solution)/shard_map/cond/branch_0_fun/all_to_all | solution.py:359
  44.0 11.4 %collective-permute-start = (bf16[6,64,640]{2,1,0:T(8,128)(2,1)}, bf16[6,64,640]{2,1,0:T(8,128)(2,1)S(1)}, u32[]{:S(2)}, u32[]{:S(2)}) collective-permute-start(bf16[6,64,640]{2,1,0:T(8,128)(2,1)} %get-tuple-element.46), channel_id=1, source_target_pairs={{128,0},{129,1},{130,2},{131,3},{132,4},{133,5},{134,6},{135,7},{1... | collective-permute-start | bytes 1474568 | tf_op jit(solution)/shard_map/ppermute | solution.py:385
  68.5 16.6 %all-to-all-start.6 = ((bf16[4,32,1152]{2,1,0:T(8,128)(2,1)}), bf16[4,32,1152]{2,1,0:T(8,128)(2,1)S(1)}, u32[]{:S(2)}, u32[]{:S(2)}) async-start(bf16[4,32,1152]{2,1,0:T(8,128)(2,1)} %shard_map.114), calls=%async_computation.6 | async-start | bytes 589824 | tf_op jit(solution)/shard_map/all_to_all | solution.py:414
  73.3 17.0 %collective-permute-start.1 = (bf16[16,2,4608]{2,1,0:T(2,128)(2,1)S(1)}, bf16[16,2,4608]{2,1,0:T(2,128)(2,1)S(1)}, u32[]{:S(2)}, u32[]{:S(2)}) collective-permute-start(bf16[16,2,4608]{2,1,0:T(2,128)(2,1)S(1)} %convert.1), channel_id=1, source_target_pairs={{0,128},{1,129},{2,130},{3,131},{4,132},{5,133},{6,134},{7,135},{8... | collective-permute-start | bytes 884744 | tf_op jit(solution)/shard_map/ppermute | solution.py:405
  85.2 11.4 %collective-permute-start.2 = (bf16[16,4,576]{2,1,0:T(4,128)(2,1)S(1)}, bf16[16,4,576]{2,1,0:T(4,128)(2,1)S(1)}, u32[]{:S(2)}, u32[]{:S(2)}) collective-permute-start(bf16[16,4,576]{2,1,0:T(4,128)(2,1)S(1)} %shard_map.115), channel_id=1, source_target_pairs={{0,128},{1,129},{2,130},{3,131},{4,132},{5,133},{6,134},{7,135},{8... | collective-permute-start | bytes 221192 | tf_op jit(solution)/shard_map/ppermute | solution.py:422
